TPU v7x, 512 devices: a whole 4x4x16 slice. The times are simulated.
512 devices in a mesh: replica: 64 (over x, z_lo, y), tensor: 8 (over z_hi, core).
Axes of the slice: x: 4, y: 4, z: 16 (z_hi: 4, z_lo: 4; z = z_hi * 4 + z_lo), core: 2. Of those that a mesh axis runs over, the one named last changes fastest.
Arguments:
- hidden: bfloat16 [8, 2048, 8192], P(None, 'replica', 'tensor'), may hold values from -6 to 6
- kv_weight: bfloat16 [2048, 8192], P('replica', 'tensor'), may hold values from -0.0625 to 0.0625
- owner: int32 [64], replicated, may hold values from 0 to 63, each once
- queries: bfloat16 [8, 2048, 8192], P(None, 'replica', 'tensor'), may hold values from -160 to 160
- pool: bfloat16 [12288, 16, 2048], P('replica', None, 'tensor'), may hold values from -17 to 17
- page_table: int32 [2048, 6], P('replica'), may hold values from 0 to 319, as said below
- lengths: int32 [2048], P('replica'), may hold values from 1 to 96
- send_pages: int32 [64, 64, 2], P('replica'), may hold values from 0 to 191, as said below
Outputs:
- new_kv: bfloat16 [8, 2048, 2048], P(None, 'replica', 'tensor')
- attended: bfloat16 [8, 2048, 8192], P(None, 'replica', 'tensor')
Inputs may be any that keep to these rules, and one draw needn't show every extreme that they name: `page_table`: entry e < 192 names page e of the home replica's own pool; otherwise the page in slot (e - 192) % 2 of the list that replica (e - 192) // 2 sends to the home replica. Only the first ceil(lengths / 16) entries of a row are read. send_pages[j, h] names pages by their index within replica j's own 192 pages.
All inputs are finite; a program needn't handle non-finite values.
Results may differ from a plain program's by a relative error of at most 0.0044.
Values may be sent and summed in bfloat16 or wider, within the bound.
No kernel may reach another device: no remote copies, remote signals or barrier semaphores. Data moves between devices by JAX's collectives and lax.ppermute only.
A program may use at most 64 MiB of HBM per device.

v0:
```python
import jax
import jax.numpy as jnp
from jax import lax
from jax.sharding import PartitionSpec as P

HD = 128


def attend(query_rows, cache, fresh, seq_lengths):
    steps_count, seq_count, width = query_rows.shape
    kv_heads = cache.shape[-1] // (2 * HD)
    group = width // (HD * kv_heads)
    span = cache.shape[1]
    query = query_rows.reshape(steps_count, seq_count, kv_heads, group, HD)
    cache = cache.reshape(seq_count, span, kv_heads, 2, HD)
    fresh = fresh.reshape(steps_count, seq_count, kv_heads, 2, HD)
    scale = HD ** (-0.5)
    past = (
        jnp.einsum(
            "tshgd,schd->tshgc", query, cache[:, :, :, 0], preferred_element_type=jnp.float32
        )
        * scale
    )
    recent = (
        jnp.einsum(
            "tshgd,ushd->tshgu", query, fresh[:, :, :, 0], preferred_element_type=jnp.float32
        )
        * scale
    )
    live = jnp.arange(span)[None, :] < seq_lengths[:, None]
    past = jnp.where(live[None, :, None, None, :], past, -jnp.inf)
    causal = jnp.arange(steps_count)[None, :] <= jnp.arange(steps_count)[:, None]
    recent = jnp.where(causal[:, None, None, None, :], recent, -jnp.inf)
    top = jnp.maximum(jnp.max(past, -1), jnp.max(recent, -1))[..., None]
    past_w = jnp.exp(past - top)
    recent_w = jnp.exp(recent - top)
    total = jnp.sum(past_w, -1) + jnp.sum(recent_w, -1)
    mixed = jnp.einsum(
        "tshgc,schd->tshgd",
        past_w.astype(jnp.bfloat16),
        cache[:, :, :, 1],
        preferred_element_type=jnp.float32,
    )
    mixed = mixed + jnp.einsum(
        "tshgu,ushd->tshgd",
        recent_w.astype(jnp.bfloat16),
        fresh[:, :, :, 1],
        preferred_element_type=jnp.float32,
    )
    result = mixed / total[..., None]
    return result.reshape(steps_count, seq_count, width).astype(jnp.bfloat16)


def on_device(hidden, kv_weight, owner, queries, pool, page_table, lengths, send_pages):
    replicas = lax.axis_size("replica")
    tensors = lax.axis_size("tensor")
    steps_count, seq_count, feature_part = hidden.shape
    row_count = steps_count * seq_count
    gathered = lax.all_gather(kv_weight, "replica", axis=0, tiled=True)
    kv_total = gathered.shape[0]
    kv_width = kv_total // tensors
    weight = jnp.take(
        gathered.reshape(replicas, kv_total // replicas, feature_part), owner, axis=0
    ).reshape(kv_total, feature_part)
    flat_rows = hidden.reshape(row_count, feature_part)
    local_weight = lax.all_to_all(weight, "tensor", split_axis=0, concat_axis=1, tiled=True)
    fresh = lax.dot_general(
        lax.all_gather(flat_rows, "tensor", axis=1, tiled=True),
        local_weight,
        (((1,), (1,)), ((), ())),
        preferred_element_type=jnp.float32,
    )
    new_kv = fresh.astype(jnp.bfloat16).reshape(steps_count, seq_count, kv_width)
    page_size = pool.shape[1]
    outgoing = jnp.take(pool, send_pages.reshape(-1), axis=0).reshape(
        replicas, -1, page_size, kv_width
    )
    arrived = lax.all_to_all(outgoing, "replica", split_axis=0, concat_axis=0, tiled=True)
    store = jnp.concatenate([pool, arrived.reshape(-1, page_size, kv_width)], axis=0)
    cache = jnp.take(store, page_table.reshape(-1), axis=0).reshape(seq_count, -1, kv_width)
    attended = attend(queries, cache, new_kv, lengths)
    return (new_kv, attended)


def solution(mesh):
    in_specs = (
        P(None, "replica", "tensor"),
        P("replica", "tensor"),
        P(),
        P(None, "replica", "tensor"),
        P("replica", None, "tensor"),
        P("replica", None),
        P("replica"),
        P("replica", None, None),
    )
    out_specs = (P(None, "replica", "tensor"), P(None, "replica", "tensor"))
    return jax.shard_map(
        on_device, mesh=mesh, in_specs=in_specs, out_specs=out_specs, check_vma=False
    )
```

profile of v0, /device:TPU:6, one launch (start us, length us, event | category | flops | bytes accessed | tf_op | source)
XLA Modules:
  0.0 640.6 jit_solution(8822864193652723364)
XLA Ops:
  8.0 0.7 all-gather.3.cloned.1.call-update
  8.7 0.8 copy.33
  9.5 0.1 reshape.235
  9.6 0.7 compare_and_fusion.1
  10.5 2.1 gather_fusion.1
  12.5 1.3 broadcast_select_fusion
  13.8 12.2 %all-to-all-start.1 = ((bf16[64,2,16,256]{3,2,1,0:T(8,128)(2,1)}), bf16[64,2,16,256]{3,2,1,0:T(8,128)(2,1)S(1)}, u32[]{:S(2)}, u32[]{:S(2)}) async-start(bf16[64,2,16,256]{3,2,1,0:T(8,128)(2,1)} %broadcast_select_fusion), calls=%async_computation.1 | async-start | bytes 2097152 | tf_op jit(solution)/shard_map/all_to_all | solution.py:78
  26.3 314.0 %all-gather.3.cloned.1.call-done = bf16[2048,1024]{1,0:T(8,128)(2,1)} async-done(((bf16[32,1024]{1,0:T(8,128)(2,1)}), bf16[2048,1024]{1,0:T(8,128)(2,1)}) %all-gather.3.cloned.1.call-update) | async-done | bytes 4194320 | tf_op jit(solution)/shard_map/all_gather | solution.py:59
  340.4 5.0 gather_fusion
  345.3 3.8 bitcast_select_fusion
  349.2 1.0 copy-done
  350.2 11.3 %all-to-all-start = ((bf16[8,256,1024]{2,1,0:T(8,128)(2,1)}), bf16[8,256,1024]{2,1,0:T(8,128)(2,1)}, u32[]{:S(2)}, u32[]{:S(2)}) async-start(bf16[8,256,1024]{2,1,0:T(8,128)(2,1)} %bitcast_select_fusion), calls=%async_computation | async-start | bytes 8388608 | tf_op jit(solution)/shard_map/all_to_all | solution.py:66
  361.5 0.5 all-gather.5.cloned.1.call-update
  362.1 0.9 copy.49
  363.4 2.0 pad_maximum_fusion
  365.4 2.0 gather_fusion.2
  367.4 2.4 gather.23
  369.8 0.6 copy_select_fusion
  370.4 0.4 copy-done.1
  370.8 0.7 fusion.21
  371.5 233.9 %all-to-all-done = bf16[8,256,1024]{2,1,0:T(8,128)(2,1)} async-done(((bf16[8,256,1024]{2,1,0:T(8,128)(2,1)}), bf16[8,256,1024]{2,1,0:T(8,128)(2,1)}, u32[]{:S(2)}, u32[]{:S(2)}) %all-to-all-start) | async-done | bytes 4194336 | tf_op jit(solution)/shard_map/all_to_all | solution.py:66
  605.5 6.5 %copy.30 = bf16[256,8,1024]{0,2,1:T(8,128)(2,1)} copy(bf16[256,8,1024]{2,0,1:T(8,128)(2,1)} %bitcast.2) | data formatting | bytes 8388608 | tf_op jit(solution)/shard_map/all_to_all | solution.py:66
  612.0 10.2 %all-gather.5.cloned.1.call-done = bf16[256,8192]{1,0:T(8,128)(2,1)} async-done(((bf16[256,1024]{1,0:T(8,128)(2,1)}), bf16[256,8192]{1,0:T(8,128)(2,1)}) %all-gather.5.cloned.1.call-update) | async-done | bytes 4194320 | tf_op jit(solution)/shard_map/all_gather | solution.py:68
  622.2 4.8 convolution_convert_fusion
  627.0 0.2 fusion.20
  627.2 2.4 fusion.22
  629.7 0.7 fusion.6
  630.3 0.5 fusion.10
  630.8 0.4 fusion.8
  631.3 0.6 divide_convert_fusion
  631.9 0.2 convert_element_type.23
  632.1 1.1 copy.41
  (38 shorter events, 1.0 us)
Async XLA Ops:
  8.0 332.4 %all-gather.3.cloned.1.call-start = ((), (), s32[]{:S(2)}) async-start(), calls=%async_computation.2 | async-start | bytes 4259840 | tf_op jit(solution)/shard_map/all_gather | solution.py:59
  12.5 13.5 %copy-start.7 = (s32[64]{0:T(128)S(1)}, s32[64]{0:T(128)}, u32[]{:S(2)}) copy-start(s32[64]{0:T(128)} %param.10) | copy-start | bytes 772
  13.8 335.4 %all-to-all-start.1 = ((bf16[64,2,16,256]{3,2,1,0:T(8,128)(2,1)}), bf16[64,2,16,256]{3,2,1,0:T(8,128)(2,1)S(1)}, u32[]{:S(2)}, u32[]{:S(2)}) async-start(bf16[64,2,16,256]{3,2,1,0:T(8,128)(2,1)} %broadcast_select_fusion), calls=%async_computation.1 | async-start | bytes 2097152 | tf_op jit(solution)/shard_map/all_to_all | solution.py:78
  349.2 12.9 %copy-start.3 = (bf16[8,32,1024]{2,1,0:T(8,128)(2,1)S(1)}, bf16[8,32,1024]{2,1,0:T(8,128)(2,1)}, u32[]{:S(2)}) copy-start(bf16[8,32,1024]{2,1,0:T(8,128)(2,1)} %param.11) | copy-start | bytes 1572868
  349.2 13.8 %copy-start.5 = (s32[32,6]{0,1:T(8,128)S(1)}, s32[32,6]{0,1:T(8,128)}, u32[]{:S(2)}) copy-start(s32[32,6]{0,1:T(8,128)} %param.13) | copy-start | bytes 2308
  349.2 14.1 %copy-start.6 = (s32[32]{0:T(128)S(1)}, s32[32]{0:T(128)}, u32[]{:S(2)}) copy-start(s32[32]{0:T(128)} %param.14) | copy-start | bytes 388
  349.2 1.0 copy-start
  350.2 255.2 %all-to-all-start = ((bf16[8,256,1024]{2,1,0:T(8,128)(2,1)}), bf16[8,256,1024]{2,1,0:T(8,128)(2,1)}, u32[]{:S(2)}, u32[]{:S(2)}) async-start(bf16[8,256,1024]{2,1,0:T(8,128)(2,1)} %bitcast_select_fusion), calls=%async_computation | async-start | bytes 8388608 | tf_op jit(solution)/shard_map/all_to_all | solution.py:66
  361.5 260.7 %all-gather.5.cloned.1.call-start = ((), (), s32[]{:S(2)}) async-start(), calls=%async_computation.3 | async-start | bytes 4718592 | tf_op jit(solution)/shard_map/all_gather | solution.py:68
  369.8 1.0 copy-start.1
  622.2 5.0 copy-start.2
  627.0 3.8 copy-start.4
Sparse Core Ops, SparseCore 0:
  10.9 329.4 all-gather.2
Sparse Core Ops, SparseCore 1:
  364.1 258.1 all-gather.4
where the time goes:
time: 651 us; the launch traced here: 641 us
  waiting for transfers between devices  559 us (86%)
  starting transfers between devices  23.6 us (4%)
  local copies, waits for them, and re-layouts  23.4 us (4%)
  between operations  15.7 us (2%)
  other arithmetic  9.59 us (1%)
  matrix products  8.91 us (1%)
    all_gather x1, waiting for transfers between devices, on_device(): gathered = lax.all_gather(kv_weight, 'replica', axis=0, tiled=True)  314 us
    all_to_all x1, waiting for transfers between devices, on_device(): lax.all_to_all(weight, 'tensor', split_axis=0, concat_axis=1, tiled=True)  234 us
  transfers between devices with their start and end apart: 4, of which 3 were waited for; matrix products, arithmetic and copies ran while one was open for 5% of the time, Pallas kernels for 0%

commit v1 on v0

v1 whole, which is shorter than its diff:
```python
import jax
import jax.numpy as jnp
from jax import lax
from jax.experimental import pallas as pl
from jax.experimental.pallas import tpu as pltpu
from jax.sharding import Mesh, PartitionSpec as P

HD = 128
SIDE = 4
CORES = 2
AXES = ("x", "zl", "y", "zh", "c")
REPLICA = ("x", "zl", "y")
TENSOR = ("zh", "c")
RING = range(SIDE)


def flat_id(x, zl, y, zh, c):
    return (((x * SIDE + zl) * SIDE + y) * SIDE + zh) * CORES + c


def member(stage, c, line, k, zl, zh):
    along_y = (c == 0) == (stage == 1)
    return flat_id(line, zl, k, zh, c) if along_y else flat_id(k, zl, line, zh, c)


def lines(stage):
    return [
        [member(stage, c, line, k, zl, zh) for k in RING]
        for line in RING for zl in RING for zh in RING for c in range(CORES)
    ]


def shift(value, stage, step):
    pairs = [
        (group[k], group[(k + step) % SIDE]) for group in lines(stage) for k in RING
    ]
    return lax.ppermute(value, AXES, pairs)


def z_shift(value, step):
    return lax.ppermute(value, "zh", [(i, (i + step) % SIDE) for i in RING])


def core_swap(value):
    return lax.ppermute(value, "c", [(0, 1), (1, 0)])


def gather_weight(held):
    first = lax.all_to_all(
        jnp.broadcast_to(held[None], (SIDE,) + held.shape), "zl", 0, 0, tiled=True
    )
    block = first.reshape((1, SIDE * held.shape[0], held.shape[1]))
    second = lax.all_to_all(
        jnp.broadcast_to(block, (SIDE,) + block.shape[1:]),
        AXES, 0, 0, axis_index_groups=lines(1),
    )
    own = second.reshape(-1, held.shape[1])
    half = own.shape[0] // 2
    up = shift(own, 2, 1)
    down = shift(own, 2, -1)
    far_up = shift(up[:half], 2, 1)
    far_down = shift(down[half:], 2, -1)
    return own, up, down, far_up, far_down


def block_places(owner, c, q):
    x, y = lax.axis_index("x"), lax.axis_index("y")
    place = jnp.arange(64)
    slot, a1, zl = place // 16, (place // 4) % 4, place % 4
    me2 = jnp.where(c == 0, x, y)
    a2 = (me2 + jnp.where(slot == 0, 0, jnp.where(slot == 1, 3, jnp.where(slot == 2, 1, 2)))) % 4
    held = jnp.where(c == 0, a2 * 16 + zl * 4 + a1, a1 * 16 + zl * 4 + a2)
    block = jnp.sum(jnp.where(owner[None, :] == held[:, None], jnp.arange(64)[None, :], 0), axis=1)
    column = block // 8
    far = (column // 2 - q) % 4
    order = jnp.where(far == 2, 0, jnp.where(far == 1, 1, jnp.where(far == 3, 2, 3)))
    order = order + jnp.where(column % 2 == c, 4, 0)
    return (order * 8 + block % 8).astype(jnp.int32)


def project_kernel(places, rows, own, up, down, far_up, far_down, first, rest, mine, total, sems):
    base = 0
    for piece in (own, up, down, far_up, far_down):
        count = piece.shape[0] // 32
        product = lax.dot_general(
            piece[...], rows[...], (((1,), (1,)), ((), ())), preferred_element_type=jnp.float32
        )
        for b in range(count):
            at = pl.multiple_of(places[base + b] * 32, 32)
            total[pl.ds(at, 32), :] = product[b * 32:(b + 1) * 32]
        base += count
    copies = [
        pltpu.make_async_copy(total.at[pl.ds(0, 256)], first, sems.at[0]),
        pltpu.make_async_copy(total.at[pl.ds(256, 768)], rest, sems.at[1]),
        pltpu.make_async_copy(total.at[pl.ds(1024, 1024)], mine, sems.at[2]),
    ]
    for copy in copies:
        copy.start()
    for copy in copies:
        copy.wait()


def project(places, rows, pieces):
    count = rows.shape[0]
    vmem = pl.BlockSpec(memory_space=pltpu.VMEM)
    return pl.pallas_call(
        project_kernel,
        out_shape=[
            jax.ShapeDtypeStruct((256, count), jnp.float32),
            jax.ShapeDtypeStruct((768, count), jnp.float32),
            jax.ShapeDtypeStruct((1024, count), jnp.float32),
        ],
        in_specs=[pl.BlockSpec(memory_space=pltpu.SMEM)] + [vmem] * 6,
        out_specs=[pl.BlockSpec(memory_space=pl.ANY)] * 3,
        scratch_shapes=[
            pltpu.VMEM((2048, count), jnp.float32),
            pltpu.SemaphoreType.DMA((3,)),
        ],
        compiler_params=pltpu.CompilerParams(vmem_limit_bytes=24 * 2**20),
        name="project",
    )(places, rows, *pieces)


def reduce_columns(first, rest, mine):
    far = mine[:256] + core_swap(first)
    near = mine[256:] + core_swap(rest)
    up, down, here = near[:256], near[256:512], near[512:]
    via_up = z_shift(far[:128], 1)
    via_down = z_shift(far[128:], -1)
    up_v = z_shift(up[128:], 1)
    down_k = z_shift(down[:128], -1)
    up_k = z_shift(up[:128] + via_up, 1)
    down_v = z_shift(down[128:] + via_down, -1)
    return here + jnp.concatenate([up_k, up_v], 0) + jnp.concatenate([down_k, down_v], 0)


def attend(query_rows, cache, fresh, seq_lengths):
    steps_count, seq_count, width = query_rows.shape
    kv_heads = cache.shape[-1] // (2 * HD)
    group = width // (HD * kv_heads)
    span = cache.shape[1]
    query = query_rows.reshape(steps_count, seq_count, kv_heads, group, HD)
    cache = cache.reshape(seq_count, span, kv_heads, 2, HD)
    fresh = fresh.reshape(steps_count, seq_count, kv_heads, 2, HD)
    scale = HD ** (-0.5)
    past = (
        jnp.einsum(
            "tshgd,schd->tshgc", query, cache[:, :, :, 0], preferred_element_type=jnp.float32
        )
        * scale
    )
    recent = (
        jnp.einsum(
            "tshgd,ushd->tshgu", query, fresh[:, :, :, 0], preferred_element_type=jnp.float32
        )
        * scale
    )
    live = jnp.arange(span)[None, :] < seq_lengths[:, None]
    past = jnp.where(live[None, :, None, None, :], past, -jnp.inf)
    causal = jnp.arange(steps_count)[None, :] <= jnp.arange(steps_count)[:, None]
    recent = jnp.where(causal[:, None, None, None, :], recent, -jnp.inf)
    top = jnp.maximum(jnp.max(past, -1), jnp.max(recent, -1))[..., None]
    past_w = jnp.exp(past - top)
    recent_w = jnp.exp(recent - top)
    total = jnp.sum(past_w, -1) + jnp.sum(recent_w, -1)
    mixed = jnp.einsum(
        "tshgc,schd->tshgd",
        past_w.astype(jnp.bfloat16),
        cache[:, :, :, 1],
        preferred_element_type=jnp.float32,
    )
    mixed = mixed + jnp.einsum(
        "tshgu,ushd->tshgd",
        recent_w.astype(jnp.bfloat16),
        fresh[:, :, :, 1],
        preferred_element_type=jnp.float32,
    )
    result = mixed / total[..., None]
    return result.reshape(steps_count, seq_count, width).astype(jnp.bfloat16)


def on_device(hidden, kv_weight, owner, queries, pool, page_table, lengths, send_pages):
    steps_count, seq_count, feature_part = hidden.shape
    page_size, kv_width = pool.shape[1:]
    c, q = lax.axis_index("c"), lax.axis_index("zh")
    outgoing = jnp.take(pool, send_pages.reshape(-1), axis=0, mode="clip").reshape(
        64, -1, page_size, kv_width
    )
    arrived = lax.all_to_all(outgoing, REPLICA, split_axis=0, concat_axis=0, tiled=True)

    pieces = gather_weight(kv_weight)
    places = block_places(owner, c, q)
    first, rest, mine = project(places, hidden.reshape(-1, feature_part), pieces)
    fresh = reduce_columns(first, rest, mine)
    new_kv = fresh.T.astype(jnp.bfloat16).reshape(steps_count, seq_count, kv_width)

    store = jnp.concatenate([pool, arrived.reshape(-1, page_size, kv_width)], axis=0)
    cache = jnp.take(store, page_table.reshape(-1), axis=0, mode="clip").reshape(seq_count, -1, kv_width)
    attended = attend(queries, cache, new_kv, lengths)
    return (new_kv, attended)


def solution(mesh):
    fine = Mesh(mesh.devices.reshape(SIDE, SIDE, SIDE, SIDE, CORES), AXES)
    in_specs = (
        P(None, REPLICA, TENSOR),
        P(REPLICA, TENSOR),
        P(),
        P(None, REPLICA, TENSOR),
        P(REPLICA, None, TENSOR),
        P(REPLICA, None),
        P(REPLICA),
        P(REPLICA, None, None),
    )
    out_specs = (P(None, REPLICA, TENSOR), P(None, REPLICA, TENSOR))
    return jax.shard_map(
        on_device, mesh=fine, in_specs=in_specs, out_specs=out_specs, check_vma=False
    )
```

time: 651 us -> 175 us (0.27)
  the two profiles are of different devices: /device:TPU:6 before, /device:TPU:14 now
where the time goes in v1:
time: 175 us; the launch traced here: 174 us
  waiting for transfers between devices  68.8 us (39%)
  starting transfers between devices  61.1 us (35%)
  local copies, waits for them, and re-layouts  17.2 us (10%)
  blocking collectives  14.6 us (8%)
  matrix products  5.14 us (3%)
  other arithmetic  3.64 us (2%)
  Pallas kernels  2.73 us (2%)
    ppermute x6, waiting for transfers between devices, z_shift(): return lax.ppermute(value, 'zh', [(i, (i + step) % SIDE) for i in RING])  33.5 us
    ppermute x6, starting transfers between devices, z_shift(): return lax.ppermute(value, 'zh', [(i, (i + step) % SIDE) for i in RING])  31.6 us
    ppermute x4, waiting for transfers between devices, shift(): return lax.ppermute(value, AXES, pairs)  26.7 us
    all_to_all x1, blocking collectives, gather_weight(): lax.all_to_all(jnp.broadcast_to(held[None], (SIDE,) + held.shape), 'zl',...  14.6 us
    ppermute x4, starting transfers between devices, shift(): return lax.ppermute(value, AXES, pairs)  12.1 us
    all_to_all x1, starting transfers between devices, on_device(): lax.all_to_all(outgoing, REPLICA, split_axis=0, concat_axis=0, tiled=True)  8.14 us
    all_to_all x1, waiting for transfers between devices, gather_weight(): lax.all_to_all(jnp.broadcast_to(block, (SIDE,) + block.shape[1:]), AXES,...  7.54 us
    all_to_all x1, starting transfers between devices, gather_weight(): lax.all_to_all(jnp.broadcast_to(block, (SIDE,) + block.shape[1:]), AXES,...  4.91 us
  transfers between devices with their start and end apart: 14, of which 10 were waited for; matrix products, arithmetic and copies ran while one was open for 5% of the time, Pallas kernels for 2%

profile of v1, /device:TPU:14, one launch (start us, length us, event | category | flops | bytes accessed | tf_op | source)
XLA Modules:
  0.0 174.3 jit_solution(2786761936098179194)
XLA Ops:
  1.5 14.6 %all_to_all.15 = bf16[4,32,1024]{2,1,0:T(8,128)(2,1)S(1)} all-to-all(bf16[4,32,1024]{2,1,0:T(8,128)(2,1)S(1)} %broadcast_in_dim.86), channel_id=1, replica_groups=mesh['x'=4,'zl'=4,'y'=4,'zh'=4,'c'=2] {'zl'}, dimensions={0} | all-to-all | bytes 524288 | tf_op jit(solution)/shard_map/all_to_all | solution.py:49
  16.1 1.1 broadcast_in_dim.88
  17.2 4.9 %all-to-all-start.1 = ((bf16[4,128,1024]{2,1,0:T(8,128)(2,1)}), bf16[4,128,1024]{2,1,0:T(8,128)(2,1)S(1)}, u32[]{:S(2)}, u32[]{:S(2)}) async-start(bf16[4,128,1024]{2,1,0:T(8,128)(2,1)} %broadcast_in_dim.88), calls=%async_computation.1 | async-start | bytes 2097152 | tf_op jit(solution)/shard_map/all_to_all | solution.py:53
  22.4 1.6 gather_fusion
  24.0 7.5 %all-to-all-done.1 = bf16[4,128,1024]{2,1,0:T(8,128)(2,1)S(1)} async-done(((bf16[4,128,1024]{2,1,0:T(8,128)(2,1)}), bf16[4,128,1024]{2,1,0:T(8,128)(2,1)S(1)}, u32[]{:S(2)}, u32[]{:S(2)}) %all-to-all-start.1) | async-done | bytes 1048608 | tf_op jit(solution)/shard_map/all_to_all | solution.py:53
  31.5 8.1 %all-to-all-start.2 = ((bf16[64,2,16,256]{3,2,1,0:T(8,128)(2,1)}), bf16[64,2,16,256]{3,2,1,0:T(8,128)(2,1)}, u32[]{:S(2)}, u32[]{:S(2)}) async-start(bf16[64,2,16,256]{3,2,1,0:T(8,128)(2,1)} %bitcast.90), calls=%async_computation.2 | async-start | bytes 2097152 | tf_op jit(solution)/shard_map/all_to_all | solution.py:189
  39.7 2.3 %collective-permute-start = (bf16[512,1024]{1,0:T(8,128)(2,1)S(1)}, bf16[512,1024]{1,0:T(8,128)(2,1)S(1)}, u32[]{:S(2)}, u32[]{:S(2)}) collective-permute-start(bf16[512,1024]{1,0:T(8,128)(2,1)S(1)} %bitcast.86), channel_id=1, source_target_pairs={{0,128},{128,256},{256,384},{384,0},{1,9},{9,17},{17,25},{25,1},{2... | collective-permute-start | bytes 3145736 | tf_op jit(solution)/shard_map/ppermute | solution.py:37
  42.0 3.6 %collective-permute-start.1 = (bf16[512,1024]{1,0:T(8,128)(2,1)S(1)}, bf16[512,1024]{1,0:T(8,128)(2,1)S(1)}, u32[]{:S(2)}, u32[]{:S(2)}) collective-permute-start(bf16[512,1024]{1,0:T(8,128)(2,1)S(1)} %bitcast.87), channel_id=1, source_target_pairs={{0,384},{128,0},{256,128},{384,256},{1,25},{9,1},{17,9},{25,17},{2... | collective-permute-start | bytes 3145736 | tf_op jit(solution)/shard_map/ppermute | solution.py:37
  45.6 16.3 %collective-permute-done.up = bf16[512,1024]{1,0:T(8,128)(2,1)S(1)} collective-permute-done((bf16[512,1024]{1,0:T(8,128)(2,1)S(1)}, bf16[512,1024]{1,0:T(8,128)(2,1)S(1)}, u32[]{:S(2)}, u32[]{:S(2)}) %collective-permute-start) | collective-permute-done | bytes 1048608 | tf_op jit(solution)/shard_map/ppermute | solution.py:37
  62.7 4.4 %collective-permute-start.2 = (bf16[256,1024]{1,0:T(8,128)(2,1)}, bf16[256,1024]{1,0:T(8,128)(2,1)}, u32[]{:S(2)}, u32[]{:S(2)}) collective-permute-start(bf16[256,1024]{1,0:T(8,128)(2,1)} %slice.70), channel_id=1, source_target_pairs={{0,128},{128,256},{256,384},{384,0},{1,9},{9,17},{17,25},{25,1},{2... | collective-permute-start | bytes 1572872 | tf_op jit(solution)/shard_map/ppermute | solution.py:37
  67.9 1.9 %collective-permute-start.3 = (bf16[256,1024]{1,0:T(8,128)(2,1)}, bf16[256,1024]{1,0:T(8,128)(2,1)}, u32[]{:S(2)}, u32[]{:S(2)}) collective-permute-start(bf16[256,1024]{1,0:T(8,128)(2,1)} %slice.71), channel_id=1, source_target_pairs={{0,384},{128,0},{256,128},{384,256},{1,25},{9,1},{17,9},{25,17},{2... | collective-permute-start | bytes 1572872 | tf_op jit(solution)/shard_map/ppermute | solution.py:37
  70.1 4.0 %collective-permute-done.2.far_up = bf16[256,1024]{1,0:T(8,128)(2,1)} collective-permute-done((bf16[256,1024]{1,0:T(8,128)(2,1)}, bf16[256,1024]{1,0:T(8,128)(2,1)}, u32[]{:S(2)}, u32[]{:S(2)}) %collective-permute-start.2) | collective-permute-done | bytes 524320 | tf_op jit(solution)/shard_map/ppermute | solution.py:37
  74.0 6.4 %collective-permute-done.3.far_down = bf16[256,1024]{1,0:T(8,128)(2,1)} collective-permute-done((bf16[256,1024]{1,0:T(8,128)(2,1)}, bf16[256,1024]{1,0:T(8,128)(2,1)}, u32[]{:S(2)}, u32[]{:S(2)}) %collective-permute-start.3) | collective-permute-done | bytes 524320 | tf_op jit(solution)/shard_map/ppermute | solution.py:37
  81.5 2.7 %project.1 = (f32[256,256]{1,0:T(8,128)S(1)}, f32[768,256]{1,0:T(8,128)S(1)}, f32[1024,256]{1,0:T(8,128)S(1)}) custom-call(s32[64]{0:T(128)S(1)} %fusion.22.places, bf16[256,1024]{1,0:T(8,128)(2,1)S(1)} %bitcast.89, bf16[512,1024]{1,0:T(8,128)(2,1)S(1)} %bitcast.88, bf16[512,1024]{1,0:T(8,128)(2,1)S(1)} %collective-permute-done.up, ...), custom_call_target="tpu_custom_call" | custom-call | tf_op jit(solution)/shard_map/project/pallas_call | solution.py:106
  84.3 1.9 %collective-permute-start.4 = (f32[768,256]{1,0:T(8,128)S(1)}, f32[768,256]{1,0:T(8,128)S(1)}, u32[]{:S(2)}, u32[]{:S(2)}) collective-permute-start(f32[768,256]{1,0:T(8,128)S(1)} %get-tuple-element.6), channel_id=1, source_target_pairs={{0,1},{1,0},{2,3},{3,2},{4,5},{5,4},{6,7},{7,6},{8,9},{9,8},{10,11... | collective-permute-start | bytes 2359304 | tf_op jit(solution)/shard_map/ppermute | solution.py:45
  86.2 2.4 %collective-permute-start.5 = (f32[256,256]{1,0:T(8,128)S(1)}, f32[256,256]{1,0:T(8,128)S(1)}, u32[]{:S(2)}, u32[]{:S(2)}) collective-permute-start(f32[256,256]{1,0:T(8,128)S(1)} %get-tuple-element.7), channel_id=1, source_target_pairs={{0,1},{1,0},{2,3},{3,2},{4,5},{5,4},{6,7},{7,6},{8,9},{9,8},{10,11... | collective-permute-start | bytes 786440 | tf_op jit(solution)/shard_map/ppermute | solution.py:45
  89.8 9.1 %collective-permute-start.6 = (f32[128,256]{1,0:T(8,128)S(1)}, f32[128,256]{1,0:T(8,128)S(1)}, u32[]{:S(2)}, u32[]{:S(2)}) collective-permute-start(f32[128,256]{1,0:T(8,128)S(1)} %get-tuple-element.20), channel_id=1, source_target_pairs={{0,2},{2,4},{4,6},{6,0},{1,3},{3,5},{5,7},{7,1},{8,10},{10,12},{12... | collective-permute-start | bytes 393224 | tf_op jit(solution)/shard_map/ppermute | solution.py:41
  99.0 3.0 %collective-permute-start.10 = (f32[128,256]{1,0:T(8,128)S(1)}, f32[128,256]{1,0:T(8,128)S(1)}, u32[]{:S(2)}, u32[]{:S(2)}) collective-permute-start(f32[128,256]{1,0:T(8,128)S(1)} %get-tuple-element.21), channel_id=1, source_target_pairs={{0,6},{2,0},{4,2},{6,4},{1,7},{3,1},{5,3},{7,5},{8,14},{10,8},{12,... | collective-permute-start | bytes 393224 | tf_op jit(solution)/shard_map/ppermute | solution.py:41
  102.1 2.1 %collective-permute-done.6 = f32[128,256]{1,0:T(8,128)S(1)} collective-permute-done((f32[128,256]{1,0:T(8,128)S(1)}, f32[128,256]{1,0:T(8,128)S(1)}, u32[]{:S(2)}, u32[]{:S(2)}) %collective-permute-start.6) | collective-permute-done | bytes 131104 | tf_op jit(solution)/shard_map/ppermute | solution.py:41
  104.2 11.0 %collective-permute-done.10 = f32[128,256]{1,0:T(8,128)S(1)} collective-permute-done((f32[128,256]{1,0:T(8,128)S(1)}, f32[128,256]{1,0:T(8,128)S(1)}, u32[]{:S(2)}, u32[]{:S(2)}) %collective-permute-start.10) | collective-permute-done | bytes 131104 | tf_op jit(solution)/shard_map/ppermute | solution.py:41
  115.3 5.2 %collective-permute-start.11 = (f32[128,256]{1,0:T(8,128)S(1)}, f32[128,256]{1,0:T(8,128)S(1)}, u32[]{:S(2)}, u32[]{:S(2)}) collective-permute-start(f32[128,256]{1,0:T(8,128)S(1)} %get-tuple-element.17), channel_id=1, source_target_pairs={{0,6},{2,0},{4,2},{6,4},{1,7},{3,1},{5,3},{7,5},{8,14},{10,8},{12,... | collective-permute-start | bytes 393224 | tf_op jit(solution)/shard_map/ppermute | solution.py:41
  120.5 9.2 %collective-permute-start.9 = (f32[128,256]{1,0:T(8,128)S(1)}, f32[128,256]{1,0:T(8,128)S(1)}, u32[]{:S(2)}, u32[]{:S(2)}) collective-permute-start(f32[128,256]{1,0:T(8,128)S(1)} %get-tuple-element.18), channel_id=1, source_target_pairs={{0,6},{2,0},{4,2},{6,4},{1,7},{3,1},{5,3},{7,5},{8,14},{10,8},{12,... | collective-permute-start | bytes 393224 | tf_op jit(solution)/shard_map/ppermute | solution.py:41
  129.7 1.9 %collective-permute-start.8 = (f32[128,256]{1,0:T(8,128)S(1)}, f32[128,256]{1,0:T(8,128)S(1)}, u32[]{:S(2)}, u32[]{:S(2)}) collective-permute-start(f32[128,256]{1,0:T(8,128)S(1)} %get-tuple-element.19), channel_id=1, source_target_pairs={{0,2},{2,4},{4,6},{6,0},{1,3},{3,5},{5,7},{7,1},{8,10},{10,12},{12... | collective-permute-start | bytes 393224 | tf_op jit(solution)/shard_map/ppermute | solution.py:41
  131.6 3.2 %collective-permute-start.7 = (f32[128,256]{1,0:T(8,128)S(1)}, f32[128,256]{1,0:T(8,128)S(1)}, u32[]{:S(2)}, u32[]{:S(2)}) collective-permute-start(f32[128,256]{1,0:T(8,128)S(1)} %get-tuple-element.16), channel_id=1, source_target_pairs={{0,2},{2,4},{4,6},{6,0},{1,3},{3,5},{5,7},{7,1},{8,10},{10,12},{12... | collective-permute-start | bytes 393224 | tf_op jit(solution)/shard_map/ppermute | solution.py:41
  135.4 15.9 %collective-permute-done.8 = f32[128,256]{1,0:T(8,128)S(1)} collective-permute-done((f32[128,256]{1,0:T(8,128)S(1)}, f32[128,256]{1,0:T(8,128)S(1)}, u32[]{:S(2)}, u32[]{:S(2)}) %collective-permute-start.8) | collective-permute-done | bytes 131104 | tf_op jit(solution)/shard_map/ppermute | solution.py:41
  151.3 4.2 %collective-permute-done.7 = f32[128,256]{1,0:T(8,128)S(1)} collective-permute-done((f32[128,256]{1,0:T(8,128)S(1)}, f32[128,256]{1,0:T(8,128)S(1)}, u32[]{:S(2)}, u32[]{:S(2)}) %collective-permute-start.7) | collective-permute-done | bytes 131104 | tf_op jit(solution)/shard_map/ppermute | solution.py:41
  156.0 3.4 %fusion.33 = (f32[8,32,8]{2,0,1:T(8,128)S(1)}, f32[8,32,1,8,8]{3,4,0,1,2:T(8,128)}) fusion(bf16[8,32,1,1,128]{4,3,1,0,2:T(2,128)(2,1)S(1)} %get-tuple-element.23, pred[8,8]{1,0:T(8,128)(4,1)S(1)} %iota_compare_fusion.1, bf16[8,32,8,128]{3,2,1,0:T(8,128)(2,1)S(1)} %bitcast.91), kind=kOutput, calls=%fused_computation.87 | convolution fusion | flops 4241408 | bytes 663616 | tf_op jit(solution)/shard_map/tshgd,ushd->tshgu/dot_general | solution.py:153
  159.4 2.0 %pad_maximum_fusion = bf16[320,16,256]{2,1,0:T(8,128)(2,1)S(1)} fusion(bf16[128,16,256]{2,1,0:T(8,128)(2,1)} %bitcast.6, bf16[192,16,256]{2,1,0:T(8,128)(2,1)} %param.12), kind=kLoop, calls=%fused_computation.2 | loop fusion | flops 1310720 | bytes 5242880 | tf_op jit(solution)/shard_map/concatenate | solution.py:197
  161.3 2.0 %gather_fusion.1 = bf16[192,16,256]{2,1,0:T(8,128)(2,1)} fusion(bf16[320,16,256]{2,1,0:T(8,128)(2,1)S(1)} %pad_maximum_fusion, s32[1024]{0:T(1024)S(1)} %pad_clamp_fusion), kind=kCustom, calls=%fused_computation.1 | custom fusion | bytes 3146496 | tf_op jit(solution)/shard_map/jit(_take)/gather | solution.py:198
  163.4 2.4 %reshape_reshape.6 = bf16[32,96,1,2,128]{4,3,1,0,2:T(2,128)(2,1)S(1)} reshape(bf16[192,16,256]{2,1,0:T(8,128)(2,1)} %gather_fusion.1) | data formatting | bytes 3145728 | tf_op jit(solution)/shard_map/reshape;reshape | solution.py:143
  165.7 3.5 %fusion.29 = (bf16[32,96,1,1,128]{4,3,1,0,2:T(2,128)(2,1)S(1)}, bf16[32,96,1,1,128]{4,3,1,0,2:T(2,128)(2,1)S(1)}) fusion(bf16[32,96,1,2,128]{4,3,1,0,2:T(2,128)(2,1)S(1)} %reshape_reshape.6), kind=kLoop, calls=%fused_computation.83 | loop fusion | bytes 3145728 | tf_op jit(solution)/shard_map/slice | solution.py:148
  173.2 1.1 copy.41
  (55 shorter events, 10.2 us)
Async XLA Ops:
  16.1 6.0 %copy-start.6 = (s32[1,64,2]{1,2,0:T(2,128)S(1)}, s32[1,64,2]{1,2,0:T(2,128)}, u32[]{:S(2)}) copy-start(s32[1,64,2]{1,2,0:T(2,128)} %param.15) | copy-start | bytes 1540
  16.1 6.3 %copy-start.1 = (bf16[192,16,256]{2,1,0:T(8,128)(2,1)S(1)}, bf16[192,16,256]{2,1,0:T(8,128)(2,1)}, u32[]{:S(2)}) copy-start(bf16[192,16,256]{2,1,0:T(8,128)(2,1)} %param.12) | copy-start | bytes 4718596
  17.2 14.3 %all-to-all-start.1 = ((bf16[4,128,1024]{2,1,0:T(8,128)(2,1)}), bf16[4,128,1024]{2,1,0:T(8,128)(2,1)S(1)}, u32[]{:S(2)}, u32[]{:S(2)}) async-start(bf16[4,128,1024]{2,1,0:T(8,128)(2,1)} %broadcast_in_dim.88), calls=%async_computation.1 | async-start | bytes 2097152 | tf_op jit(solution)/shard_map/all_to_all | solution.py:53
  31.5 127.8 %all-to-all-start.2 = ((bf16[64,2,16,256]{3,2,1,0:T(8,128)(2,1)}), bf16[64,2,16,256]{3,2,1,0:T(8,128)(2,1)}, u32[]{:S(2)}, u32[]{:S(2)}) async-start(bf16[64,2,16,256]{3,2,1,0:T(8,128)(2,1)} %bitcast.90), calls=%async_computation.2 | async-start | bytes 2097152 | tf_op jit(solution)/shard_map/all_to_all | solution.py:189
  39.7 30.1 %copy-start.8 = (s32[64]{0:T(128)S(1)}, s32[64]{0:T(128)}, u32[]{:S(2)}) copy-start(s32[64]{0:T(128)} %param.10) | copy-start | bytes 772
  39.7 22.1 %collective-permute-start = (bf16[512,1024]{1,0:T(8,128)(2,1)S(1)}, bf16[512,1024]{1,0:T(8,128)(2,1)S(1)}, u32[]{:S(2)}, u32[]{:S(2)}) collective-permute-start(bf16[512,1024]{1,0:T(8,128)(2,1)S(1)} %bitcast.86), channel_id=1, source_target_pairs={{0,128},{128,256},{256,384},{384,0},{1,9},{9,17},{17,25},{25,1},{2... | collective-permute-start | bytes 3145736 | tf_op jit(solution)/shard_map/ppermute | solution.py:37
  42.0 25.1 %collective-permute-start.1 = (bf16[512,1024]{1,0:T(8,128)(2,1)S(1)}, bf16[512,1024]{1,0:T(8,128)(2,1)S(1)}, u32[]{:S(2)}, u32[]{:S(2)}) collective-permute-start(bf16[512,1024]{1,0:T(8,128)(2,1)S(1)} %bitcast.87), channel_id=1, source_target_pairs={{0,384},{128,0},{256,128},{384,256},{1,25},{9,1},{17,9},{25,17},{2... | collective-permute-start | bytes 3145736 | tf_op jit(solution)/shard_map/ppermute | solution.py:37
  62.7 11.4 %collective-permute-start.2 = (bf16[256,1024]{1,0:T(8,128)(2,1)}, bf16[256,1024]{1,0:T(8,128)(2,1)}, u32[]{:S(2)}, u32[]{:S(2)}) collective-permute-start(bf16[256,1024]{1,0:T(8,128)(2,1)} %slice.70), channel_id=1, source_target_pairs={{0,128},{128,256},{256,384},{384,0},{1,9},{9,17},{17,25},{25,1},{2... | collective-permute-start | bytes 1572872 | tf_op jit(solution)/shard_map/ppermute | solution.py:37
  67.9 12.6 %collective-permute-start.3 = (bf16[256,1024]{1,0:T(8,128)(2,1)}, bf16[256,1024]{1,0:T(8,128)(2,1)}, u32[]{:S(2)}, u32[]{:S(2)}) collective-permute-start(bf16[256,1024]{1,0:T(8,128)(2,1)} %slice.71), channel_id=1, source_target_pairs={{0,384},{128,0},{256,128},{384,256},{1,25},{9,1},{17,9},{25,17},{2... | collective-permute-start | bytes 1572872 | tf_op jit(solution)/shard_map/ppermute | solution.py:37
  80.5 1.0 copy-start
  81.5 7.1 %copy-start.7 = (s32[32]{0:T(128)S(1)}, s32[32]{0:T(128)}, u32[]{:S(2)}) copy-start(s32[32]{0:T(128)} %param.14) | copy-start | bytes 388
  84.3 17.7 %collective-permute-start.4 = (f32[768,256]{1,0:T(8,128)S(1)}, f32[768,256]{1,0:T(8,128)S(1)}, u32[]{:S(2)}, u32[]{:S(2)}) collective-permute-start(f32[768,256]{1,0:T(8,128)S(1)} %get-tuple-element.6), channel_id=1, source_target_pairs={{0,1},{1,0},{2,3},{3,2},{4,5},{5,4},{6,7},{7,6},{8,9},{9,8},{10,11... | collective-permute-start | bytes 2359304 | tf_op jit(solution)/shard_map/ppermute | solution.py:45
  86.2 3.6 %collective-permute-start.5 = (f32[256,256]{1,0:T(8,128)S(1)}, f32[256,256]{1,0:T(8,128)S(1)}, u32[]{:S(2)}, u32[]{:S(2)}) collective-permute-start(f32[256,256]{1,0:T(8,128)S(1)} %get-tuple-element.7), channel_id=1, source_target_pairs={{0,1},{1,0},{2,3},{3,2},{4,5},{5,4},{6,7},{7,6},{8,9},{9,8},{10,11... | collective-permute-start | bytes 786440 | tf_op jit(solution)/shard_map/ppermute | solution.py:45
  89.8 14.4 %collective-permute-start.6 = (f32[128,256]{1,0:T(8,128)S(1)}, f32[128,256]{1,0:T(8,128)S(1)}, u32[]{:S(2)}, u32[]{:S(2)}) collective-permute-start(f32[128,256]{1,0:T(8,128)S(1)} %get-tuple-element.20), channel_id=1, source_target_pairs={{0,2},{2,4},{4,6},{6,0},{1,3},{3,5},{5,7},{7,1},{8,10},{10,12},{12... | collective-permute-start | bytes 393224 | tf_op jit(solution)/shard_map/ppermute | solution.py:41
  98.9 35.9 %copy-start.5 = (s32[32,6]{0,1:T(8,128)S(1)}, s32[32,6]{0,1:T(8,128)}, u32[]{:S(2)}) copy-start(s32[32,6]{0,1:T(8,128)} %param.13) | copy-start | bytes 2308
  98.9 36.1 %copy-start.3 = (bf16[8,32,1024]{2,1,0:T(8,128)(2,1)S(1)}, bf16[8,32,1024]{2,1,0:T(8,128)(2,1)}, u32[]{:S(2)}) copy-start(bf16[8,32,1024]{2,1,0:T(8,128)(2,1)} %param.11) | copy-start | bytes 1572868
  99.0 16.3 %collective-permute-start.10 = (f32[128,256]{1,0:T(8,128)S(1)}, f32[128,256]{1,0:T(8,128)S(1)}, u32[]{:S(2)}, u32[]{:S(2)}) collective-permute-start(f32[128,256]{1,0:T(8,128)S(1)} %get-tuple-element.21), channel_id=1, source_target_pairs={{0,6},{2,0},{4,2},{6,4},{1,7},{3,1},{5,3},{7,5},{8,14},{10,8},{12,... | collective-permute-start | bytes 393224 | tf_op jit(solution)/shard_map/ppermute | solution.py:41
  115.3 19.9 %collective-permute-start.11 = (f32[128,256]{1,0:T(8,128)S(1)}, f32[128,256]{1,0:T(8,128)S(1)}, u32[]{:S(2)}, u32[]{:S(2)}) collective-permute-start(f32[128,256]{1,0:T(8,128)S(1)} %get-tuple-element.17), channel_id=1, source_target_pairs={{0,6},{2,0},{4,2},{6,4},{1,7},{3,1},{5,3},{7,5},{8,14},{10,8},{12,... | collective-permute-start | bytes 393224 | tf_op jit(solution)/shard_map/ppermute | solution.py:41
  120.5 14.9 %collective-permute-start.9 = (f32[128,256]{1,0:T(8,128)S(1)}, f32[128,256]{1,0:T(8,128)S(1)}, u32[]{:S(2)}, u32[]{:S(2)}) collective-permute-start(f32[128,256]{1,0:T(8,128)S(1)} %get-tuple-element.18), channel_id=1, source_target_pairs={{0,6},{2,0},{4,2},{6,4},{1,7},{3,1},{5,3},{7,5},{8,14},{10,8},{12,... | collective-permute-start | bytes 393224 | tf_op jit(solution)/shard_map/ppermute | solution.py:41
  129.7 21.6 %collective-permute-start.8 = (f32[128,256]{1,0:T(8,128)S(1)}, f32[128,256]{1,0:T(8,128)S(1)}, u32[]{:S(2)}, u32[]{:S(2)}) collective-permute-start(f32[128,256]{1,0:T(8,128)S(1)} %get-tuple-element.19), channel_id=1, source_target_pairs={{0,2},{2,4},{4,6},{6,0},{1,3},{3,5},{5,7},{7,1},{8,10},{10,12},{12... | collective-permute-start | bytes 393224 | tf_op jit(solution)/shard_map/ppermute | solution.py:41
  131.6 23.9 %collective-permute-start.7 = (f32[128,256]{1,0:T(8,128)S(1)}, f32[128,256]{1,0:T(8,128)S(1)}, u32[]{:S(2)}, u32[]{:S(2)}) collective-permute-start(f32[128,256]{1,0:T(8,128)S(1)} %get-tuple-element.16), channel_id=1, source_target_pairs={{0,2},{2,4},{4,6},{6,0},{1,3},{3,5},{5,7},{7,1},{8,10},{10,12},{12... | collective-permute-start | bytes 393224 | tf_op jit(solution)/shard_map/ppermute | solution.py:41
  155.7 5.6 %copy-start.4 = (bf16[256,256]{1,0:T(8,128)(2,1)}, bf16[256,256]{1,0:T(8,128)(2,1)S(1)}, u32[]{:S(2)}) copy-start(bf16[256,256]{1,0:T(8,128)(2,1)S(1)} %copy.30) | copy-start | bytes 393220
  170.7 1.2 copy-start.2

commit v2 on v1

v2 whole, which is shorter than its diff:
```python
import jax
import jax.numpy as jnp
from jax import lax
from jax.experimental import pallas as pl
from jax.experimental.pallas import tpu as pltpu
from jax.sharding import Mesh, PartitionSpec as P

HD = 128
SIDE = 4
CORES = 2
SCALE = 16.0
SPAN = 96
WIDE = 128
AXES = ("x", "zl", "y", "zh", "c")
REPLICA = ("x", "zl", "y")
TENSOR = ("zh", "c")
RING = range(SIDE)


def flat_id(x, zl, y, zh, c):
    return (((x * SIDE + zl) * SIDE + y) * SIDE + zh) * CORES + c


def member(stage, c, line, k, zl, zh):
    along_y = (c == 0) == (stage == 1)
    return flat_id(line, zl, k, zh, c) if along_y else flat_id(k, zl, line, zh, c)


def lines(stage):
    return [
        [member(stage, c, line, k, zl, zh) for k in RING]
        for line in RING for zl in RING for zh in RING for c in range(CORES)
    ]


def shift(value, stage, step):
    pairs = [
        (group[k], group[(k + step) % SIDE]) for group in lines(stage) for k in RING
    ]
    return lax.ppermute(value, AXES, pairs)


def partner(zh, c, step):
    return zh ^ 1 if (c == 0) == (step == 1) else SIDE - 1 - zh


def z_exchange(value, step):
    pairs = [
        (zh * CORES + c, partner(zh, c, step) * CORES + c) for zh in RING for c in range(CORES)
    ]
    sent = (value * SCALE).astype(jnp.float16)
    return lax.ppermute(sent, TENSOR, pairs).astype(jnp.float32) * (1.0 / SCALE)


def core_swap(value):
    return lax.ppermute(value, "c", [(0, 1), (1, 0)])


def gather_weight(held):
    first = lax.all_to_all(
        jnp.broadcast_to(held[None], (SIDE,) + held.shape), "zl", 0, 0, tiled=True
    )
    block = first.reshape((1, SIDE * held.shape[0], held.shape[1]))
    second = lax.all_to_all(
        jnp.broadcast_to(block, (SIDE,) + block.shape[1:]),
        AXES, 0, 0, axis_index_groups=lines(1),
    )
    own = second.reshape(-1, held.shape[1])
    half = own.shape[0] // 2
    up_on, down_on = shift(own[:half], 2, 1), shift(own[half:], 2, -1)
    up_end, down_end = shift(own[half:], 2, 1), shift(own[:half], 2, -1)
    far_up, far_down = shift(up_on, 2, 1), shift(down_on, 2, -1)
    return own, up_on, up_end, down_end, down_on, far_up, far_down


def block_places(owner, c, q):
    x, y = lax.axis_index("x"), lax.axis_index("y")
    place = jnp.arange(64)
    slot, a1, zl = place // 16, (place // 4) % 4, place % 4
    me2 = jnp.where(c == 0, x, y)
    a2 = (me2 + jnp.where(slot == 0, 0, jnp.where(slot == 1, 3, jnp.where(slot == 2, 1, 2)))) % 4
    held = jnp.where(c == 0, a2 * 16 + zl * 4 + a1, a1 * 16 + zl * 4 + a2)
    block = jnp.sum(jnp.where(owner[None, :] == held[:, None], jnp.arange(64)[None, :], 0), axis=1)
    column = block // 8
    target, core = column // 2, column % 2
    order = jnp.where((target == (q ^ 1)) == (core == 0), 1, 2)
    order = jnp.where(target == q, 3, jnp.where(target == (q + 2) % 4, 0, order))
    order = order + jnp.where(core == c, 4, 0)
    return (order * 8 + block % 8).astype(jnp.int32)


def project_kernel(places, rows, own, up_on, up_end, down_end, down_on, far_up, far_down, away, near, late, total, sems):
    base = 0
    for piece in (own, up_on, up_end, down_end, down_on, far_up, far_down):
        count = piece.shape[0] // 32
        product = lax.dot_general(
            piece[...], rows[...], (((1,), (1,)), ((), ())), preferred_element_type=jnp.float32
        )
        for b in range(count):
            at = pl.multiple_of(places[base + b] * 32, 32)
            total[pl.ds(at, 32), :] = product[b * 32:(b + 1) * 32]
        base += count
    copies, base = [], 0
    for i, out in enumerate((away, near, late)):
        copies.append(pltpu.make_async_copy(total.at[pl.ds(base, out.shape[0])], out, sems.at[i]))
        base += out.shape[0]
    for copy in copies:
        copy.start()
    for copy in copies:
        copy.wait()


def project(places, rows, pieces):
    count = rows.shape[0]
    vmem = pl.BlockSpec(memory_space=pltpu.VMEM)
    return pl.pallas_call(
        project_kernel,
        out_shape=[
            jax.ShapeDtypeStruct((size, count), jnp.float32) for size in (1024, 512, 512)
        ],
        in_specs=[pl.BlockSpec(memory_space=pltpu.SMEM)] + [vmem] * 8,
        out_specs=[pl.BlockSpec(memory_space=pl.ANY)] * 3,
        scratch_shapes=[
            pltpu.VMEM((2048, count), jnp.float32),
            pltpu.SemaphoreType.DMA((3,)),
        ],
        compiler_params=pltpu.CompilerParams(vmem_limit_bytes=24 * 2**20),
        name="project",
    )(places, rows, *pieces)


def reduce_columns(away, near, late):
    got = core_swap(away)
    got_near = z_exchange(near + got[:512], 1)
    got_late = z_exchange(late[:256] + got[512:768] + got_near[:256], 2)
    return got, (late[256:], got[768:], got_near[256:], got_late)


def past_kernel(table, lengths, queries, pool, arrived, scores, folded, values, cells, wide):
    steps, seqs, _ = queries.shape
    pages = pool.shape[0]

    def fetch(s, _):
        for e in range(SPAN // 16):
            entry = table[s * (SPAN // 16) + e]
            mine = pool[jnp.minimum(entry, pages - 1)]
            sent = arrived[jnp.maximum(entry - pages, 0)]
            cells[s, e * 16:(e + 1) * 16] = jnp.where(entry < pages, mine, sent)
        return 0

    lax.fori_loop(0, seqs, fetch, 0, unroll=2)
    cells[:, SPAN:, :] = jnp.zeros((seqs, WIDE - SPAN, cells.shape[2]), cells.dtype)
    for t in range(steps):
        for h in range(8):
            wide[h, pl.ds(t * seqs, seqs), :] = queries[t, :, h * HD:(h + 1) * HD].astype(jnp.float32)
    for s in range(seqs):
        folded[s] = jnp.concatenate(
            [wide[h, pl.ds(s, steps, stride=seqs), :] for h in range(8)], axis=0
        ).astype(jnp.bfloat16)
    column = lax.broadcasted_iota(jnp.int32, (64, WIDE), 1)
    for s in range(seqs):
        scores[s] = lax.dot_general(
            folded[s], cells[s, :, :HD], (((1,), (1,)), ((), ())),
            preferred_element_type=jnp.float32,
        ) * (HD ** -0.5)
    for s in range(seqs):
        live = (column < lengths[s]) | (column >= SPAN)
        scores[s] = jnp.where(live, scores[s], -jnp.inf)
    for s in range(seqs):
        values[s] = cells[s, :, HD:]


def past(table, lengths, queries, pool, arrived):
    steps, seqs, _ = queries.shape
    smem = pl.BlockSpec(memory_space=pltpu.SMEM)
    vmem = pl.BlockSpec(memory_space=pltpu.VMEM)
    return pl.pallas_call(
        past_kernel,
        out_shape=[
            jax.ShapeDtypeStruct((seqs, 64, WIDE), jnp.float32),
            jax.ShapeDtypeStruct((seqs, 64, HD), jnp.bfloat16),
            jax.ShapeDtypeStruct((seqs, WIDE, HD), jnp.bfloat16),
        ],
        in_specs=[smem, smem, vmem, vmem, vmem],
        out_specs=[vmem, vmem, vmem],
        scratch_shapes=[
            pltpu.VMEM((seqs, WIDE, 2 * HD), jnp.bfloat16),
            pltpu.VMEM((8, steps * seqs, HD), jnp.float32),
        ],
        compiler_params=pltpu.CompilerParams(vmem_limit_bytes=24 * 2**20),
        cost_estimate=pl.CostEstimate(flops=70_000_000, bytes_accessed=8_000_000, transcendentals=0),
        name="past",
    )(table, lengths, queries, pool, arrived)


def finish_kernel(*refs):
    *parts, scores, folded, values, new_kv, attended, wide, keys, mixed, weights, totals, own = refs
    seqs = scores.shape[0]
    steps = new_kv.shape[0]
    fresh = parts[0][...].astype(jnp.float32)
    for part in parts[1:]:
        fresh = fresh + part[...].astype(jnp.float32)
    fresh = fresh.T.astype(jnp.bfloat16)
    for t in range(steps):
        new_kv[t] = fresh[t * seqs:(t + 1) * seqs]
    wide[0] = fresh[:, :HD].astype(jnp.float32)
    wide[1] = fresh[:, HD:].astype(jnp.float32)
    lanes = lax.broadcasted_iota(jnp.int32, (64, WIDE), 1)
    step = lax.broadcasted_iota(jnp.int32, (64, WIDE), 0) % steps
    later = (lanes - SPAN) > step
    zeros = jnp.zeros((16 - steps, HD), jnp.float32)
    keys[...] = jnp.zeros(keys.shape, keys.dtype)
    for s in range(seqs):
        key, value = (
            jnp.concatenate([wide[i, pl.ds(s, steps, stride=seqs), :], zeros], axis=0)
            for i in range(2)
        )
        keys[s, pl.ds(SPAN, 16), :] = key.astype(jnp.bfloat16)
        own[s] = value.astype(jnp.bfloat16)
    for s in range(seqs):
        recent = lax.dot_general(
            folded[s], keys[s], (((1,), (1,)), ((), ())), preferred_element_type=jnp.float32
        ) * (HD ** -0.5)
        mixed[pl.ds(s * 64, 64), :] = jnp.where(later, -jnp.inf, scores[s] + recent)
    for s in range(seqs):
        score = mixed[pl.ds(s * 64, 64), :]
        weight = jnp.exp(score - jnp.max(score, axis=1, keepdims=True))
        weights[s] = weight.astype(jnp.bfloat16)
        totals[s] = jnp.broadcast_to(jnp.sum(weight, axis=1, keepdims=True), (64, HD))
    for s in range(seqs):
        value = jnp.concatenate([values[s, :SPAN], own[s], values[s, SPAN + 16:]], axis=0)
        out = lax.dot_general(
            weights[s], value, (((1,), (0,)), ((), ())), preferred_element_type=jnp.float32
        )
        mixed[pl.ds(s * 64, 64), :] = out / totals[s]
    for t in range(steps):
        for h in range(8):
            attended[t, :, h * HD:(h + 1) * HD] = mixed[
                pl.ds(h * steps + t, seqs, stride=64), :
            ].astype(jnp.bfloat16)


def finish(parts, scores, folded, values, steps):
    seqs = scores.shape[0]
    vmem = pl.BlockSpec(memory_space=pltpu.VMEM)
    return pl.pallas_call(
        finish_kernel,
        out_shape=[
            jax.ShapeDtypeStruct((steps, seqs, 2 * HD), jnp.bfloat16),
            jax.ShapeDtypeStruct((steps, seqs, 8 * HD), jnp.bfloat16),
        ],
        in_specs=[vmem] * (len(parts) + 3),
        out_specs=[vmem, vmem],
        scratch_shapes=[
            pltpu.VMEM((2, steps * seqs, HD), jnp.float32),
            pltpu.VMEM((seqs, WIDE, HD), jnp.bfloat16),
            pltpu.VMEM((seqs * 64, HD), jnp.float32),
            pltpu.VMEM((seqs, 64, WIDE), jnp.bfloat16),
            pltpu.VMEM((seqs, 64, HD), jnp.float32),
            pltpu.VMEM((seqs, 16, HD), jnp.bfloat16),
        ],
        compiler_params=pltpu.CompilerParams(vmem_limit_bytes=24 * 2**20),
        cost_estimate=pl.CostEstimate(flops=140_000_000, bytes_accessed=4_000_000, transcendentals=262144),
        name="finish",
    )(*parts, scores, folded, values)


def on_device(hidden, kv_weight, owner, queries, pool, page_table, lengths, send_pages):
    steps_count, _, feature_part = hidden.shape
    page_size, kv_width = pool.shape[1:]
    c, q = lax.axis_index("c"), lax.axis_index("zh")
    outgoing = jnp.take(pool, send_pages.reshape(-1), axis=0, mode="clip").reshape(
        64, -1, page_size, kv_width
    )
    arrived = lax.all_to_all(outgoing, REPLICA, split_axis=0, concat_axis=0, tiled=True)

    pieces, arrived = lax.optimization_barrier((gather_weight(kv_weight), arrived))
    places = block_places(owner, c, q)
    swapped, parts = reduce_columns(*project(places, hidden.reshape(-1, feature_part), pieces))
    queries, _ = lax.optimization_barrier((queries, swapped))
    scores, folded, values = past(
        page_table.reshape(-1), lengths, queries, pool, arrived.reshape(-1, page_size, kv_width)
    )
    return tuple(finish(parts, scores, folded, values, steps_count))


def solution(mesh):
    fine = Mesh(mesh.devices.reshape(SIDE, SIDE, SIDE, SIDE, CORES), AXES)
    in_specs = (
        P(None, REPLICA, TENSOR),
        P(REPLICA, TENSOR),
        P(),
        P(None, REPLICA, TENSOR),
        P(REPLICA, None, TENSOR),
        P(REPLICA, None),
        P(REPLICA),
        P(REPLICA, None, None),
    )
    out_specs = (P(None, REPLICA, TENSOR), P(None, REPLICA, TENSOR))
    return jax.shard_map(
        on_device, mesh=fine, in_specs=in_specs, out_specs=out_specs, check_vma=False
    )
```

time: 175 us -> 121 us (0.69)
  the two profiles are of different devices: /device:TPU:14 before, /device:TPU:6 now
where the time goes in v2:
time: 121 us; the launch traced here: 120 us
  starting transfers between devices  45.5 us (38%)
  waiting for transfers between devices  44.4 us (37%)
  blocking collectives  14.6 us (12%)
  Pallas kernels  9.38 us (8%)
  local copies, waits for them, and re-layouts  5.11 us (4%)
    ppermute x2, waiting for transfers between devices, z_exchange(): return lax.ppermute(sent, TENSOR, pairs).astype(jnp.float32) * (1.0 / SCALE)  18.9 us
    ppermute x6, starting transfers between devices, shift(): return lax.ppermute(value, AXES, pairs)  17.5 us
    all_to_all x1, blocking collectives, gather_weight(): lax.all_to_all(jnp.broadcast_to(held[None], (SIDE,) + held.shape), 'zl',...  14.6 us
    ppermute x2, starting transfers between devices, z_exchange(): return lax.ppermute(sent, TENSOR, pairs).astype(jnp.float32) * (1.0 / SCALE)  14.4 us
    ppermute x6, waiting for transfers between devices, shift(): return lax.ppermute(value, AXES, pairs)  13.8 us
    all_to_all x1, waiting for transfers between devices, gather_weight(): lax.all_to_all(jnp.broadcast_to(block, (SIDE,) + block.shape[1:]), AXES,...  9.01 us
    all_to_all x1, starting transfers between devices, on_device(): lax.all_to_all(outgoing, REPLICA, split_axis=0, concat_axis=0, tiled=True)  7.24 us
    all_to_all x1, starting transfers between devices, gather_weight(): lax.all_to_all(jnp.broadcast_to(block, (SIDE,) + block.shape[1:]), AXES,...  4.46 us
  transfers between devices with their start and end apart: 11, of which 9 were waited for; matrix products, arithmetic and copies ran while one was open for 3% of the time, Pallas kernels for 3%

profile of v2, /device:TPU:6, one launch (start us, length us, event | category | flops | bytes accessed | tf_op | source)
XLA Modules:
  0.0 120.3 jit_solution(9150555971437558262)
XLA Ops:
  0.6 0.9 broadcast_in_dim.50
  1.5 14.6 %all_to_all.15 = bf16[4,32,1024]{2,1,0:T(8,128)(2,1)S(1)} all-to-all(bf16[4,32,1024]{2,1,0:T(8,128)(2,1)S(1)} %broadcast_in_dim.50), channel_id=1, replica_groups=mesh['x'=4,'zl'=4,'y'=4,'zh'=4,'c'=2] {'zl'}, dimensions={0} | all-to-all | bytes 524288 | tf_op jit(solution)/shard_map/all_to_all | solution.py:60
  16.1 1.1 broadcast_in_dim.52
  17.2 4.5 %all-to-all-start.1 = ((bf16[4,128,1024]{2,1,0:T(8,128)(2,1)}), bf16[4,128,1024]{2,1,0:T(8,128)(2,1)S(1)}, u32[]{:S(2)}, u32[]{:S(2)}) async-start(bf16[4,128,1024]{2,1,0:T(8,128)(2,1)} %broadcast_in_dim.52), calls=%async_computation.1 | async-start | bytes 2097152 | tf_op jit(solution)/shard_map/all_to_all | solution.py:64
  21.7 0.1 reshape.99
  21.9 1.6 %gather_fusion = bf16[128,16,256]{2,1,0:T(8,128)(2,1)} fusion(bf16[192,16,256]{2,1,0:T(8,128)(2,1)S(1)} %copy-done, s32[1024]{0:T(1024)S(1)} %pad_clamp_fusion), kind=kCustom, calls=%fused_computation | custom fusion | bytes 2097664 | tf_op jit(solution)/shard_map/jit(_take)/gather | solution.py:272
  23.5 9.0 %all-to-all-done.1 = bf16[4,128,1024]{2,1,0:T(8,128)(2,1)S(1)} async-done(((bf16[4,128,1024]{2,1,0:T(8,128)(2,1)}), bf16[4,128,1024]{2,1,0:T(8,128)(2,1)S(1)}, u32[]{:S(2)}, u32[]{:S(2)}) %all-to-all-start.1) | async-done | bytes 1048608 | tf_op jit(solution)/shard_map/all_to_all | solution.py:64
  32.5 7.2 %all-to-all-start.2 = ((bf16[64,2,16,256]{3,2,1,0:T(8,128)(2,1)}), bf16[64,2,16,256]{3,2,1,0:T(8,128)(2,1)}, u32[]{:S(2)}, u32[]{:S(2)}) async-start(bf16[64,2,16,256]{3,2,1,0:T(8,128)(2,1)} %bitcast.9), calls=%async_computation.2 | async-start | bytes 2097152 | tf_op jit(solution)/shard_map/all_to_all | solution.py:275
  39.8 1.1 fusion.10
  40.9 2.2 %collective-permute-start = (bf16[256,1024]{1,0:T(8,128)(2,1)}, bf16[256,1024]{1,0:T(8,128)(2,1)}, u32[]{:S(2)}, u32[]{:S(2)}) collective-permute-start(bf16[256,1024]{1,0:T(8,128)(2,1)} %bitcast.3), channel_id=1, source_target_pairs={{0,128},{128,256},{256,384},{384,0},{1,9},{9,17},{17,25},{25,1},{2... | collective-permute-start | bytes 1572872 | tf_op jit(solution)/shard_map/ppermute | solution.py:40
  43.1 3.6 %collective-permute-start.3 = (bf16[256,1024]{1,0:T(8,128)(2,1)}, bf16[256,1024]{1,0:T(8,128)(2,1)}, u32[]{:S(2)}, u32[]{:S(2)}) collective-permute-start(bf16[256,1024]{1,0:T(8,128)(2,1)} %bitcast.4), channel_id=1, source_target_pairs={{0,384},{128,0},{256,128},{384,256},{1,25},{9,1},{17,9},{25,17},{2... | collective-permute-start | bytes 1572872 | tf_op jit(solution)/shard_map/ppermute | solution.py:40
  46.7 3.4 %collective-permute-start.1 = (bf16[256,1024]{1,0:T(8,128)(2,1)}, bf16[256,1024]{1,0:T(8,128)(2,1)}, u32[]{:S(2)}, u32[]{:S(2)}) collective-permute-start(bf16[256,1024]{1,0:T(8,128)(2,1)} %bitcast.4), channel_id=1, source_target_pairs={{0,128},{128,256},{256,384},{384,0},{1,9},{9,17},{17,25},{25,1},{2... | collective-permute-start | bytes 1572872 | tf_op jit(solution)/shard_map/ppermute | solution.py:40
  50.2 2.4 %collective-permute-start.2 = (bf16[256,1024]{1,0:T(8,128)(2,1)}, bf16[256,1024]{1,0:T(8,128)(2,1)}, u32[]{:S(2)}, u32[]{:S(2)}) collective-permute-start(bf16[256,1024]{1,0:T(8,128)(2,1)} %bitcast.3), channel_id=1, source_target_pairs={{0,384},{128,0},{256,128},{384,256},{1,25},{9,1},{17,9},{25,17},{2... | collective-permute-start | bytes 1572872 | tf_op jit(solution)/shard_map/ppermute | solution.py:40
  52.6 3.4 %collective-permute-done.up_on = bf16[256,1024]{1,0:T(8,128)(2,1)} collective-permute-done((bf16[256,1024]{1,0:T(8,128)(2,1)}, bf16[256,1024]{1,0:T(8,128)(2,1)}, u32[]{:S(2)}, u32[]{:S(2)}) %collective-permute-start) | collective-permute-done | bytes 524320 | tf_op jit(solution)/shard_map/ppermute | solution.py:40
  55.9 3.9 %collective-permute-start.4 = (bf16[256,1024]{1,0:T(8,128)(2,1)}, bf16[256,1024]{1,0:T(8,128)(2,1)}, u32[]{:S(2)}, u32[]{:S(2)}) collective-permute-start(bf16[256,1024]{1,0:T(8,128)(2,1)} %collective-permute-done.up_on), channel_id=1, source_target_pairs={{0,128},{128,256},{256,384},{384,0},{1,9},{9,17},{17,25},{25,1},{2... | collective-permute-start | bytes 1572872 | tf_op jit(solution)/shard_map/ppermute | solution.py:40
  59.9 1.9 %collective-permute-start.5 = (bf16[256,1024]{1,0:T(8,128)(2,1)}, bf16[256,1024]{1,0:T(8,128)(2,1)}, u32[]{:S(2)}, u32[]{:S(2)}) collective-permute-start(bf16[256,1024]{1,0:T(8,128)(2,1)} %collective-permute-done.3.down_on), channel_id=1, source_target_pairs={{0,384},{128,0},{256,128},{384,256},{1,25},{9,1},{17,9},{25,17},{2... | collective-permute-start | bytes 1572872 | tf_op jit(solution)/shard_map/ppermute | solution.py:40
  61.9 0.2 select_reduce_fusion
  62.1 0.6 collective-permute-done.1.up_end
  62.7 1.9 %collective-permute-done.2.down_end = bf16[256,1024]{1,0:T(8,128)(2,1)} collective-permute-done((bf16[256,1024]{1,0:T(8,128)(2,1)}, bf16[256,1024]{1,0:T(8,128)(2,1)}, u32[]{:S(2)}, u32[]{:S(2)}) %collective-permute-start.2) | collective-permute-done | bytes 524320 | tf_op jit(solution)/shard_map/ppermute | solution.py:40
  64.6 3.7 %collective-permute-done.4.far_up = bf16[256,1024]{1,0:T(8,128)(2,1)} collective-permute-done((bf16[256,1024]{1,0:T(8,128)(2,1)}, bf16[256,1024]{1,0:T(8,128)(2,1)}, u32[]{:S(2)}, u32[]{:S(2)}) %collective-permute-start.4) | collective-permute-done | bytes 524320 | tf_op jit(solution)/shard_map/ppermute | solution.py:40
  68.3 4.2 %collective-permute-done.5.far_down = bf16[256,1024]{1,0:T(8,128)(2,1)} collective-permute-done((bf16[256,1024]{1,0:T(8,128)(2,1)}, bf16[256,1024]{1,0:T(8,128)(2,1)}, u32[]{:S(2)}, u32[]{:S(2)}) %collective-permute-start.5) | collective-permute-done | bytes 524320 | tf_op jit(solution)/shard_map/ppermute | solution.py:40
  72.5 3.4 %project.1 = (f32[1024,256]{1,0:T(8,128)S(1)}, f32[512,256]{1,0:T(8,128)S(1)}, f32[512,256]{1,0:T(8,128)S(1)}) custom-call(s32[64]{0:T(128)S(1)} %fusion.4.places, bf16[256,1024]{1,0:T(8,128)(2,1)S(1)} %bitcast.8, bf16[512,1024]{1,0:T(8,128)(2,1)S(1)} %bitcast.7, bf16[256,1024]{1,0:T(8,128)(2,1)} %collective-permute-done.up_on, ...), custom_call_target="tpu_custom_call" | custom-call | tf_op jit(solution)/shard_map/project/pallas_call | solution.py:116
  75.8 1.9 %collective-permute-start.6 = (f32[1024,256]{1,0:T(8,128)S(1)}, f32[1024,256]{1,0:T(8,128)S(1)}, u32[]{:S(2)}, u32[]{:S(2)}) collective-permute-start(f32[1024,256]{1,0:T(8,128)S(1)} %get-tuple-element.25), channel_id=1, source_target_pairs={{0,1},{1,0},{2,3},{3,2},{4,5},{5,4},{6,7},{7,6},{8,9},{9,8},{10,11... | collective-permute-start | bytes 3145736 | tf_op jit(solution)/shard_map/ppermute | solution.py:56
  77.8 2.6 %collective-permute-done.6 = f32[1024,256]{1,0:T(8,128)S(1)} collective-permute-done((f32[1024,256]{1,0:T(8,128)S(1)}, f32[1024,256]{1,0:T(8,128)S(1)}, u32[]{:S(2)}, u32[]{:S(2)}) %collective-permute-start.6) | collective-permute-done | bytes 1048608 | tf_op jit(solution)/shard_map/ppermute | solution.py:56
  80.5 9.2 %collective-permute-start.7 = (f16[512,256]{1,0:T(8,128)(2,1)S(1)}, f16[512,256]{1,0:T(8,128)(2,1)S(1)}, u32[]{:S(2)}, u32[]{:S(2)}) collective-permute-start(f16[512,256]{1,0:T(8,128)(2,1)S(1)} %fusion.1), channel_id=1, source_target_pairs={{0,2},{1,7},{2,0},{3,5},{4,6},{5,3},{6,4},{7,1},{8,10},{9,15},{10,... | collective-permute-start | bytes 786440 | tf_op jit(solution)/shard_map/ppermute | solution.py:52
  89.7 13.0 %collective-permute-done.7 = f16[512,256]{1,0:T(8,128)(2,1)S(1)} collective-permute-done((f16[512,256]{1,0:T(8,128)(2,1)S(1)}, f16[512,256]{1,0:T(8,128)(2,1)S(1)}, u32[]{:S(2)}, u32[]{:S(2)}) %collective-permute-start.7) | collective-permute-done | bytes 262176 | tf_op jit(solution)/shard_map/ppermute | solution.py:52
  102.8 0.1 fusion.3
  102.9 5.2 %collective-permute-start.8 = (f16[256,256]{1,0:T(8,128)(2,1)S(1)}, f16[256,256]{1,0:T(8,128)(2,1)S(1)}, u32[]{:S(2)}, u32[]{:S(2)}) collective-permute-start(f16[256,256]{1,0:T(8,128)(2,1)S(1)} %get-tuple-element.32), channel_id=1, source_target_pairs={{0,6},{1,3},{2,4},{3,1},{4,2},{5,7},{6,0},{7,5},{8,14},{9,11},{10,... | collective-permute-start | bytes 393224 | tf_op jit(solution)/shard_map/ppermute | solution.py:52
  108.1 0.1 reshape.95.table
  108.3 3.2 %past.1 = (f32[32,64,128]{2,1,0:T(8,128)S(1)}, bf16[32,64,128]{2,1,0:T(8,128)(2,1)S(1)}, bf16[32,128,128]{2,1,0:T(8,128)(2,1)S(1)}) custom-call(s32[192]{0:T(256)S(1)} %reshape.95.table, s32[32]{0:T(128)S(1)} %copy-done.3, bf16[8,32,1024]{2,1,0:T(8,128)(2,1)S(1)} %copy-done.2, bf16[192,16,256]{2,1,0:T(8,128)(2,1)S(1)} %copy-done, ...), custom_call_target="tpu_custom_call" | custom-call | flops 70000000 | bytes 8000000 | tf_op jit(solution)/shard_map/past/pallas_call | solution.py:177
  111.5 6.0 %collective-permute-done.8 = f16[256,256]{1,0:T(8,128)(2,1)S(1)} collective-permute-done((f16[256,256]{1,0:T(8,128)(2,1)S(1)}, f16[256,256]{1,0:T(8,128)(2,1)S(1)}, u32[]{:S(2)}, u32[]{:S(2)}) %collective-permute-start.8) | collective-permute-done | bytes 131104 | tf_op jit(solution)/shard_map/ppermute | solution.py:52
  117.5 2.8 %finish.1 = (bf16[8,32,256]{2,1,0:T(8,128)(2,1)}, bf16[8,32,1024]{2,1,0:T(8,128)(2,1)}) custom-call(f32[256,256]{1,0:T(8,128)S(1)} %get-tuple-element.36.refs_0_, f32[256,256]{1,0:T(8,128)S(1)} %get-tuple-element.33.refs_1_, f32[256,256]{1,0:T(8,128)S(1)} %get-tuple-element.37.refs_2_, f32[256,256]{1,0:T(8,128)S(1)} %convert_multiply_fusion.1.refs_3_, ...), custom_call_target="tpu_custom_call" | custom-call | flops 140000000 | bytes 4000000 | tf_op jit(solution)/shard_map/finish/pallas_call | solution.py:246
  (24 shorter events, 0.4 us)
Async XLA Ops:
  16.1 5.6 %copy-start.5 = (s32[1,64,2]{1,2,0:T(2,128)S(1)}, s32[1,64,2]{1,2,0:T(2,128)}, u32[]{:S(2)}) copy-start(s32[1,64,2]{1,2,0:T(2,128)} %param.15) | copy-start | bytes 1540
  16.1 5.8 %copy-start = (bf16[192,16,256]{2,1,0:T(8,128)(2,1)S(1)}, bf16[192,16,256]{2,1,0:T(8,128)(2,1)}, u32[]{:S(2)}) copy-start(bf16[192,16,256]{2,1,0:T(8,128)(2,1)} %pool.1) | copy-start | bytes 4718596
  17.2 15.4 %all-to-all-start.1 = ((bf16[4,128,1024]{2,1,0:T(8,128)(2,1)}), bf16[4,128,1024]{2,1,0:T(8,128)(2,1)S(1)}, u32[]{:S(2)}, u32[]{:S(2)}) async-start(bf16[4,128,1024]{2,1,0:T(8,128)(2,1)} %broadcast_in_dim.52), calls=%async_computation.1 | async-start | bytes 2097152 | tf_op jit(solution)/shard_map/all_to_all | solution.py:64
  32.5 39.9 %all-to-all-start.2 = ((bf16[64,2,16,256]{3,2,1,0:T(8,128)(2,1)}), bf16[64,2,16,256]{3,2,1,0:T(8,128)(2,1)}, u32[]{:S(2)}, u32[]{:S(2)}) async-start(bf16[64,2,16,256]{3,2,1,0:T(8,128)(2,1)} %bitcast.9), calls=%async_computation.2 | async-start | bytes 2097152 | tf_op jit(solution)/shard_map/all_to_all | solution.py:275
  39.8 22.1 %copy-start.6 = (s32[64]{0:T(128)S(1)}, s32[64]{0:T(128)}, u32[]{:S(2)}) copy-start(s32[64]{0:T(128)} %param.10) | copy-start | bytes 772
  39.8 32.7 %copy-start.1 = (bf16[8,32,1024]{2,1,0:T(8,128)(2,1)S(1)}, bf16[8,32,1024]{2,1,0:T(8,128)(2,1)}, u32[]{:S(2)}) copy-start(bf16[8,32,1024]{2,1,0:T(8,128)(2,1)} %param.8) | copy-start | bytes 1572868
  40.9 15.1 %collective-permute-start = (bf16[256,1024]{1,0:T(8,128)(2,1)}, bf16[256,1024]{1,0:T(8,128)(2,1)}, u32[]{:S(2)}, u32[]{:S(2)}) collective-permute-start(bf16[256,1024]{1,0:T(8,128)(2,1)} %bitcast.3), channel_id=1, source_target_pairs={{0,128},{128,256},{256,384},{384,0},{1,9},{9,17},{17,25},{25,1},{2... | collective-permute-start | bytes 1572872 | tf_op jit(solution)/shard_map/ppermute | solution.py:40
  43.1 16.8 %collective-permute-start.3 = (bf16[256,1024]{1,0:T(8,128)(2,1)}, bf16[256,1024]{1,0:T(8,128)(2,1)}, u32[]{:S(2)}, u32[]{:S(2)}) collective-permute-start(bf16[256,1024]{1,0:T(8,128)(2,1)} %bitcast.4), channel_id=1, source_target_pairs={{0,384},{128,0},{256,128},{384,256},{1,25},{9,1},{17,9},{25,17},{2... | collective-permute-start | bytes 1572872 | tf_op jit(solution)/shard_map/ppermute | solution.py:40
  46.7 15.9 %collective-permute-start.1 = (bf16[256,1024]{1,0:T(8,128)(2,1)}, bf16[256,1024]{1,0:T(8,128)(2,1)}, u32[]{:S(2)}, u32[]{:S(2)}) collective-permute-start(bf16[256,1024]{1,0:T(8,128)(2,1)} %bitcast.4), channel_id=1, source_target_pairs={{0,128},{128,256},{256,384},{384,0},{1,9},{9,17},{17,25},{25,1},{2... | collective-permute-start | bytes 1572872 | tf_op jit(solution)/shard_map/ppermute | solution.py:40
  50.2 14.4 %collective-permute-start.2 = (bf16[256,1024]{1,0:T(8,128)(2,1)}, bf16[256,1024]{1,0:T(8,128)(2,1)}, u32[]{:S(2)}, u32[]{:S(2)}) collective-permute-start(bf16[256,1024]{1,0:T(8,128)(2,1)} %bitcast.3), channel_id=1, source_target_pairs={{0,384},{128,0},{256,128},{384,256},{1,25},{9,1},{17,9},{25,17},{2... | collective-permute-start | bytes 1572872 | tf_op jit(solution)/shard_map/ppermute | solution.py:40
  55.9 12.3 %collective-permute-start.4 = (bf16[256,1024]{1,0:T(8,128)(2,1)}, bf16[256,1024]{1,0:T(8,128)(2,1)}, u32[]{:S(2)}, u32[]{:S(2)}) collective-permute-start(bf16[256,1024]{1,0:T(8,128)(2,1)} %collective-permute-done.up_on), channel_id=1, source_target_pairs={{0,128},{128,256},{256,384},{384,0},{1,9},{9,17},{17,25},{25,1},{2... | collective-permute-start | bytes 1572872 | tf_op jit(solution)/shard_map/ppermute | solution.py:40
  59.9 12.6 %collective-permute-start.5 = (bf16[256,1024]{1,0:T(8,128)(2,1)}, bf16[256,1024]{1,0:T(8,128)(2,1)}, u32[]{:S(2)}, u32[]{:S(2)}) collective-permute-start(bf16[256,1024]{1,0:T(8,128)(2,1)} %collective-permute-done.3.down_on), channel_id=1, source_target_pairs={{0,384},{128,0},{256,128},{384,256},{1,25},{9,1},{17,9},{25,17},{2... | collective-permute-start | bytes 1572872 | tf_op jit(solution)/shard_map/ppermute | solution.py:40
  75.8 4.6 %collective-permute-start.6 = (f32[1024,256]{1,0:T(8,128)S(1)}, f32[1024,256]{1,0:T(8,128)S(1)}, u32[]{:S(2)}, u32[]{:S(2)}) collective-permute-start(f32[1024,256]{1,0:T(8,128)S(1)} %get-tuple-element.25), channel_id=1, source_target_pairs={{0,1},{1,0},{2,3},{3,2},{4,5},{5,4},{6,7},{7,6},{8,9},{9,8},{10,11... | collective-permute-start | bytes 3145736 | tf_op jit(solution)/shard_map/ppermute | solution.py:56
  80.5 27.6 %copy-start.4 = (s32[32,6]{0,1:T(8,128)S(1)}, s32[32,6]{0,1:T(8,128)}, u32[]{:S(2)}) copy-start(s32[32,6]{0,1:T(8,128)} %param.13) | copy-start | bytes 2308
  80.5 27.8 %copy-start.2 = (bf16[8,32,1024]{2,1,0:T(8,128)(2,1)S(1)}, bf16[8,32,1024]{2,1,0:T(8,128)(2,1)}, u32[]{:S(2)}) copy-start(bf16[8,32,1024]{2,1,0:T(8,128)(2,1)} %queries) | copy-start | bytes 1572868
  80.5 27.8 %copy-start.3 = (s32[32]{0:T(128)S(1)}, s32[32]{0:T(128)}, u32[]{:S(2)}) copy-start(s32[32]{0:T(128)} %lengths.1) | copy-start | bytes 388
  80.5 22.2 %collective-permute-start.7 = (f16[512,256]{1,0:T(8,128)(2,1)S(1)}, f16[512,256]{1,0:T(8,128)(2,1)S(1)}, u32[]{:S(2)}, u32[]{:S(2)}) collective-permute-start(f16[512,256]{1,0:T(8,128)(2,1)S(1)} %fusion.1), channel_id=1, source_target_pairs={{0,2},{1,7},{2,0},{3,5},{4,6},{5,3},{6,4},{7,1},{8,10},{9,15},{10,... | collective-permute-start | bytes 786440 | tf_op jit(solution)/shard_map/ppermute | solution.py:52
  102.9 14.6 %collective-permute-start.8 = (f16[256,256]{1,0:T(8,128)(2,1)S(1)}, f16[256,256]{1,0:T(8,128)(2,1)S(1)}, u32[]{:S(2)}, u32[]{:S(2)}) collective-permute-start(f16[256,256]{1,0:T(8,128)(2,1)S(1)} %get-tuple-element.32), channel_id=1, source_target_pairs={{0,6},{1,3},{2,4},{3,1},{4,2},{5,7},{6,0},{7,5},{8,14},{9,11},{10,... | collective-permute-start | bytes 393224 | tf_op jit(solution)/shard_map/ppermute | solution.py:52

commit v3 on v2

--- a/solution.py
+++ b/solution.py
@@ -48,15 +48,18 @@
     pairs = [
         (zh * CORES + c, partner(zh, c, step) * CORES + c) for zh in RING for c in range(CORES)
     ]
-    sent = (value * SCALE).astype(jnp.float16)
-    return lax.ppermute(sent, TENSOR, pairs).astype(jnp.float32) * (1.0 / SCALE)
+    return lax.ppermute((value * SCALE).astype(jnp.float16), TENSOR, pairs)
+
+
+def unscaled(value):
+    return value.astype(jnp.float32) * (1.0 / SCALE)
 
 
 def core_swap(value):
     return lax.ppermute(value, "c", [(0, 1), (1, 0)])
 
 
-def gather_weight(held):
+def gather_weight(held, outgoing):
     first = lax.all_to_all(
         jnp.broadcast_to(held[None], (SIDE,) + held.shape), "zl", 0, 0, tiled=True
     )
@@ -65,12 +68,14 @@
         jnp.broadcast_to(block, (SIDE,) + block.shape[1:]),
         AXES, 0, 0, axis_index_groups=lines(1),
     )
+    second, outgoing = lax.optimization_barrier((second, outgoing))
     own = second.reshape(-1, held.shape[1])
     half = own.shape[0] // 2
-    up_on, down_on = shift(own[:half], 2, 1), shift(own[half:], 2, -1)
-    up_end, down_end = shift(own[half:], 2, 1), shift(own[:half], 2, -1)
+    low, high = own[:half], own[half:]
+    up_on, down_on = shift(low, 2, 1), shift(high, 2, -1)
+    up_end, down_end = shift(high, 2, 1), shift(low, 2, -1)
     far_up, far_down = shift(up_on, 2, 1), shift(down_on, 2, -1)
-    return own, up_on, up_end, down_end, down_on, far_up, far_down
+    return outgoing, (low, high, up_on, up_end, down_end, down_on, far_up, far_down)
 
 
 def block_places(owner, c, q):
@@ -89,17 +94,19 @@
     return (order * 8 + block % 8).astype(jnp.int32)
 
 
-def project_kernel(places, rows, own, up_on, up_end, down_end, down_on, far_up, far_down, away, near, late, total, sems):
+def project_kernel(
+    places, rows, low, high, up_on, up_end, down_end, down_on, far_up, far_down, away, near, late,
+    total, sems,
+):
     base = 0
-    for piece in (own, up_on, up_end, down_end, down_on, far_up, far_down):
-        count = piece.shape[0] // 32
+    for piece in (low, high, up_on, up_end, down_end, down_on, far_up, far_down):
         product = lax.dot_general(
             piece[...], rows[...], (((1,), (1,)), ((), ())), preferred_element_type=jnp.float32
         )
-        for b in range(count):
+        for b in range(piece.shape[0] // 32):
             at = pl.multiple_of(places[base + b] * 32, 32)
             total[pl.ds(at, 32), :] = product[b * 32:(b + 1) * 32]
-        base += count
+        base += piece.shape[0] // 32
     copies, base = [], 0
     for i, out in enumerate((away, near, late)):
         copies.append(pltpu.make_async_copy(total.at[pl.ds(base, out.shape[0])], out, sems.at[i]))
@@ -118,22 +125,27 @@
         out_shape=[
             jax.ShapeDtypeStruct((size, count), jnp.float32) for size in (1024, 512, 512)
         ],
-        in_specs=[pl.BlockSpec(memory_space=pltpu.SMEM)] + [vmem] * 8,
+        in_specs=[pl.BlockSpec(memory_space=pltpu.SMEM)] + [vmem] * 9,
         out_specs=[pl.BlockSpec(memory_space=pl.ANY)] * 3,
         scratch_shapes=[
             pltpu.VMEM((2048, count), jnp.float32),
             pltpu.SemaphoreType.DMA((3,)),
         ],
-        compiler_params=pltpu.CompilerParams(vmem_limit_bytes=24 * 2**20),
+        compiler_params=pltpu.CompilerParams(vmem_limit_bytes=16 * 2**20),
+        cost_estimate=pl.CostEstimate(flops=40_000_000_000, bytes_accessed=6000000, transcendentals=0),
         name="project",
     )(places, rows, *pieces)
 
 
-def reduce_columns(away, near, late):
+def reduce_columns(arrived, away, near, late):
     got = core_swap(away)
-    got_near = z_exchange(near + got[:512], 1)
-    got_late = z_exchange(late[:256] + got[512:768] + got_near[:256], 2)
-    return got, (late[256:], got[768:], got_near[256:], got_late)
+    got_far = z_exchange(near[:256] + got[:256], 1)
+    got_near = z_exchange(near[256:] + got[256:512], 1)
+    second, here = lax.optimization_barrier((late[:256] + got[512:768], late[256:] + got[768:]))
+    got_far, arrived = lax.optimization_barrier((got_far, arrived))
+    got_late = z_exchange(second + unscaled(got_far), 2)
+    here, got_late = lax.optimization_barrier((here + unscaled(got_near), got_late))
+    return got, arrived, here + unscaled(got_late)
 
 
 def past_kernel(table, lengths, queries, pool, arrived, scores, folded, values, cells, wide):
@@ -142,7 +154,7 @@
 
     def fetch(s, _):
         for e in range(SPAN // 16):
-            entry = table[s * (SPAN // 16) + e]
+            entry = table[s, e]
             mine = pool[jnp.minimum(entry, pages - 1)]
             sent = arrived[jnp.maximum(entry - pages, 0)]
             cells[s, e * 16:(e + 1) * 16] = jnp.where(entry < pages, mine, sent)
@@ -187,20 +199,17 @@
             pltpu.VMEM((seqs, WIDE, 2 * HD), jnp.bfloat16),
             pltpu.VMEM((8, steps * seqs, HD), jnp.float32),
         ],
-        compiler_params=pltpu.CompilerParams(vmem_limit_bytes=24 * 2**20),
+        compiler_params=pltpu.CompilerParams(vmem_limit_bytes=16 * 2**20),
         cost_estimate=pl.CostEstimate(flops=70_000_000, bytes_accessed=8_000_000, transcendentals=0),
         name="past",
     )(table, lengths, queries, pool, arrived)
 
 
 def finish_kernel(*refs):
-    *parts, scores, folded, values, new_kv, attended, wide, keys, mixed, weights, totals, own = refs
+    total, scores, folded, values, new_kv, attended, wide, keys, mixed, weights, totals, own = refs
     seqs = scores.shape[0]
     steps = new_kv.shape[0]
-    fresh = parts[0][...].astype(jnp.float32)
-    for part in parts[1:]:
-        fresh = fresh + part[...].astype(jnp.float32)
-    fresh = fresh.T.astype(jnp.bfloat16)
+    fresh = total[...].T.astype(jnp.bfloat16)
     for t in range(steps):
         new_kv[t] = fresh[t * seqs:(t + 1) * seqs]
     wide[0] = fresh[:, :HD].astype(jnp.float32)
@@ -240,7 +249,7 @@
             ].astype(jnp.bfloat16)
 
 
-def finish(parts, scores, folded, values, steps):
+def finish(total, scores, folded, values, steps):
     seqs = scores.shape[0]
     vmem = pl.BlockSpec(memory_space=pltpu.VMEM)
     return pl.pallas_call(
@@ -249,7 +258,7 @@
             jax.ShapeDtypeStruct((steps, seqs, 2 * HD), jnp.bfloat16),
             jax.ShapeDtypeStruct((steps, seqs, 8 * HD), jnp.bfloat16),
         ],
-        in_specs=[vmem] * (len(parts) + 3),
+        in_specs=[vmem] * 4,
         out_specs=[vmem, vmem],
         scratch_shapes=[
             pltpu.VMEM((2, steps * seqs, HD), jnp.float32),
@@ -259,10 +268,10 @@
             pltpu.VMEM((seqs, 64, HD), jnp.float32),
             pltpu.VMEM((seqs, 16, HD), jnp.bfloat16),
         ],
-        compiler_params=pltpu.CompilerParams(vmem_limit_bytes=24 * 2**20),
+        compiler_params=pltpu.CompilerParams(vmem_limit_bytes=16 * 2**20),
         cost_estimate=pl.CostEstimate(flops=140_000_000, bytes_accessed=4_000_000, transcendentals=262144),
         name="finish",
-    )(*parts, scores, folded, values)
+    )(total, scores, folded, values)
 
 
 def on_device(hidden, kv_weight, owner, queries, pool, page_table, lengths, send_pages):
@@ -272,16 +281,15 @@
     outgoing = jnp.take(pool, send_pages.reshape(-1), axis=0, mode="clip").reshape(
         64, -1, page_size, kv_width
     )
+    outgoing, pieces = gather_weight(kv_weight, outgoing)
     arrived = lax.all_to_all(outgoing, REPLICA, split_axis=0, concat_axis=0, tiled=True)
-
-    pieces, arrived = lax.optimization_barrier((gather_weight(kv_weight), arrived))
     places = block_places(owner, c, q)
-    swapped, parts = reduce_columns(*project(places, hidden.reshape(-1, feature_part), pieces))
+    swapped, arrived, total = reduce_columns(arrived, *project(places, hidden.reshape(-1, feature_part), pieces))
     queries, _ = lax.optimization_barrier((queries, swapped))
     scores, folded, values = past(
-        page_table.reshape(-1), lengths, queries, pool, arrived.reshape(-1, page_size, kv_width)
-    )
-    return tuple(finish(parts, scores, folded, values, steps_count))
+        page_table, lengths, queries, pool, arrived.reshape(-1, page_size, kv_width)
+    )
+    return tuple(finish(total, scores, folded, values, steps_count))
 
 
 def solution(mesh):

time: 121 us -> 116 us (0.959)
  waiting for transfers between devices: 44.4 us -> 25 us
  starting transfers between devices: 45.5 us -> 56.3 us
  other arithmetic: 0.48 us -> 3.1 us
    ppermute x2 -> x3, waiting for transfers between devices: 18.9 us -> 3.42 us  [z_exchange(): return lax.ppermute((value * SCALE).astype(jnp.float16), TENSOR, pairs)]
    ppermute x2 -> x3, starting transfers between devices: 14.4 us -> 23.9 us  [z_exchange(): return lax.ppermute((value * SCALE).astype(jnp.float16), TENSOR, pairs)]
    ppermute x6, waiting for transfers between devices: 13.8 us -> 9.93 us  [shift(): return lax.ppermute(value, AXES, pairs)]
    convert_element_type x2, other arithmetic: 0.19 us -> 1.9 us  [z_exchange(): return lax.ppermute((value * SCALE).astype(jnp.float16), TENSOR, pairs)]
  transfers between devices with their start and end apart: 11 -> 12, of which waited for: 9 -> 5; matrix products, arithmetic and copies ran while one was open for 3% -> 4% of each run, Pallas kernels for 3% -> 5%
where the time goes in v3:
time: 116 us; the launch traced here: 115 us
  starting transfers between devices  56.3 us (49%)
  waiting for transfers between devices  25 us (22%)
  blocking collectives  14.6 us (13%)
  Pallas kernels  9.03 us (8%)
  local copies, waits for them, and re-layouts  5.88 us (5%)
  other arithmetic  3.1 us (3%)
    ppermute x3, starting transfers between devices, z_exchange(): return lax.ppermute((value * SCALE).astype(jnp.float16), TENSOR, pairs)  23.9 us
    ppermute x6, starting transfers between devices, shift(): return lax.ppermute(value, AXES, pairs)  18.4 us
    all_to_all x1, blocking collectives, gather_weight(): lax.all_to_all(jnp.broadcast_to(held[None], (SIDE,) + held.shape), 'zl',...  14.6 us
    ppermute x6, waiting for transfers between devices, shift(): return lax.ppermute(value, AXES, pairs)  9.93 us
    all_to_all x1, waiting for transfers between devices, gather_weight(): lax.all_to_all(jnp.broadcast_to(block, (SIDE,) + block.shape[1:]), AXES,...  8.98 us
    all_to_all x1, starting transfers between devices, on_device(): lax.all_to_all(outgoing, REPLICA, split_axis=0, concat_axis=0, tiled=True)  7.64 us
    all_to_all x1, starting transfers between devices, gather_weight(): lax.all_to_all(jnp.broadcast_to(block, (SIDE,) + block.shape[1:]), AXES,...  4.46 us
    pallas_call x1, Pallas kernels, project(): pl.pallas_call(project_kernel, out_shape=[jax.ShapeDtypeStruct((size, cou...  3.49 us
  transfers between devices with their start and end apart: 12, of which 5 were waited for; matrix products, arithmetic and copies ran while one was open for 4% of the time, Pallas kernels for 5%

profile of v3, /device:TPU:6, one launch (start us, length us, event | category | flops | bytes accessed | tf_op | source)
XLA Modules:
  0.0 114.8 jit_solution(5161167425104450497)
XLA Ops:
  0.6 0.9 broadcast_in_dim.50
  1.5 14.6 %all_to_all.15 = bf16[4,32,1024]{2,1,0:T(8,128)(2,1)S(1)} all-to-all(bf16[4,32,1024]{2,1,0:T(8,128)(2,1)S(1)} %broadcast_in_dim.50), channel_id=1, replica_groups=mesh['x'=4,'zl'=4,'y'=4,'zh'=4,'c'=2] {'zl'}, dimensions={0} | all-to-all | bytes 524288 | tf_op jit(solution)/shard_map/all_to_all | solution.py:63
  16.1 1.1 broadcast_in_dim.52
  17.2 4.5 %all-to-all-start.1 = ((bf16[4,128,1024]{2,1,0:T(8,128)(2,1)}), bf16[4,128,1024]{2,1,0:T(8,128)(2,1)S(1)}, u32[]{:S(2)}, u32[]{:S(2)}) async-start(bf16[4,128,1024]{2,1,0:T(8,128)(2,1)} %broadcast_in_dim.52), calls=%async_computation.1 | async-start | bytes 2097152 | tf_op jit(solution)/shard_map/all_to_all | solution.py:67
  21.6 0.1 copy.14
  21.7 0.1 reshape.92
  21.9 1.6 %gather_fusion = bf16[128,16,256]{2,1,0:T(8,128)(2,1)} fusion(bf16[192,16,256]{2,1,0:T(8,128)(2,1)S(1)} %copy-done, s32[1024]{0:T(1024)S(1)} %pad_clamp_fusion), kind=kCustom, calls=%fused_computation | custom fusion | bytes 2097664 | tf_op jit(solution)/shard_map/jit(_take)/gather | solution.py:281
  23.5 9.0 %all-to-all-done.1 = bf16[4,128,1024]{2,1,0:T(8,128)(2,1)S(1)} async-done(((bf16[4,128,1024]{2,1,0:T(8,128)(2,1)}), bf16[4,128,1024]{2,1,0:T(8,128)(2,1)S(1)}, u32[]{:S(2)}, u32[]{:S(2)}) %all-to-all-start.1) | async-done | bytes 1048608 | tf_op jit(solution)/shard_map/all_to_all | solution.py:67
  32.5 0.9 fusion.10
  33.4 2.4 %collective-permute-start = (bf16[256,1024]{1,0:T(8,128)(2,1)}, bf16[256,1024]{1,0:T(8,128)(2,1)}, u32[]{:S(2)}, u32[]{:S(2)}) collective-permute-start(bf16[256,1024]{1,0:T(8,128)(2,1)} %bitcast.3.low), channel_id=1, source_target_pairs={{0,128},{128,256},{256,384},{384,0},{1,9},{9,17},{17,25},{25,1},{2... | collective-permute-start | bytes 1572872 | tf_op jit(solution)/shard_map/ppermute | solution.py:40
  35.8 3.5 %collective-permute-start.3 = (bf16[256,1024]{1,0:T(8,128)(2,1)S(1)}, bf16[256,1024]{1,0:T(8,128)(2,1)}, u32[]{:S(2)}, u32[]{:S(2)}) collective-permute-start(bf16[256,1024]{1,0:T(8,128)(2,1)S(1)} %bitcast.7), channel_id=1, source_target_pairs={{0,384},{128,0},{256,128},{384,256},{1,25},{9,1},{17,9},{25,17},{2... | collective-permute-start | bytes 1572872 | tf_op jit(solution)/shard_map/ppermute | solution.py:40
  39.3 3.6 %collective-permute-start.1 = (bf16[256,1024]{1,0:T(8,128)(2,1)S(1)}, bf16[256,1024]{1,0:T(8,128)(2,1)}, u32[]{:S(2)}, u32[]{:S(2)}) collective-permute-start(bf16[256,1024]{1,0:T(8,128)(2,1)S(1)} %bitcast.8), channel_id=1, source_target_pairs={{0,128},{128,256},{256,384},{384,0},{1,9},{9,17},{17,25},{25,1},{2... | collective-permute-start | bytes 1572872 | tf_op jit(solution)/shard_map/ppermute | solution.py:40
  42.9 2.2 %collective-permute-start.2 = (bf16[256,1024]{1,0:T(8,128)(2,1)}, bf16[256,1024]{1,0:T(8,128)(2,1)}, u32[]{:S(2)}, u32[]{:S(2)}) collective-permute-start(bf16[256,1024]{1,0:T(8,128)(2,1)} %bitcast.3.low), channel_id=1, source_target_pairs={{0,384},{128,0},{256,128},{384,256},{1,25},{9,1},{17,9},{25,17},{2... | collective-permute-start | bytes 1572872 | tf_op jit(solution)/shard_map/ppermute | solution.py:40
  45.1 4.8 %collective-permute-start.4 = (bf16[256,1024]{1,0:T(8,128)(2,1)}, bf16[256,1024]{1,0:T(8,128)(2,1)}, u32[]{:S(2)}, u32[]{:S(2)}) collective-permute-start(bf16[256,1024]{1,0:T(8,128)(2,1)} %collective-permute-done.up_on), channel_id=1, source_target_pairs={{0,128},{128,256},{256,384},{384,0},{1,9},{9,17},{17,25},{25,1},{2... | collective-permute-start | bytes 1572872 | tf_op jit(solution)/shard_map/ppermute | solution.py:40
  50.0 1.9 %collective-permute-start.5 = (bf16[256,1024]{1,0:T(8,128)(2,1)}, bf16[256,1024]{1,0:T(8,128)(2,1)}, u32[]{:S(2)}, u32[]{:S(2)}) collective-permute-start(bf16[256,1024]{1,0:T(8,128)(2,1)} %collective-permute-done.3.down_on), channel_id=1, source_target_pairs={{0,384},{128,0},{256,128},{384,256},{1,25},{9,1},{17,9},{25,17},{2... | collective-permute-start | bytes 1572872 | tf_op jit(solution)/shard_map/ppermute | solution.py:40
  51.9 0.2 select_reduce_fusion
  52.2 7.6 %all-to-all-start.2 = ((bf16[64,2,16,256]{3,2,1,0:T(8,128)(2,1)}), bf16[64,2,16,256]{3,2,1,0:T(8,128)(2,1)S(1)}, u32[]{:S(2)}, u32[]{:S(2)}) async-start(bf16[64,2,16,256]{3,2,1,0:T(8,128)(2,1)} %bitcast.11), calls=%async_computation.2 | async-start | bytes 2097152 | tf_op jit(solution)/shard_map/all_to_all | solution.py:285
  59.8 9.9 %collective-permute-done.5.far_down = bf16[256,1024]{1,0:T(8,128)(2,1)} collective-permute-done((bf16[256,1024]{1,0:T(8,128)(2,1)}, bf16[256,1024]{1,0:T(8,128)(2,1)}, u32[]{:S(2)}, u32[]{:S(2)}) %collective-permute-start.5) | collective-permute-done | bytes 524320 | tf_op jit(solution)/shard_map/ppermute | solution.py:40
  69.8 1.0 copy-done.3
  70.8 3.5 %project.1 = (f32[1024,256]{1,0:T(8,128)S(1)}, f32[512,256]{1,0:T(8,128)S(1)}, f32[512,256]{1,0:T(8,128)S(1)}) custom-call(s32[64]{0:T(128)S(1)} %fusion.4.places, bf16[256,1024]{1,0:T(8,128)(2,1)S(1)} %bitcast.10, bf16[256,1024]{1,0:T(8,128)(2,1)} %bitcast.3.low, bf16[256,1024]{1,0:T(8,128)(2,1)S(1)} %bitcast.9, ...), custom_call_target="tpu_custom_call" | custom-call | flops 40000000000 | bytes 6000000 | tf_op jit(solution)/shard_map/project/pallas_call | solution.py:123
  74.3 1.9 %collective-permute-start.6 = (f32[1024,256]{1,0:T(8,128)S(1)}, f32[1024,256]{1,0:T(8,128)S(1)}, u32[]{:S(2)}, u32[]{:S(2)}) collective-permute-start(f32[1024,256]{1,0:T(8,128)S(1)} %get-tuple-element.19), channel_id=1, source_target_pairs={{0,1},{1,0},{2,3},{3,2},{4,5},{5,4},{6,7},{7,6},{8,9},{9,8},{10,11... | collective-permute-start | bytes 3145736 | tf_op jit(solution)/shard_map/ppermute | solution.py:59
  76.2 2.6 %collective-permute-done.6 = f32[1024,256]{1,0:T(8,128)S(1)} collective-permute-done((f32[1024,256]{1,0:T(8,128)S(1)}, f32[1024,256]{1,0:T(8,128)S(1)}, u32[]{:S(2)}, u32[]{:S(2)}) %collective-permute-start.6) | collective-permute-done | bytes 1048608 | tf_op jit(solution)/shard_map/ppermute | solution.py:59
  78.9 0.9 fusion.1
  79.7 9.1 %collective-permute-start.8 = (f16[256,256]{1,0:T(8,128)(2,1)}, f16[256,256]{1,0:T(8,128)(2,1)}, u32[]{:S(2)}, u32[]{:S(2)}) collective-permute-start(f16[256,256]{1,0:T(8,128)(2,1)} %get-tuple-element.32), channel_id=1, source_target_pairs={{0,2},{1,7},{2,0},{3,5},{4,6},{5,3},{6,4},{7,1},{8,10},{9,15},{10,... | collective-permute-start | bytes 393224 | tf_op jit(solution)/shard_map/ppermute | solution.py:51
  88.9 1.9 %collective-permute-start.7 = (f16[256,256]{1,0:T(8,128)(2,1)}, f16[256,256]{1,0:T(8,128)(2,1)}, u32[]{:S(2)}, u32[]{:S(2)}) collective-permute-start(f16[256,256]{1,0:T(8,128)(2,1)} %get-tuple-element.33), channel_id=1, source_target_pairs={{0,2},{1,7},{2,0},{3,5},{4,6},{5,3},{6,4},{7,1},{8,10},{9,15},{10,... | collective-permute-start | bytes 393224 | tf_op jit(solution)/shard_map/ppermute | solution.py:51
  90.9 1.4 %collective-permute-done.8 = f16[256,256]{1,0:T(8,128)(2,1)} collective-permute-done((f16[256,256]{1,0:T(8,128)(2,1)}, f16[256,256]{1,0:T(8,128)(2,1)}, u32[]{:S(2)}, u32[]{:S(2)}) %collective-permute-start.8) | collective-permute-done | bytes 131104 | tf_op jit(solution)/shard_map/ppermute | solution.py:51
  92.2 1.0 multiply_convert_fusion
  93.3 12.9 %collective-permute-start.9 = (f16[256,256]{1,0:T(8,128)(2,1)S(1)}, f16[256,256]{1,0:T(8,128)(2,1)S(1)}, u32[]{:S(2)}, u32[]{:S(2)}) collective-permute-start(f16[256,256]{1,0:T(8,128)(2,1)S(1)} %multiply_convert_fusion), channel_id=1, source_target_pairs={{0,6},{1,3},{2,4},{3,1},{4,2},{5,7},{6,0},{7,5},{8,14},{9,11},{10,... | collective-permute-start | bytes 393224 | tf_op jit(solution)/shard_map/ppermute | solution.py:51
  106.2 0.9 multiply_add_fusion.1
  107.1 2.8 %past.1 = (f32[32,64,128]{2,1,0:T(8,128)S(1)}, bf16[32,64,128]{2,1,0:T(8,128)(2,1)S(1)}, bf16[32,128,128]{2,1,0:T(8,128)(2,1)S(1)}) custom-call(s32[32,6]{1,0:T(8,128)S(1)} %copy.15.table, s32[32]{0:T(128)S(1)} %copy-done.2, bf16[8,32,1024]{2,1,0:T(8,128)(2,1)S(1)} %copy-done.1, bf16[192,16,256]{2,1,0:T(8,128)(2,1)S(1)} %copy-done, ...), custom_call_target="tpu_custom_call" | custom-call | flops 70000000 | bytes 8000000 | tf_op jit(solution)/shard_map/past/pallas_call | solution.py:189
  109.9 2.1 %collective-permute-done.9 = f16[256,256]{1,0:T(8,128)(2,1)S(1)} collective-permute-done((f16[256,256]{1,0:T(8,128)(2,1)S(1)}, f16[256,256]{1,0:T(8,128)(2,1)S(1)}, u32[]{:S(2)}, u32[]{:S(2)}) %collective-permute-start.9) | collective-permute-done | bytes 131104 | tf_op jit(solution)/shard_map/ppermute | solution.py:51
  112.0 2.8 %finish.1 = (bf16[8,32,256]{2,1,0:T(8,128)(2,1)}, bf16[8,32,1024]{2,1,0:T(8,128)(2,1)}) custom-call(f32[256,256]{1,0:T(8,128)S(1)} %multiply_add_fusion.refs_0_, f32[32,64,128]{2,1,0:T(8,128)S(1)} %get-tuple-element.29.refs_1_, bf16[32,64,128]{2,1,0:T(8,128)(2,1)S(1)} %get-tuple-element.30.refs_2_, bf16[32,128,128]{2,1,0:T(8,128)(2,1)S(1)} %get-tuple-element.31.refs_3_), custom_call_target="tpu_custom_call" | custom-call | flops 140000000 | bytes 4000000 | tf_op jit(solution)/shard_map/finish/pallas_call | solution.py:255
  (25 shorter events, 0.2 us)
Async XLA Ops:
  16.1 5.6 %copy-start.5 = (s32[1,64,2]{1,2,0:T(2,128)S(1)}, s32[1,64,2]{1,2,0:T(2,128)}, u32[]{:S(2)}) copy-start(s32[1,64,2]{1,2,0:T(2,128)} %param.15) | copy-start | bytes 1540
  16.1 5.8 %copy-start = (bf16[192,16,256]{2,1,0:T(8,128)(2,1)S(1)}, bf16[192,16,256]{2,1,0:T(8,128)(2,1)}, u32[]{:S(2)}) copy-start(bf16[192,16,256]{2,1,0:T(8,128)(2,1)} %pool.1) | copy-start | bytes 4718596
  17.2 15.4 %all-to-all-start.1 = ((bf16[4,128,1024]{2,1,0:T(8,128)(2,1)}), bf16[4,128,1024]{2,1,0:T(8,128)(2,1)S(1)}, u32[]{:S(2)}, u32[]{:S(2)}) async-start(bf16[4,128,1024]{2,1,0:T(8,128)(2,1)} %broadcast_in_dim.52), calls=%async_computation.1 | async-start | bytes 2097152 | tf_op jit(solution)/shard_map/all_to_all | solution.py:67
  23.5 28.4 %copy-start.6 = (s32[64]{0:T(128)S(1)}, s32[64]{0:T(128)}, u32[]{:S(2)}) copy-start(s32[64]{0:T(128)} %param.10) | copy-start | bytes 772
  33.4 11.7 %collective-permute-start = (bf16[256,1024]{1,0:T(8,128)(2,1)}, bf16[256,1024]{1,0:T(8,128)(2,1)}, u32[]{:S(2)}, u32[]{:S(2)}) collective-permute-start(bf16[256,1024]{1,0:T(8,128)(2,1)} %bitcast.3.low), channel_id=1, source_target_pairs={{0,128},{128,256},{256,384},{384,0},{1,9},{9,17},{17,25},{25,1},{2... | collective-permute-start | bytes 1572872 | tf_op jit(solution)/shard_map/ppermute | solution.py:40
  35.8 14.2 %collective-permute-start.3 = (bf16[256,1024]{1,0:T(8,128)(2,1)S(1)}, bf16[256,1024]{1,0:T(8,128)(2,1)}, u32[]{:S(2)}, u32[]{:S(2)}) collective-permute-start(bf16[256,1024]{1,0:T(8,128)(2,1)S(1)} %bitcast.7), channel_id=1, source_target_pairs={{0,384},{128,0},{256,128},{384,256},{1,25},{9,1},{17,9},{25,17},{2... | collective-permute-start | bytes 1572872 | tf_op jit(solution)/shard_map/ppermute | solution.py:40
  39.3 20.5 %collective-permute-start.1 = (bf16[256,1024]{1,0:T(8,128)(2,1)S(1)}, bf16[256,1024]{1,0:T(8,128)(2,1)}, u32[]{:S(2)}, u32[]{:S(2)}) collective-permute-start(bf16[256,1024]{1,0:T(8,128)(2,1)S(1)} %bitcast.8), channel_id=1, source_target_pairs={{0,128},{128,256},{256,384},{384,0},{1,9},{9,17},{17,25},{25,1},{2... | collective-permute-start | bytes 1572872 | tf_op jit(solution)/shard_map/ppermute | solution.py:40
  42.9 16.9 %collective-permute-start.2 = (bf16[256,1024]{1,0:T(8,128)(2,1)}, bf16[256,1024]{1,0:T(8,128)(2,1)}, u32[]{:S(2)}, u32[]{:S(2)}) collective-permute-start(bf16[256,1024]{1,0:T(8,128)(2,1)} %bitcast.3.low), channel_id=1, source_target_pairs={{0,384},{128,0},{256,128},{384,256},{1,25},{9,1},{17,9},{25,17},{2... | collective-permute-start | bytes 1572872 | tf_op jit(solution)/shard_map/ppermute | solution.py:40
  45.1 14.7 %collective-permute-start.4 = (bf16[256,1024]{1,0:T(8,128)(2,1)}, bf16[256,1024]{1,0:T(8,128)(2,1)}, u32[]{:S(2)}, u32[]{:S(2)}) collective-permute-start(bf16[256,1024]{1,0:T(8,128)(2,1)} %collective-permute-done.up_on), channel_id=1, source_target_pairs={{0,128},{128,256},{256,384},{384,0},{1,9},{9,17},{17,25},{25,1},{2... | collective-permute-start | bytes 1572872 | tf_op jit(solution)/shard_map/ppermute | solution.py:40
  50.0 19.8 %collective-permute-start.5 = (bf16[256,1024]{1,0:T(8,128)(2,1)}, bf16[256,1024]{1,0:T(8,128)(2,1)}, u32[]{:S(2)}, u32[]{:S(2)}) collective-permute-start(bf16[256,1024]{1,0:T(8,128)(2,1)} %collective-permute-done.3.down_on), channel_id=1, source_target_pairs={{0,384},{128,0},{256,128},{384,256},{1,25},{9,1},{17,9},{25,17},{2... | collective-permute-start | bytes 1572872 | tf_op jit(solution)/shard_map/ppermute | solution.py:40
  52.2 40.1 %all-to-all-start.2 = ((bf16[64,2,16,256]{3,2,1,0:T(8,128)(2,1)}), bf16[64,2,16,256]{3,2,1,0:T(8,128)(2,1)S(1)}, u32[]{:S(2)}, u32[]{:S(2)}) async-start(bf16[64,2,16,256]{3,2,1,0:T(8,128)(2,1)} %bitcast.11), calls=%async_computation.2 | async-start | bytes 2097152 | tf_op jit(solution)/shard_map/all_to_all | solution.py:285
  69.8 1.0 copy-start.3
  74.3 14.5 %copy-start.4 = (s32[32,6]{0,1:T(8,128)S(1)}, s32[32,6]{0,1:T(8,128)}, u32[]{:S(2)}) copy-start(s32[32,6]{0,1:T(8,128)} %param.13) | copy-start | bytes 2308
  74.3 4.6 %collective-permute-start.6 = (f32[1024,256]{1,0:T(8,128)S(1)}, f32[1024,256]{1,0:T(8,128)S(1)}, u32[]{:S(2)}, u32[]{:S(2)}) collective-permute-start(f32[1024,256]{1,0:T(8,128)S(1)} %get-tuple-element.19), channel_id=1, source_target_pairs={{0,1},{1,0},{2,3},{3,2},{4,5},{5,4},{6,7},{7,6},{8,9},{9,8},{10,11... | collective-permute-start | bytes 3145736 | tf_op jit(solution)/shard_map/ppermute | solution.py:59
  78.9 28.2 %copy-start.1 = (bf16[8,32,1024]{2,1,0:T(8,128)(2,1)S(1)}, bf16[8,32,1024]{2,1,0:T(8,128)(2,1)}, u32[]{:S(2)}) copy-start(bf16[8,32,1024]{2,1,0:T(8,128)(2,1)} %queries) | copy-start | bytes 1572868
  78.9 28.2 %copy-start.2 = (s32[32]{0:T(128)S(1)}, s32[32]{0:T(128)}, u32[]{:S(2)}) copy-start(s32[32]{0:T(128)} %lengths.1) | copy-start | bytes 388
  79.7 12.5 %collective-permute-start.8 = (f16[256,256]{1,0:T(8,128)(2,1)}, f16[256,256]{1,0:T(8,128)(2,1)}, u32[]{:S(2)}, u32[]{:S(2)}) collective-permute-start(f16[256,256]{1,0:T(8,128)(2,1)} %get-tuple-element.32), channel_id=1, source_target_pairs={{0,2},{1,7},{2,0},{3,5},{4,6},{5,3},{6,4},{7,1},{8,10},{9,15},{10,... | collective-permute-start | bytes 393224 | tf_op jit(solution)/shard_map/ppermute | solution.py:51
  88.9 17.2 %collective-permute-start.7 = (f16[256,256]{1,0:T(8,128)(2,1)}, f16[256,256]{1,0:T(8,128)(2,1)}, u32[]{:S(2)}, u32[]{:S(2)}) collective-permute-start(f16[256,256]{1,0:T(8,128)(2,1)} %get-tuple-element.33), channel_id=1, source_target_pairs={{0,2},{1,7},{2,0},{3,5},{4,6},{5,3},{6,4},{7,1},{8,10},{9,15},{10,... | collective-permute-start | bytes 393224 | tf_op jit(solution)/shard_map/ppermute | solution.py:51
  93.3 18.7 %collective-permute-start.9 = (f16[256,256]{1,0:T(8,128)(2,1)S(1)}, f16[256,256]{1,0:T(8,128)(2,1)S(1)}, u32[]{:S(2)}, u32[]{:S(2)}) collective-permute-start(f16[256,256]{1,0:T(8,128)(2,1)S(1)} %multiply_convert_fusion), channel_id=1, source_target_pairs={{0,6},{1,3},{2,4},{3,1},{4,2},{5,7},{6,0},{7,5},{8,14},{9,11},{10,... | collective-permute-start | bytes 393224 | tf_op jit(solution)/shard_map/ppermute | solution.py:51

commit v4 on v3

--- a/solution.py
+++ b/solution.py
@@ -63,17 +63,12 @@
     first = lax.all_to_all(
         jnp.broadcast_to(held[None], (SIDE,) + held.shape), "zl", 0, 0, tiled=True
     )
-    block = first.reshape((1, SIDE * held.shape[0], held.shape[1]))
-    second = lax.all_to_all(
-        jnp.broadcast_to(block, (SIDE,) + block.shape[1:]),
-        AXES, 0, 0, axis_index_groups=lines(1),
-    )
-    second, outgoing = lax.optimization_barrier((second, outgoing))
-    own = second.reshape(-1, held.shape[1])
-    half = own.shape[0] // 2
-    low, high = own[:half], own[half:]
-    up_on, down_on = shift(low, 2, 1), shift(high, 2, -1)
-    up_end, down_end = shift(high, 2, 1), shift(low, 2, -1)
+    first, outgoing = lax.optimization_barrier((first, outgoing))
+    block = first.reshape(-1, held.shape[1])
+    high = jnp.concatenate([shift(block, 1, 2), shift(block, 1, -1)])
+    low = jnp.concatenate([block, shift(block, 1, 1)])
+    down_on, up_on = shift(high, 2, -1), shift(low, 2, 1)
+    down_end, up_end = shift(low, 2, -1), shift(high, 2, 1)
     far_up, far_down = shift(up_on, 2, 1), shift(down_on, 2, -1)
     return outgoing, (low, high, up_on, up_end, down_end, down_on, far_up, far_down)
 
@@ -82,8 +77,9 @@
     x, y = lax.axis_index("x"), lax.axis_index("y")
     place = jnp.arange(64)
     slot, a1, zl = place // 16, (place // 4) % 4, place % 4
-    me2 = jnp.where(c == 0, x, y)
-    a2 = (me2 + jnp.where(slot == 0, 0, jnp.where(slot == 1, 3, jnp.where(slot == 2, 1, 2)))) % 4
+    me1, me2 = jnp.where(c == 0, y, x), jnp.where(c == 0, x, y)
+    turns = lambda k: jnp.where(k == 0, 0, jnp.where(k == 1, 3, jnp.where(k == 2, 1, 2)))
+    a1, a2 = (me1 - a1) % SIDE, (me2 + turns(slot)) % SIDE
     held = jnp.where(c == 0, a2 * 16 + zl * 4 + a1, a1 * 16 + zl * 4 + a2)
     block = jnp.sum(jnp.where(owner[None, :] == held[:, None], jnp.arange(64)[None, :], 0), axis=1)
     column = block // 8

time: 116 us -> 112 us (0.966)
  the two profiles are of different devices: /device:TPU:6 before, /device:TPU:128 now
where the time goes in v4:
time: 112 us; the launch traced here: 111 us
  starting transfers between devices  65.1 us (58%)
  waiting for transfers between devices  27.6 us (25%)
  Pallas kernels  8.88 us (8%)
  local copies, waits for them, and re-layouts  5.67 us (5%)
  other arithmetic  3.14 us (3%)
    ppermute x9, starting transfers between devices, shift(): return lax.ppermute(value, AXES, pairs)  31.4 us
    ppermute x3, starting transfers between devices, z_exchange(): return lax.ppermute((value * SCALE).astype(jnp.float16), TENSOR, pairs)  18.6 us
    ppermute x9, waiting for transfers between devices, shift(): return lax.ppermute(value, AXES, pairs)  10.2 us
    all_to_all x1, starting transfers between devices, on_device(): lax.all_to_all(outgoing, REPLICA, split_axis=0, concat_axis=0, tiled=True)  7.28 us
    all_to_all x1, waiting for transfers between devices, on_device(): lax.all_to_all(outgoing, REPLICA, split_axis=0, concat_axis=0, tiled=True)  6.2 us
    all_to_all x1, starting transfers between devices, gather_weight(): lax.all_to_all(jnp.broadcast_to(held[None], (SIDE,) + held.shape), 'zl',...  5.89 us
    all_to_all x1, waiting for transfers between devices, gather_weight(): lax.all_to_all(jnp.broadcast_to(held[None], (SIDE,) + held.shape), 'zl',...  4.94 us
    ppermute x3, waiting for transfers between devices, z_exchange(): return lax.ppermute((value * SCALE).astype(jnp.float16), TENSOR, pairs)  3.65 us
  transfers between devices with their start and end apart: 15, of which 8 were waited for; matrix products, arithmetic and copies ran while one was open for 6% of the time, Pallas kernels for 6%

profile of v4, /device:TPU:128, one launch (start us, length us, event | category | flops | bytes accessed | tf_op | source)
XLA Modules:
  0.0 111.3 jit_solution(11809502421158820492)
XLA Ops:
  0.6 1.6 %broadcast_in_dim.43 = bf16[4,32,1024]{2,1,0:T(8,128)(2,1)} broadcast(bf16[32,1024]{1,0:T(8,128)(2,1)} %param.9), dimensions={1,2} | broadcast | bytes 327680 | tf_op jit(solution)/shard_map/broadcast_in_dim | solution.py:64
  2.2 5.9 %all-to-all-start = ((bf16[4,32,1024]{2,1,0:T(8,128)(2,1)}), bf16[4,32,1024]{2,1,0:T(8,128)(2,1)S(1)}, u32[]{:S(2)}, u32[]{:S(2)}) async-start(bf16[4,32,1024]{2,1,0:T(8,128)(2,1)} %broadcast_in_dim.43), calls=%async_computation | async-start | bytes 524288 | tf_op jit(solution)/shard_map/all_to_all | solution.py:63
  8.1 0.8 copy.14
  9.0 3.0 %gather_fusion = bf16[128,16,256]{2,1,0:T(8,128)(2,1)} fusion(bf16[192,16,256]{2,1,0:T(8,128)(2,1)} %pool.1, s32[1024]{0:T(1024)S(1)} %pad_clamp_fusion), kind=kCustom, calls=%fused_computation | custom fusion | bytes 2097664 | tf_op jit(solution)/shard_map/jit(_take)/gather | solution.py:277
  12.1 4.9 %all-to-all-done = bf16[4,32,1024]{2,1,0:T(8,128)(2,1)S(1)} async-done(((bf16[4,32,1024]{2,1,0:T(8,128)(2,1)}), bf16[4,32,1024]{2,1,0:T(8,128)(2,1)S(1)}, u32[]{:S(2)}, u32[]{:S(2)}) %all-to-all-start) | async-done | bytes 262176 | tf_op jit(solution)/shard_map/all_to_all | solution.py:63
  17.0 5.1 %collective-permute-start.1 = (bf16[128,1024]{1,0:T(8,128)(2,1)S(1)}, bf16[128,1024]{1,0:T(8,128)(2,1)S(1)}, u32[]{:S(2)}, u32[]{:S(2)}) collective-permute-start(bf16[128,1024]{1,0:T(8,128)(2,1)S(1)} %bitcast.7), channel_id=1, source_target_pairs={{0,16},{8,24},{16,0},{24,8},{1,257},{129,385},{257,1},{385,129},{2... | collective-permute-start | bytes 786440 | tf_op jit(solution)/shard_map/ppermute | solution.py:40
  22.1 3.0 %collective-permute-start.2 = (bf16[128,1024]{1,0:T(8,128)(2,1)S(1)}, bf16[128,1024]{1,0:T(8,128)(2,1)S(1)}, u32[]{:S(2)}, u32[]{:S(2)}) collective-permute-start(bf16[128,1024]{1,0:T(8,128)(2,1)S(1)} %bitcast.8), channel_id=1, source_target_pairs={{0,24},{8,0},{16,8},{24,16},{1,385},{129,1},{257,129},{385,257},{2... | collective-permute-start | bytes 786440 | tf_op jit(solution)/shard_map/ppermute | solution.py:40
  25.1 2.9 %collective-permute-start = (bf16[128,1024]{1,0:T(8,128)(2,1)S(1)}, bf16[128,1024]{1,0:T(8,128)(2,1)S(1)}, u32[]{:S(2)}, u32[]{:S(2)}) collective-permute-start(bf16[128,1024]{1,0:T(8,128)(2,1)S(1)} %bitcast.9), channel_id=1, source_target_pairs={{0,8},{8,16},{16,24},{24,0},{1,129},{129,257},{257,385},{385,1},{2... | collective-permute-start | bytes 786440 | tf_op jit(solution)/shard_map/ppermute | solution.py:40
  28.0 2.4 %collective-permute-done.2 = bf16[128,1024]{1,0:T(8,128)(2,1)S(1)} collective-permute-done((bf16[128,1024]{1,0:T(8,128)(2,1)S(1)}, bf16[128,1024]{1,0:T(8,128)(2,1)S(1)}, u32[]{:S(2)}, u32[]{:S(2)}) %collective-permute-start.2) | collective-permute-done | bytes 262176 | tf_op jit(solution)/shard_map/ppermute | solution.py:40
  30.4 4.8 %collective-permute-start.6 = (bf16[256,1024]{1,0:T(8,128)(2,1)S(1)}, bf16[256,1024]{1,0:T(8,128)(2,1)}, u32[]{:S(2)}, u32[]{:S(2)}) collective-permute-start(bf16[256,1024]{1,0:T(8,128)(2,1)S(1)} %constant_dynamic-update-slice_fusion.high), channel_id=1, source_target_pairs={{0,384},{128,0},{256,128},{384,256},{1,25},{9,1},{17,9},{25,17},{2... | collective-permute-start | bytes 1572872 | tf_op jit(solution)/shard_map/ppermute | solution.py:40
  35.3 2.7 %collective-permute-start.3 = (bf16[256,1024]{1,0:T(8,128)(2,1)S(1)}, bf16[256,1024]{1,0:T(8,128)(2,1)}, u32[]{:S(2)}, u32[]{:S(2)}) collective-permute-start(bf16[256,1024]{1,0:T(8,128)(2,1)S(1)} %pad_maximum_fusion.low), channel_id=1, source_target_pairs={{0,128},{128,256},{256,384},{384,0},{1,9},{9,17},{17,25},{25,1},{2... | collective-permute-start | bytes 1572872 | tf_op jit(solution)/shard_map/ppermute | solution.py:40
  38.0 3.4 %collective-permute-start.4 = (bf16[256,1024]{1,0:T(8,128)(2,1)S(1)}, bf16[256,1024]{1,0:T(8,128)(2,1)}, u32[]{:S(2)}, u32[]{:S(2)}) collective-permute-start(bf16[256,1024]{1,0:T(8,128)(2,1)S(1)} %constant_dynamic-update-slice_fusion.high), channel_id=1, source_target_pairs={{0,128},{128,256},{256,384},{384,0},{1,9},{9,17},{17,25},{25,1},{2... | collective-permute-start | bytes 1572872 | tf_op jit(solution)/shard_map/ppermute | solution.py:40
  41.4 3.7 %collective-permute-start.5 = (bf16[256,1024]{1,0:T(8,128)(2,1)S(1)}, bf16[256,1024]{1,0:T(8,128)(2,1)}, u32[]{:S(2)}, u32[]{:S(2)}) collective-permute-start(bf16[256,1024]{1,0:T(8,128)(2,1)S(1)} %pad_maximum_fusion.low), channel_id=1, source_target_pairs={{0,384},{128,0},{256,128},{384,256},{1,25},{9,1},{17,9},{25,17},{2... | collective-permute-start | bytes 1572872 | tf_op jit(solution)/shard_map/ppermute | solution.py:40
  45.1 3.1 %collective-permute-start.8 = (bf16[256,1024]{1,0:T(8,128)(2,1)}, bf16[256,1024]{1,0:T(8,128)(2,1)}, u32[]{:S(2)}, u32[]{:S(2)}) collective-permute-start(bf16[256,1024]{1,0:T(8,128)(2,1)} %collective-permute-done.6.down_on), channel_id=1, source_target_pairs={{0,384},{128,0},{256,128},{384,256},{1,25},{9,1},{17,9},{25,17},{2... | collective-permute-start | bytes 1572872 | tf_op jit(solution)/shard_map/ppermute | solution.py:40
  48.2 2.7 %collective-permute-start.7 = (bf16[256,1024]{1,0:T(8,128)(2,1)}, bf16[256,1024]{1,0:T(8,128)(2,1)}, u32[]{:S(2)}, u32[]{:S(2)}) collective-permute-start(bf16[256,1024]{1,0:T(8,128)(2,1)} %collective-permute-done.3.up_on), channel_id=1, source_target_pairs={{0,128},{128,256},{256,384},{384,0},{1,9},{9,17},{17,25},{25,1},{2... | collective-permute-start | bytes 1572872 | tf_op jit(solution)/shard_map/ppermute | solution.py:40
  51.2 7.3 %all-to-all-start.1 = ((bf16[64,2,16,256]{3,2,1,0:T(8,128)(2,1)}), bf16[64,2,16,256]{3,2,1,0:T(8,128)(2,1)S(1)}, u32[]{:S(2)}, u32[]{:S(2)}) async-start(bf16[64,2,16,256]{3,2,1,0:T(8,128)(2,1)} %bitcast.6), calls=%async_computation.1 | async-start | bytes 2097152 | tf_op jit(solution)/shard_map/all_to_all | solution.py:281
  58.5 1.7 %collective-permute-done.8.far_down = bf16[256,1024]{1,0:T(8,128)(2,1)} collective-permute-done((bf16[256,1024]{1,0:T(8,128)(2,1)}, bf16[256,1024]{1,0:T(8,128)(2,1)}, u32[]{:S(2)}, u32[]{:S(2)}) %collective-permute-start.8) | collective-permute-done | bytes 524320 | tf_op jit(solution)/shard_map/ppermute | solution.py:40
  60.2 6.1 %collective-permute-done.7.far_up = bf16[256,1024]{1,0:T(8,128)(2,1)} collective-permute-done((bf16[256,1024]{1,0:T(8,128)(2,1)}, bf16[256,1024]{1,0:T(8,128)(2,1)}, u32[]{:S(2)}, u32[]{:S(2)}) %collective-permute-start.7) | collective-permute-done | bytes 524320 | tf_op jit(solution)/shard_map/ppermute | solution.py:40
  66.3 3.3 %project.1 = (f32[1024,256]{1,0:T(8,128)S(1)}, f32[512,256]{1,0:T(8,128)S(1)}, f32[512,256]{1,0:T(8,128)S(1)}) custom-call(s32[64]{0:T(128)S(1)} %fusion.4.places, bf16[256,1024]{1,0:T(8,128)(2,1)S(1)} %bitcast.5, bf16[256,1024]{1,0:T(8,128)(2,1)S(1)} %pad_maximum_fusion.low, bf16[256,1024]{1,0:T(8,128)(2,1)S(1)} %constant_dynamic-update-slice_fusion.high, ...), custom_call_target="tpu_custom_call" | custom-call | flops 40000000000 | bytes 6000000 | tf_op jit(solution)/shard_map/project/pallas_call | solution.py:119
  69.7 1.9 %collective-permute-start.9 = (f32[1024,256]{1,0:T(8,128)S(1)}, f32[1024,256]{1,0:T(8,128)S(1)}, u32[]{:S(2)}, u32[]{:S(2)}) collective-permute-start(f32[1024,256]{1,0:T(8,128)S(1)} %get-tuple-element.19), channel_id=1, source_target_pairs={{0,1},{1,0},{2,3},{3,2},{4,5},{5,4},{6,7},{7,6},{8,9},{9,8},{10,11... | collective-permute-start | bytes 3145736 | tf_op jit(solution)/shard_map/ppermute | solution.py:59
  71.6 2.6 %collective-permute-done.9 = f32[1024,256]{1,0:T(8,128)S(1)} collective-permute-done((f32[1024,256]{1,0:T(8,128)S(1)}, f32[1024,256]{1,0:T(8,128)S(1)}, u32[]{:S(2)}, u32[]{:S(2)}) %collective-permute-start.9) | collective-permute-done | bytes 1048608 | tf_op jit(solution)/shard_map/ppermute | solution.py:59
  74.2 0.9 fusion.1
  75.1 1.9 %collective-permute-start.11 = (f16[256,256]{1,0:T(8,128)(2,1)}, f16[256,256]{1,0:T(8,128)(2,1)}, u32[]{:S(2)}, u32[]{:S(2)}) collective-permute-start(f16[256,256]{1,0:T(8,128)(2,1)} %get-tuple-element.32), channel_id=1, source_target_pairs={{0,2},{1,7},{2,0},{3,5},{4,6},{5,3},{6,4},{7,1},{8,10},{9,15},{10,... | collective-permute-start | bytes 393224 | tf_op jit(solution)/shard_map/ppermute | solution.py:51
  77.1 7.8 %collective-permute-start.10 = (f16[256,256]{1,0:T(8,128)(2,1)}, f16[256,256]{1,0:T(8,128)(2,1)}, u32[]{:S(2)}, u32[]{:S(2)}) collective-permute-start(f16[256,256]{1,0:T(8,128)(2,1)} %get-tuple-element.33), channel_id=1, source_target_pairs={{0,2},{1,7},{2,0},{3,5},{4,6},{5,3},{6,4},{7,1},{8,10},{9,15},{10,... | collective-permute-start | bytes 393224 | tf_op jit(solution)/shard_map/ppermute | solution.py:51
  84.9 1.8 %collective-permute-done.11 = f16[256,256]{1,0:T(8,128)(2,1)} collective-permute-done((f16[256,256]{1,0:T(8,128)(2,1)}, f16[256,256]{1,0:T(8,128)(2,1)}, u32[]{:S(2)}, u32[]{:S(2)}) %collective-permute-start.11) | collective-permute-done | bytes 131104 | tf_op jit(solution)/shard_map/ppermute | solution.py:51
  86.7 6.2 %all-to-all-done.1 = bf16[64,2,16,256]{3,2,1,0:T(8,128)(2,1)S(1)} async-done(((bf16[64,2,16,256]{3,2,1,0:T(8,128)(2,1)}), bf16[64,2,16,256]{3,2,1,0:T(8,128)(2,1)S(1)}, u32[]{:S(2)}, u32[]{:S(2)}) %all-to-all-start.1) | async-done | bytes 1048608 | tf_op jit(solution)/shard_map/all_to_all | solution.py:281
  92.9 1.0 multiply_convert_fusion
  94.0 8.9 %collective-permute-start.12 = (f16[256,256]{1,0:T(8,128)(2,1)S(1)}, f16[256,256]{1,0:T(8,128)(2,1)S(1)}, u32[]{:S(2)}, u32[]{:S(2)}) collective-permute-start(f16[256,256]{1,0:T(8,128)(2,1)S(1)} %multiply_convert_fusion), channel_id=1, source_target_pairs={{0,6},{1,3},{2,4},{3,1},{4,2},{5,7},{6,0},{7,5},{8,14},{9,11},{10,... | collective-permute-start | bytes 393224 | tf_op jit(solution)/shard_map/ppermute | solution.py:51
  102.9 0.9 multiply_add_fusion.1
  103.9 2.8 %past.1 = (f32[32,64,128]{2,1,0:T(8,128)S(1)}, bf16[32,64,128]{2,1,0:T(8,128)(2,1)S(1)}, bf16[32,128,128]{2,1,0:T(8,128)(2,1)S(1)}) custom-call(s32[32,6]{1,0:T(8,128)S(1)} %copy.15.table, s32[32]{0:T(128)S(1)} %copy-done.2, bf16[8,32,1024]{2,1,0:T(8,128)(2,1)S(1)} %copy-done.1, bf16[192,16,256]{2,1,0:T(8,128)(2,1)S(1)} %copy-done, ...), custom_call_target="tpu_custom_call" | custom-call | flops 70000000 | bytes 8000000 | tf_op jit(solution)/shard_map/past/pallas_call | solution.py:185
  106.7 1.9 %collective-permute-done.12 = f16[256,256]{1,0:T(8,128)(2,1)S(1)} collective-permute-done((f16[256,256]{1,0:T(8,128)(2,1)S(1)}, f16[256,256]{1,0:T(8,128)(2,1)S(1)}, u32[]{:S(2)}, u32[]{:S(2)}) %collective-permute-start.12) | collective-permute-done | bytes 131104 | tf_op jit(solution)/shard_map/ppermute | solution.py:51
  108.6 2.8 %finish.1 = (bf16[8,32,256]{2,1,0:T(8,128)(2,1)}, bf16[8,32,1024]{2,1,0:T(8,128)(2,1)}) custom-call(f32[256,256]{1,0:T(8,128)S(1)} %multiply_add_fusion.refs_0_, f32[32,64,128]{2,1,0:T(8,128)S(1)} %get-tuple-element.29.refs_1_, bf16[32,64,128]{2,1,0:T(8,128)(2,1)S(1)} %get-tuple-element.30.refs_2_, bf16[32,128,128]{2,1,0:T(8,128)(2,1)S(1)} %get-tuple-element.31.refs_3_), custom_call_target="tpu_custom_call" | custom-call | flops 140000000 | bytes 4000000 | tf_op jit(solution)/shard_map/finish/pallas_call | solution.py:251
  (29 shorter events, 0.6 us)
Async XLA Ops:
  2.2 14.8 %all-to-all-start = ((bf16[4,32,1024]{2,1,0:T(8,128)(2,1)}), bf16[4,32,1024]{2,1,0:T(8,128)(2,1)S(1)}, u32[]{:S(2)}, u32[]{:S(2)}) async-start(bf16[4,32,1024]{2,1,0:T(8,128)(2,1)} %broadcast_in_dim.43), calls=%async_computation | async-start | bytes 524288 | tf_op jit(solution)/shard_map/all_to_all | solution.py:63
  12.1 38.9 %copy-start.5 = (s32[64]{0:T(128)S(1)}, s32[64]{0:T(128)}, u32[]{:S(2)}) copy-start(s32[64]{0:T(128)} %param.10) | copy-start | bytes 772
  17.0 11.0 %collective-permute-start.1 = (bf16[128,1024]{1,0:T(8,128)(2,1)S(1)}, bf16[128,1024]{1,0:T(8,128)(2,1)S(1)}, u32[]{:S(2)}, u32[]{:S(2)}) collective-permute-start(bf16[128,1024]{1,0:T(8,128)(2,1)S(1)} %bitcast.7), channel_id=1, source_target_pairs={{0,16},{8,24},{16,0},{24,8},{1,257},{129,385},{257,1},{385,129},{2... | collective-permute-start | bytes 786440 | tf_op jit(solution)/shard_map/ppermute | solution.py:40
  22.1 8.3 %collective-permute-start.2 = (bf16[128,1024]{1,0:T(8,128)(2,1)S(1)}, bf16[128,1024]{1,0:T(8,128)(2,1)S(1)}, u32[]{:S(2)}, u32[]{:S(2)}) collective-permute-start(bf16[128,1024]{1,0:T(8,128)(2,1)S(1)} %bitcast.8), channel_id=1, source_target_pairs={{0,24},{8,0},{16,8},{24,16},{1,385},{129,1},{257,129},{385,257},{2... | collective-permute-start | bytes 786440 | tf_op jit(solution)/shard_map/ppermute | solution.py:40
  25.1 10.1 %collective-permute-start = (bf16[128,1024]{1,0:T(8,128)(2,1)S(1)}, bf16[128,1024]{1,0:T(8,128)(2,1)S(1)}, u32[]{:S(2)}, u32[]{:S(2)}) collective-permute-start(bf16[128,1024]{1,0:T(8,128)(2,1)S(1)} %bitcast.9), channel_id=1, source_target_pairs={{0,8},{8,16},{16,24},{24,0},{1,129},{129,257},{257,385},{385,1},{2... | collective-permute-start | bytes 786440 | tf_op jit(solution)/shard_map/ppermute | solution.py:40
  30.4 35.9 %copy-start.3 = (bf16[8,32,1024]{2,1,0:T(8,128)(2,1)S(1)}, bf16[8,32,1024]{2,1,0:T(8,128)(2,1)}, u32[]{:S(2)}) copy-start(bf16[8,32,1024]{2,1,0:T(8,128)(2,1)} %param.8) | copy-start | bytes 1572868
  30.4 14.7 %collective-permute-start.6 = (bf16[256,1024]{1,0:T(8,128)(2,1)S(1)}, bf16[256,1024]{1,0:T(8,128)(2,1)}, u32[]{:S(2)}, u32[]{:S(2)}) collective-permute-start(bf16[256,1024]{1,0:T(8,128)(2,1)S(1)} %constant_dynamic-update-slice_fusion.high), channel_id=1, source_target_pairs={{0,384},{128,0},{256,128},{384,256},{1,25},{9,1},{17,9},{25,17},{2... | collective-permute-start | bytes 1572872 | tf_op jit(solution)/shard_map/ppermute | solution.py:40
  35.3 12.9 %collective-permute-start.3 = (bf16[256,1024]{1,0:T(8,128)(2,1)S(1)}, bf16[256,1024]{1,0:T(8,128)(2,1)}, u32[]{:S(2)}, u32[]{:S(2)}) collective-permute-start(bf16[256,1024]{1,0:T(8,128)(2,1)S(1)} %pad_maximum_fusion.low), channel_id=1, source_target_pairs={{0,128},{128,256},{256,384},{384,0},{1,9},{9,17},{17,25},{25,1},{2... | collective-permute-start | bytes 1572872 | tf_op jit(solution)/shard_map/ppermute | solution.py:40
  38.0 20.5 %collective-permute-start.4 = (bf16[256,1024]{1,0:T(8,128)(2,1)S(1)}, bf16[256,1024]{1,0:T(8,128)(2,1)}, u32[]{:S(2)}, u32[]{:S(2)}) collective-permute-start(bf16[256,1024]{1,0:T(8,128)(2,1)S(1)} %constant_dynamic-update-slice_fusion.high), channel_id=1, source_target_pairs={{0,128},{128,256},{256,384},{384,0},{1,9},{9,17},{17,25},{25,1},{2... | collective-permute-start | bytes 1572872 | tf_op jit(solution)/shard_map/ppermute | solution.py:40
  41.4 17.1 %collective-permute-start.5 = (bf16[256,1024]{1,0:T(8,128)(2,1)S(1)}, bf16[256,1024]{1,0:T(8,128)(2,1)}, u32[]{:S(2)}, u32[]{:S(2)}) collective-permute-start(bf16[256,1024]{1,0:T(8,128)(2,1)S(1)} %pad_maximum_fusion.low), channel_id=1, source_target_pairs={{0,384},{128,0},{256,128},{384,256},{1,25},{9,1},{17,9},{25,17},{2... | collective-permute-start | bytes 1572872 | tf_op jit(solution)/shard_map/ppermute | solution.py:40
  45.1 15.2 %collective-permute-start.8 = (bf16[256,1024]{1,0:T(8,128)(2,1)}, bf16[256,1024]{1,0:T(8,128)(2,1)}, u32[]{:S(2)}, u32[]{:S(2)}) collective-permute-start(bf16[256,1024]{1,0:T(8,128)(2,1)} %collective-permute-done.6.down_on), channel_id=1, source_target_pairs={{0,384},{128,0},{256,128},{384,256},{1,25},{9,1},{17,9},{25,17},{2... | collective-permute-start | bytes 1572872 | tf_op jit(solution)/shard_map/ppermute | solution.py:40
  48.2 18.1 %collective-permute-start.7 = (bf16[256,1024]{1,0:T(8,128)(2,1)}, bf16[256,1024]{1,0:T(8,128)(2,1)}, u32[]{:S(2)}, u32[]{:S(2)}) collective-permute-start(bf16[256,1024]{1,0:T(8,128)(2,1)} %collective-permute-done.3.up_on), channel_id=1, source_target_pairs={{0,128},{128,256},{256,384},{384,0},{1,9},{9,17},{17,25},{25,1},{2... | collective-permute-start | bytes 1572872 | tf_op jit(solution)/shard_map/ppermute | solution.py:40
  51.2 41.7 %all-to-all-start.1 = ((bf16[64,2,16,256]{3,2,1,0:T(8,128)(2,1)}), bf16[64,2,16,256]{3,2,1,0:T(8,128)(2,1)S(1)}, u32[]{:S(2)}, u32[]{:S(2)}) async-start(bf16[64,2,16,256]{3,2,1,0:T(8,128)(2,1)} %bitcast.6), calls=%async_computation.1 | async-start | bytes 2097152 | tf_op jit(solution)/shard_map/all_to_all | solution.py:281
  69.7 7.4 %copy-start.4 = (s32[32,6]{0,1:T(8,128)S(1)}, s32[32,6]{0,1:T(8,128)}, u32[]{:S(2)}) copy-start(s32[32,6]{0,1:T(8,128)} %param.13) | copy-start | bytes 2308
  69.7 4.6 %collective-permute-start.9 = (f32[1024,256]{1,0:T(8,128)S(1)}, f32[1024,256]{1,0:T(8,128)S(1)}, u32[]{:S(2)}, u32[]{:S(2)}) collective-permute-start(f32[1024,256]{1,0:T(8,128)S(1)} %get-tuple-element.19), channel_id=1, source_target_pairs={{0,1},{1,0},{2,3},{3,2},{4,5},{5,4},{6,7},{7,6},{8,9},{9,8},{10,11... | collective-permute-start | bytes 3145736 | tf_op jit(solution)/shard_map/ppermute | solution.py:59
  74.2 29.6 %copy-start = (bf16[192,16,256]{2,1,0:T(8,128)(2,1)S(1)}, bf16[192,16,256]{2,1,0:T(8,128)(2,1)}, u32[]{:S(2)}) copy-start(bf16[192,16,256]{2,1,0:T(8,128)(2,1)} %pool.1) | copy-start | bytes 4718596
  74.2 29.6 %copy-start.1 = (bf16[8,32,1024]{2,1,0:T(8,128)(2,1)S(1)}, bf16[8,32,1024]{2,1,0:T(8,128)(2,1)}, u32[]{:S(2)}) copy-start(bf16[8,32,1024]{2,1,0:T(8,128)(2,1)} %queries) | copy-start | bytes 1572868
  74.2 29.6 %copy-start.2 = (s32[32]{0:T(128)S(1)}, s32[32]{0:T(128)}, u32[]{:S(2)}) copy-start(s32[32]{0:T(128)} %lengths.1) | copy-start | bytes 388
  75.1 11.6 %collective-permute-start.11 = (f16[256,256]{1,0:T(8,128)(2,1)}, f16[256,256]{1,0:T(8,128)(2,1)}, u32[]{:S(2)}, u32[]{:S(2)}) collective-permute-start(f16[256,256]{1,0:T(8,128)(2,1)} %get-tuple-element.32), channel_id=1, source_target_pairs={{0,2},{1,7},{2,0},{3,5},{4,6},{5,3},{6,4},{7,1},{8,10},{9,15},{10,... | collective-permute-start | bytes 393224 | tf_op jit(solution)/shard_map/ppermute | solution.py:51
  77.1 25.8 %collective-permute-start.10 = (f16[256,256]{1,0:T(8,128)(2,1)}, f16[256,256]{1,0:T(8,128)(2,1)}, u32[]{:S(2)}, u32[]{:S(2)}) collective-permute-start(f16[256,256]{1,0:T(8,128)(2,1)} %get-tuple-element.33), channel_id=1, source_target_pairs={{0,2},{1,7},{2,0},{3,5},{4,6},{5,3},{6,4},{7,1},{8,10},{9,15},{10,... | collective-permute-start | bytes 393224 | tf_op jit(solution)/shard_map/ppermute | solution.py:51
  94.0 14.6 %collective-permute-start.12 = (f16[256,256]{1,0:T(8,128)(2,1)S(1)}, f16[256,256]{1,0:T(8,128)(2,1)S(1)}, u32[]{:S(2)}, u32[]{:S(2)}) collective-permute-start(f16[256,256]{1,0:T(8,128)(2,1)S(1)} %multiply_convert_fusion), channel_id=1, source_target_pairs={{0,6},{1,3},{2,4},{3,1},{4,2},{5,7},{6,0},{7,5},{8,14},{9,11},{10,... | collective-permute-start | bytes 393224 | tf_op jit(solution)/shard_map/ppermute | solution.py:51

commit v5 on v4

--- a/solution.py
+++ b/solution.py
@@ -8,7 +8,6 @@
 HD = 128
 SIDE = 4
 CORES = 2
-SCALE = 16.0
 SPAN = 96
 WIDE = 128
 AXES = ("x", "zl", "y", "zh", "c")
@@ -48,11 +47,7 @@
     pairs = [
         (zh * CORES + c, partner(zh, c, step) * CORES + c) for zh in RING for c in range(CORES)
     ]
-    return lax.ppermute((value * SCALE).astype(jnp.float16), TENSOR, pairs)
-
-
-def unscaled(value):
-    return value.astype(jnp.float32) * (1.0 / SCALE)
+    return lax.ppermute(value, TENSOR, pairs)
 
 
 def core_swap(value):
@@ -139,9 +134,9 @@
     got_near = z_exchange(near[256:] + got[256:512], 1)
     second, here = lax.optimization_barrier((late[:256] + got[512:768], late[256:] + got[768:]))
     got_far, arrived = lax.optimization_barrier((got_far, arrived))
-    got_late = z_exchange(second + unscaled(got_far), 2)
-    here, got_late = lax.optimization_barrier((here + unscaled(got_near), got_late))
-    return got, arrived, here + unscaled(got_late)
+    got_late = z_exchange(second + got_far, 2)
+    here, got_late = lax.optimization_barrier((here + got_near, got_late))
+    return got, arrived, here + got_late
 
 
 def past_kernel(table, lengths, queries, pool, arrived, scores, folded, values, cells, wide):

time: 112 us -> 129 us (1.15)
  the two profiles are of different devices: /device:TPU:128 before, /device:TPU:6 now
where the time goes in v5:
time: 129 us; the launch traced here: 128 us
  starting transfers between devices  66.4 us (51%)
  waiting for transfers between devices  40.3 us (31%)
  Pallas kernels  8.72 us (7%)
  local copies, waits for them, and re-layouts  6.73 us (5%)
  other arithmetic  4.91 us (4%)
    ppermute x9, starting transfers between devices, shift(): return lax.ppermute(value, AXES, pairs)  29.8 us
    ppermute x3, starting transfers between devices, z_exchange(): return lax.ppermute(value, TENSOR, pairs)  21 us
    ppermute x3, waiting for transfers between devices, z_exchange(): return lax.ppermute(value, TENSOR, pairs)  18.6 us
    ppermute x9, waiting for transfers between devices, shift(): return lax.ppermute(value, AXES, pairs)  7.93 us
    all_to_all x1, starting transfers between devices, on_device(): lax.all_to_all(outgoing, REPLICA, split_axis=0, concat_axis=0, tiled=True)  7.84 us
    all_to_all x1, waiting for transfers between devices, on_device(): lax.all_to_all(outgoing, REPLICA, split_axis=0, concat_axis=0, tiled=True)  6.13 us
    all_to_all x1, starting transfers between devices, gather_weight(): lax.all_to_all(jnp.broadcast_to(held[None], (SIDE,) + held.shape), 'zl',...  5.89 us
    all_to_all x1, waiting for transfers between devices, gather_weight(): lax.all_to_all(jnp.broadcast_to(held[None], (SIDE,) + held.shape), 'zl',...  4.94 us
  transfers between devices with their start and end apart: 15, of which 9 were waited for; matrix products, arithmetic and copies ran while one was open for 6% of the time, Pallas kernels for 5%

profile of v5, /device:TPU:6, one launch (start us, length us, event | category | flops | bytes accessed | tf_op | source)
XLA Modules:
  0.0 128.0 jit_solution(6713454632440510551)
XLA Ops:
  0.6 1.6 %broadcast_in_dim.43 = bf16[4,32,1024]{2,1,0:T(8,128)(2,1)} broadcast(bf16[32,1024]{1,0:T(8,128)(2,1)} %param.9), dimensions={1,2} | broadcast | bytes 327680 | tf_op jit(solution)/shard_map/broadcast_in_dim | solution.py:59
  2.2 5.9 %all-to-all-start = ((bf16[4,32,1024]{2,1,0:T(8,128)(2,1)}), bf16[4,32,1024]{2,1,0:T(8,128)(2,1)S(1)}, u32[]{:S(2)}, u32[]{:S(2)}) async-start(bf16[4,32,1024]{2,1,0:T(8,128)(2,1)} %broadcast_in_dim.43), calls=%async_computation | async-start | bytes 524288 | tf_op jit(solution)/shard_map/all_to_all | solution.py:58
  9.0 3.1 %gather_fusion = bf16[128,16,256]{2,1,0:T(8,128)(2,1)} fusion(bf16[192,16,256]{2,1,0:T(8,128)(2,1)} %pool.1, s32[1024]{0:T(1024)S(1)} %pad_clamp_fusion), kind=kCustom, calls=%fused_computation | custom fusion | bytes 2097664 | tf_op jit(solution)/shard_map/jit(_take)/gather | solution.py:272
  12.1 4.9 %all-to-all-done = bf16[4,32,1024]{2,1,0:T(8,128)(2,1)S(1)} async-done(((bf16[4,32,1024]{2,1,0:T(8,128)(2,1)}), bf16[4,32,1024]{2,1,0:T(8,128)(2,1)S(1)}, u32[]{:S(2)}, u32[]{:S(2)}) %all-to-all-start) | async-done | bytes 262176 | tf_op jit(solution)/shard_map/all_to_all | solution.py:58
  17.0 5.1 %collective-permute-start.1 = (bf16[128,1024]{1,0:T(8,128)(2,1)S(1)}, bf16[128,1024]{1,0:T(8,128)(2,1)S(1)}, u32[]{:S(2)}, u32[]{:S(2)}) collective-permute-start(bf16[128,1024]{1,0:T(8,128)(2,1)S(1)} %bitcast.7), channel_id=1, source_target_pairs={{0,16},{8,24},{16,0},{24,8},{1,257},{129,385},{257,1},{385,129},{2... | collective-permute-start | bytes 786440 | tf_op jit(solution)/shard_map/ppermute | solution.py:39
  22.1 3.0 %collective-permute-start.2 = (bf16[128,1024]{1,0:T(8,128)(2,1)S(1)}, bf16[128,1024]{1,0:T(8,128)(2,1)S(1)}, u32[]{:S(2)}, u32[]{:S(2)}) collective-permute-start(bf16[128,1024]{1,0:T(8,128)(2,1)S(1)} %bitcast.8), channel_id=1, source_target_pairs={{0,24},{8,0},{16,8},{24,16},{1,385},{129,1},{257,129},{385,257},{2... | collective-permute-start | bytes 786440 | tf_op jit(solution)/shard_map/ppermute | solution.py:39
  25.1 2.9 %collective-permute-start = (bf16[128,1024]{1,0:T(8,128)(2,1)S(1)}, bf16[128,1024]{1,0:T(8,128)(2,1)S(1)}, u32[]{:S(2)}, u32[]{:S(2)}) collective-permute-start(bf16[128,1024]{1,0:T(8,128)(2,1)S(1)} %bitcast.9), channel_id=1, source_target_pairs={{0,8},{8,16},{16,24},{24,0},{1,129},{129,257},{257,385},{385,1},{2... | collective-permute-start | bytes 786440 | tf_op jit(solution)/shard_map/ppermute | solution.py:39
  28.0 2.4 %collective-permute-done.2 = bf16[128,1024]{1,0:T(8,128)(2,1)S(1)} collective-permute-done((bf16[128,1024]{1,0:T(8,128)(2,1)S(1)}, bf16[128,1024]{1,0:T(8,128)(2,1)S(1)}, u32[]{:S(2)}, u32[]{:S(2)}) %collective-permute-start.2) | collective-permute-done | bytes 262176 | tf_op jit(solution)/shard_map/ppermute | solution.py:39
  30.4 2.9 %collective-permute-start.6 = (bf16[256,1024]{1,0:T(8,128)(2,1)S(1)}, bf16[256,1024]{1,0:T(8,128)(2,1)S(1)}, u32[]{:S(2)}, u32[]{:S(2)}) collective-permute-start(bf16[256,1024]{1,0:T(8,128)(2,1)S(1)} %constant_dynamic-update-slice_fusion.high), channel_id=1, source_target_pairs={{0,384},{128,0},{256,128},{384,256},{1,25},{9,1},{17,9},{25,17},{2... | collective-permute-start | bytes 1572872 | tf_op jit(solution)/shard_map/ppermute | solution.py:39
  33.3 1.3 collective-permute-done
  34.6 3.1 %collective-permute-start.3 = (bf16[256,1024]{1,0:T(8,128)(2,1)S(1)}, bf16[256,1024]{1,0:T(8,128)(2,1)}, u32[]{:S(2)}, u32[]{:S(2)}) collective-permute-start(bf16[256,1024]{1,0:T(8,128)(2,1)S(1)} %pad_maximum_fusion.low), channel_id=1, source_target_pairs={{0,128},{128,256},{256,384},{384,0},{1,9},{9,17},{17,25},{25,1},{2... | collective-permute-start | bytes 1572872 | tf_op jit(solution)/shard_map/ppermute | solution.py:39
  37.7 2.7 %collective-permute-start.4 = (bf16[256,1024]{1,0:T(8,128)(2,1)S(1)}, bf16[256,1024]{1,0:T(8,128)(2,1)}, u32[]{:S(2)}, u32[]{:S(2)}) collective-permute-start(bf16[256,1024]{1,0:T(8,128)(2,1)S(1)} %constant_dynamic-update-slice_fusion.high), channel_id=1, source_target_pairs={{0,128},{128,256},{256,384},{384,0},{1,9},{9,17},{17,25},{25,1},{2... | collective-permute-start | bytes 1572872 | tf_op jit(solution)/shard_map/ppermute | solution.py:39
  40.4 3.1 %collective-permute-start.5 = (bf16[256,1024]{1,0:T(8,128)(2,1)S(1)}, bf16[256,1024]{1,0:T(8,128)(2,1)}, u32[]{:S(2)}, u32[]{:S(2)}) collective-permute-start(bf16[256,1024]{1,0:T(8,128)(2,1)S(1)} %pad_maximum_fusion.low), channel_id=1, source_target_pairs={{0,384},{128,0},{256,128},{384,256},{1,25},{9,1},{17,9},{25,17},{2... | collective-permute-start | bytes 1572872 | tf_op jit(solution)/shard_map/ppermute | solution.py:39
  43.5 2.8 %collective-permute-start.8 = (bf16[256,1024]{1,0:T(8,128)(2,1)S(1)}, bf16[256,1024]{1,0:T(8,128)(2,1)}, u32[]{:S(2)}, u32[]{:S(2)}) collective-permute-start(bf16[256,1024]{1,0:T(8,128)(2,1)S(1)} %collective-permute-done.6.down_on), channel_id=1, source_target_pairs={{0,384},{128,0},{256,128},{384,256},{1,25},{9,1},{17,9},{25,17},{2... | collective-permute-start | bytes 1572872 | tf_op jit(solution)/shard_map/ppermute | solution.py:39
  46.3 4.3 %collective-permute-start.7 = (bf16[256,1024]{1,0:T(8,128)(2,1)}, bf16[256,1024]{1,0:T(8,128)(2,1)}, u32[]{:S(2)}, u32[]{:S(2)}) collective-permute-start(bf16[256,1024]{1,0:T(8,128)(2,1)} %collective-permute-done.3.up_on), channel_id=1, source_target_pairs={{0,128},{128,256},{256,384},{384,0},{1,9},{9,17},{17,25},{25,1},{2... | collective-permute-start | bytes 1572872 | tf_op jit(solution)/shard_map/ppermute | solution.py:39
  50.9 7.8 %all-to-all-start.1 = ((bf16[64,2,16,256]{3,2,1,0:T(8,128)(2,1)}), bf16[64,2,16,256]{3,2,1,0:T(8,128)(2,1)S(1)}, u32[]{:S(2)}, u32[]{:S(2)}) async-start(bf16[64,2,16,256]{3,2,1,0:T(8,128)(2,1)} %bitcast.6), calls=%async_computation.1 | async-start | bytes 2097152 | tf_op jit(solution)/shard_map/all_to_all | solution.py:276
  58.8 1.7 %collective-permute-done.8.far_down = bf16[256,1024]{1,0:T(8,128)(2,1)} collective-permute-done((bf16[256,1024]{1,0:T(8,128)(2,1)S(1)}, bf16[256,1024]{1,0:T(8,128)(2,1)}, u32[]{:S(2)}, u32[]{:S(2)}) %collective-permute-start.8) | collective-permute-done | bytes 524320 | tf_op jit(solution)/shard_map/ppermute | solution.py:39
  60.5 2.5 %collective-permute-done.7.far_up = bf16[256,1024]{1,0:T(8,128)(2,1)} collective-permute-done((bf16[256,1024]{1,0:T(8,128)(2,1)}, bf16[256,1024]{1,0:T(8,128)(2,1)}, u32[]{:S(2)}, u32[]{:S(2)}) %collective-permute-start.7) | collective-permute-done | bytes 524320 | tf_op jit(solution)/shard_map/ppermute | solution.py:39
  63.1 1.0 copy-done.5
  64.1 3.2 %project.1 = (f32[1024,256]{1,0:T(8,128)S(1)}, f32[512,256]{1,0:T(8,128)S(1)}, f32[512,256]{1,0:T(8,128)S(1)}) custom-call(s32[64]{0:T(128)S(1)} %fusion.places, bf16[256,1024]{1,0:T(8,128)(2,1)S(1)} %bitcast.5, bf16[256,1024]{1,0:T(8,128)(2,1)S(1)} %pad_maximum_fusion.low, bf16[256,1024]{1,0:T(8,128)(2,1)S(1)} %constant_dynamic-update-slice_fusion.high, ...), custom_call_target="tpu_custom_call" | custom-call | flops 40000000000 | bytes 6000000 | tf_op jit(solution)/shard_map/project/pallas_call | solution.py:114
  67.3 1.9 %collective-permute-start.9 = (f32[1024,256]{1,0:T(8,128)S(1)}, f32[1024,256]{1,0:T(8,128)S(1)}, u32[]{:S(2)}, u32[]{:S(2)}) collective-permute-start(f32[1024,256]{1,0:T(8,128)S(1)} %get-tuple-element.19), channel_id=1, source_target_pairs={{0,1},{1,0},{2,3},{3,2},{4,5},{5,4},{6,7},{7,6},{8,9},{9,8},{10,11... | collective-permute-start | bytes 3145736 | tf_op jit(solution)/shard_map/ppermute | solution.py:54
  69.2 2.6 %collective-permute-done.9 = f32[1024,256]{1,0:T(8,128)S(1)} collective-permute-done((f32[1024,256]{1,0:T(8,128)S(1)}, f32[1024,256]{1,0:T(8,128)S(1)}, u32[]{:S(2)}, u32[]{:S(2)}) %collective-permute-start.9) | collective-permute-done | bytes 1048608 | tf_op jit(solution)/shard_map/ppermute | solution.py:54
  72.8 9.2 %collective-permute-start.11 = (f32[256,256]{1,0:T(8,128)S(1)}, f32[256,256]{1,0:T(8,128)}, u32[]{:S(2)}, u32[]{:S(2)}) collective-permute-start(f32[256,256]{1,0:T(8,128)S(1)} %get-tuple-element.32), channel_id=1, source_target_pairs={{0,2},{1,7},{2,0},{3,5},{4,6},{5,3},{6,4},{7,1},{8,10},{9,15},{10,... | collective-permute-start | bytes 786440 | tf_op jit(solution)/shard_map/ppermute | solution.py:50
  82.0 1.9 %collective-permute-start.10 = (f32[256,256]{1,0:T(8,128)}, f32[256,256]{1,0:T(8,128)}, u32[]{:S(2)}, u32[]{:S(2)}) collective-permute-start(f32[256,256]{1,0:T(8,128)} %get-tuple-element.33), channel_id=1, source_target_pairs={{0,2},{1,7},{2,0},{3,5},{4,6},{5,3},{6,4},{7,1},{8,10},{9,15},{10,... | collective-permute-start | bytes 786440 | tf_op jit(solution)/shard_map/ppermute | solution.py:50
  83.9 9.8 %collective-permute-done.11 = f32[256,256]{1,0:T(8,128)} collective-permute-done((f32[256,256]{1,0:T(8,128)S(1)}, f32[256,256]{1,0:T(8,128)}, u32[]{:S(2)}, u32[]{:S(2)}) %collective-permute-start.11) | collective-permute-done | bytes 262176 | tf_op jit(solution)/shard_map/ppermute | solution.py:50
  93.7 6.1 %all-to-all-done.1 = bf16[64,2,16,256]{3,2,1,0:T(8,128)(2,1)S(1)} async-done(((bf16[64,2,16,256]{3,2,1,0:T(8,128)(2,1)}), bf16[64,2,16,256]{3,2,1,0:T(8,128)(2,1)S(1)}, u32[]{:S(2)}, u32[]{:S(2)}) %all-to-all-start.1) | async-done | bytes 1048608 | tf_op jit(solution)/shard_map/all_to_all | solution.py:276
  99.8 1.8 %add.149 = f32[256,256]{1,0:T(8,128)} add(f32[256,256]{1,0:T(8,128)} %get-tuple-element.22, f32[256,256]{1,0:T(8,128)} %collective-permute-done.11) | non-fusion elementwise | flops 65536 | bytes 786432 | tf_op jit(solution)/shard_map/add | solution.py:137
  101.6 9.9 %collective-permute-start.12 = (f32[256,256]{1,0:T(8,128)}, f32[256,256]{1,0:T(8,128)}, u32[]{:S(2)}, u32[]{:S(2)}) collective-permute-start(f32[256,256]{1,0:T(8,128)} %add.149), channel_id=1, source_target_pairs={{0,6},{1,3},{2,4},{3,1},{4,2},{5,7},{6,0},{7,5},{8,14},{9,11},{10,... | collective-permute-start | bytes 786440 | tf_op jit(solution)/shard_map/ppermute | solution.py:50
  111.5 1.0 add.147
  112.5 2.8 %past.1 = (f32[32,64,128]{2,1,0:T(8,128)S(1)}, bf16[32,64,128]{2,1,0:T(8,128)(2,1)S(1)}, bf16[32,128,128]{2,1,0:T(8,128)(2,1)S(1)}) custom-call(s32[32,6]{1,0:T(8,128)S(1)} %copy.15.table, s32[32]{0:T(128)S(1)} %copy-done.2, bf16[8,32,1024]{2,1,0:T(8,128)(2,1)S(1)} %copy-done.1, bf16[192,16,256]{2,1,0:T(8,128)(2,1)S(1)} %copy-done, ...), custom_call_target="tpu_custom_call" | custom-call | flops 70000000 | bytes 8000000 | tf_op jit(solution)/shard_map/past/pallas_call | solution.py:180
  115.3 8.9 %collective-permute-done.12 = f32[256,256]{1,0:T(8,128)} collective-permute-done((f32[256,256]{1,0:T(8,128)}, f32[256,256]{1,0:T(8,128)}, u32[]{:S(2)}, u32[]{:S(2)}) %collective-permute-start.12) | collective-permute-done | bytes 262176 | tf_op jit(solution)/shard_map/ppermute | solution.py:50
  125.2 2.8 %finish.1 = (bf16[8,32,256]{2,1,0:T(8,128)(2,1)}, bf16[8,32,1024]{2,1,0:T(8,128)(2,1)}) custom-call(f32[256,256]{1,0:T(8,128)S(1)} %add.150.refs_0_, f32[32,64,128]{2,1,0:T(8,128)S(1)} %get-tuple-element.29.refs_1_, bf16[32,64,128]{2,1,0:T(8,128)(2,1)S(1)} %get-tuple-element.30.refs_2_, bf16[32,128,128]{2,1,0:T(8,128)(2,1)S(1)} %get-tuple-element.31.refs_3_), custom_call_target="tpu_custom_call" | custom-call | flops 140000000 | bytes 4000000 | tf_op jit(solution)/shard_map/finish/pallas_call | solution.py:246
  (33 shorter events, 3.2 us)
Async XLA Ops:
  2.2 14.8 %all-to-all-start = ((bf16[4,32,1024]{2,1,0:T(8,128)(2,1)}), bf16[4,32,1024]{2,1,0:T(8,128)(2,1)S(1)}, u32[]{:S(2)}, u32[]{:S(2)}) async-start(bf16[4,32,1024]{2,1,0:T(8,128)(2,1)} %broadcast_in_dim.43), calls=%async_computation | async-start | bytes 524288 | tf_op jit(solution)/shard_map/all_to_all | solution.py:58
  12.1 38.6 %copy-start.7 = (s32[64]{0:T(128)S(1)}, s32[64]{0:T(128)}, u32[]{:S(2)}) copy-start(s32[64]{0:T(128)} %param.10) | copy-start | bytes 772
  17.0 11.0 %collective-permute-start.1 = (bf16[128,1024]{1,0:T(8,128)(2,1)S(1)}, bf16[128,1024]{1,0:T(8,128)(2,1)S(1)}, u32[]{:S(2)}, u32[]{:S(2)}) collective-permute-start(bf16[128,1024]{1,0:T(8,128)(2,1)S(1)} %bitcast.7), channel_id=1, source_target_pairs={{0,16},{8,24},{16,0},{24,8},{1,257},{129,385},{257,1},{385,129},{2... | collective-permute-start | bytes 786440 | tf_op jit(solution)/shard_map/ppermute | solution.py:39
  22.1 8.3 %collective-permute-start.2 = (bf16[128,1024]{1,0:T(8,128)(2,1)S(1)}, bf16[128,1024]{1,0:T(8,128)(2,1)S(1)}, u32[]{:S(2)}, u32[]{:S(2)}) collective-permute-start(bf16[128,1024]{1,0:T(8,128)(2,1)S(1)} %bitcast.8), channel_id=1, source_target_pairs={{0,24},{8,0},{16,8},{24,16},{1,385},{129,1},{257,129},{385,257},{2... | collective-permute-start | bytes 786440 | tf_op jit(solution)/shard_map/ppermute | solution.py:39
  25.1 9.5 %collective-permute-start = (bf16[128,1024]{1,0:T(8,128)(2,1)S(1)}, bf16[128,1024]{1,0:T(8,128)(2,1)S(1)}, u32[]{:S(2)}, u32[]{:S(2)}) collective-permute-start(bf16[128,1024]{1,0:T(8,128)(2,1)S(1)} %bitcast.9), channel_id=1, source_target_pairs={{0,8},{8,16},{16,24},{24,0},{1,129},{129,257},{257,385},{385,1},{2... | collective-permute-start | bytes 786440 | tf_op jit(solution)/shard_map/ppermute | solution.py:39
  30.4 32.7 %copy-start.3 = (bf16[8,32,1024]{2,1,0:T(8,128)(2,1)S(1)}, bf16[8,32,1024]{2,1,0:T(8,128)(2,1)}, u32[]{:S(2)}) copy-start(bf16[8,32,1024]{2,1,0:T(8,128)(2,1)} %param.8) | copy-start | bytes 1572868
  30.4 13.1 %collective-permute-start.6 = (bf16[256,1024]{1,0:T(8,128)(2,1)S(1)}, bf16[256,1024]{1,0:T(8,128)(2,1)S(1)}, u32[]{:S(2)}, u32[]{:S(2)}) collective-permute-start(bf16[256,1024]{1,0:T(8,128)(2,1)S(1)} %constant_dynamic-update-slice_fusion.high), channel_id=1, source_target_pairs={{0,384},{128,0},{256,128},{384,256},{1,25},{9,1},{17,9},{25,17},{2... | collective-permute-start | bytes 1572872 | tf_op jit(solution)/shard_map/ppermute | solution.py:39
  34.6 11.7 %collective-permute-start.3 = (bf16[256,1024]{1,0:T(8,128)(2,1)S(1)}, bf16[256,1024]{1,0:T(8,128)(2,1)}, u32[]{:S(2)}, u32[]{:S(2)}) collective-permute-start(bf16[256,1024]{1,0:T(8,128)(2,1)S(1)} %pad_maximum_fusion.low), channel_id=1, source_target_pairs={{0,128},{128,256},{256,384},{384,0},{1,9},{9,17},{17,25},{25,1},{2... | collective-permute-start | bytes 1572872 | tf_op jit(solution)/shard_map/ppermute | solution.py:39
  37.7 21.1 %collective-permute-start.4 = (bf16[256,1024]{1,0:T(8,128)(2,1)S(1)}, bf16[256,1024]{1,0:T(8,128)(2,1)}, u32[]{:S(2)}, u32[]{:S(2)}) collective-permute-start(bf16[256,1024]{1,0:T(8,128)(2,1)S(1)} %constant_dynamic-update-slice_fusion.high), channel_id=1, source_target_pairs={{0,128},{128,256},{256,384},{384,0},{1,9},{9,17},{17,25},{25,1},{2... | collective-permute-start | bytes 1572872 | tf_op jit(solution)/shard_map/ppermute | solution.py:39
  40.4 18.4 %collective-permute-start.5 = (bf16[256,1024]{1,0:T(8,128)(2,1)S(1)}, bf16[256,1024]{1,0:T(8,128)(2,1)}, u32[]{:S(2)}, u32[]{:S(2)}) collective-permute-start(bf16[256,1024]{1,0:T(8,128)(2,1)S(1)} %pad_maximum_fusion.low), channel_id=1, source_target_pairs={{0,384},{128,0},{256,128},{384,256},{1,25},{9,1},{17,9},{25,17},{2... | collective-permute-start | bytes 1572872 | tf_op jit(solution)/shard_map/ppermute | solution.py:39
  43.5 19.5 %copy-start.4 = (bf16[256,1024]{1,0:T(8,128)(2,1)}, bf16[256,1024]{1,0:T(8,128)(2,1)S(1)}, u32[]{:S(2)}) copy-start(bf16[256,1024]{1,0:T(8,128)(2,1)S(1)} %collective-permute-done.6.down_on) | copy-start | bytes 1572868
  43.5 17.0 %collective-permute-start.8 = (bf16[256,1024]{1,0:T(8,128)(2,1)S(1)}, bf16[256,1024]{1,0:T(8,128)(2,1)}, u32[]{:S(2)}, u32[]{:S(2)}) collective-permute-start(bf16[256,1024]{1,0:T(8,128)(2,1)S(1)} %collective-permute-done.6.down_on), channel_id=1, source_target_pairs={{0,384},{128,0},{256,128},{384,256},{1,25},{9,1},{17,9},{25,17},{2... | collective-permute-start | bytes 1572872 | tf_op jit(solution)/shard_map/ppermute | solution.py:39
  46.3 16.7 %collective-permute-start.7 = (bf16[256,1024]{1,0:T(8,128)(2,1)}, bf16[256,1024]{1,0:T(8,128)(2,1)}, u32[]{:S(2)}, u32[]{:S(2)}) collective-permute-start(bf16[256,1024]{1,0:T(8,128)(2,1)} %collective-permute-done.3.up_on), channel_id=1, source_target_pairs={{0,128},{128,256},{256,384},{384,0},{1,9},{9,17},{17,25},{25,1},{2... | collective-permute-start | bytes 1572872 | tf_op jit(solution)/shard_map/ppermute | solution.py:39
  50.9 48.9 %all-to-all-start.1 = ((bf16[64,2,16,256]{3,2,1,0:T(8,128)(2,1)}), bf16[64,2,16,256]{3,2,1,0:T(8,128)(2,1)S(1)}, u32[]{:S(2)}, u32[]{:S(2)}) async-start(bf16[64,2,16,256]{3,2,1,0:T(8,128)(2,1)} %bitcast.6), calls=%async_computation.1 | async-start | bytes 2097152 | tf_op jit(solution)/shard_map/all_to_all | solution.py:276
  63.1 1.0 copy-start.5
  67.3 4.6 %collective-permute-start.9 = (f32[1024,256]{1,0:T(8,128)S(1)}, f32[1024,256]{1,0:T(8,128)S(1)}, u32[]{:S(2)}, u32[]{:S(2)}) collective-permute-start(f32[1024,256]{1,0:T(8,128)S(1)} %get-tuple-element.19), channel_id=1, source_target_pairs={{0,1},{1,0},{2,3},{3,2},{4,5},{5,4},{6,7},{7,6},{8,9},{9,8},{10,11... | collective-permute-start | bytes 3145736 | tf_op jit(solution)/shard_map/ppermute | solution.py:54
  71.8 39.6 %copy-start.6 = (s32[32,6]{0,1:T(8,128)S(1)}, s32[32,6]{0,1:T(8,128)}, u32[]{:S(2)}) copy-start(s32[32,6]{0,1:T(8,128)} %param.13) | copy-start | bytes 2308
  71.8 40.7 %copy-start.1 = (bf16[8,32,1024]{2,1,0:T(8,128)(2,1)S(1)}, bf16[8,32,1024]{2,1,0:T(8,128)(2,1)}, u32[]{:S(2)}) copy-start(bf16[8,32,1024]{2,1,0:T(8,128)(2,1)} %queries) | copy-start | bytes 1572868
  72.8 39.8 %copy-start = (bf16[192,16,256]{2,1,0:T(8,128)(2,1)S(1)}, bf16[192,16,256]{2,1,0:T(8,128)(2,1)}, u32[]{:S(2)}) copy-start(bf16[192,16,256]{2,1,0:T(8,128)(2,1)} %pool.1) | copy-start | bytes 4718596
  72.8 39.8 %copy-start.2 = (s32[32]{0:T(128)S(1)}, s32[32]{0:T(128)}, u32[]{:S(2)}) copy-start(s32[32]{0:T(128)} %lengths.1) | copy-start | bytes 388
  72.8 20.9 %collective-permute-start.11 = (f32[256,256]{1,0:T(8,128)S(1)}, f32[256,256]{1,0:T(8,128)}, u32[]{:S(2)}, u32[]{:S(2)}) collective-permute-start(f32[256,256]{1,0:T(8,128)S(1)} %get-tuple-element.32), channel_id=1, source_target_pairs={{0,2},{1,7},{2,0},{3,5},{4,6},{5,3},{6,4},{7,1},{8,10},{9,15},{10,... | collective-permute-start | bytes 786440 | tf_op jit(solution)/shard_map/ppermute | solution.py:50
  82.0 29.5 %collective-permute-start.10 = (f32[256,256]{1,0:T(8,128)}, f32[256,256]{1,0:T(8,128)}, u32[]{:S(2)}, u32[]{:S(2)}) collective-permute-start(f32[256,256]{1,0:T(8,128)} %get-tuple-element.33), channel_id=1, source_target_pairs={{0,2},{1,7},{2,0},{3,5},{4,6},{5,3},{6,4},{7,1},{8,10},{9,15},{10,... | collective-permute-start | bytes 786440 | tf_op jit(solution)/shard_map/ppermute | solution.py:50
  101.6 22.7 %collective-permute-start.12 = (f32[256,256]{1,0:T(8,128)}, f32[256,256]{1,0:T(8,128)}, u32[]{:S(2)}, u32[]{:S(2)}) collective-permute-start(f32[256,256]{1,0:T(8,128)} %add.149), channel_id=1, source_target_pairs={{0,6},{1,3},{2,4},{3,1},{4,2},{5,7},{6,0},{7,5},{8,14},{9,11},{10,... | collective-permute-start | bytes 786440 | tf_op jit(solution)/shard_map/ppermute | solution.py:50

commit v6 on v4

--- a/solution.py
+++ b/solution.py
@@ -274,9 +274,7 @@
     steps_count, _, feature_part = hidden.shape
     page_size, kv_width = pool.shape[1:]
     c, q = lax.axis_index("c"), lax.axis_index("zh")
-    outgoing = jnp.take(pool, send_pages.reshape(-1), axis=0, mode="clip").reshape(
-        64, -1, page_size, kv_width
-    )
+    outgoing = jnp.take(pool, send_pages.reshape(-1), axis=0, mode="clip").reshape(-1, kv_width)
     outgoing, pieces = gather_weight(kv_weight, outgoing)
     arrived = lax.all_to_all(outgoing, REPLICA, split_axis=0, concat_axis=0, tiled=True)
     places = block_places(owner, c, q)

time: 112 us -> 112 us (level)
  no operation moved by 1% of the time
where the time goes in v6:
time: 112 us; the launch traced here: 111 us
  starting transfers between devices  65.1 us (58%)
  waiting for transfers between devices  27.6 us (25%)
  Pallas kernels  8.88 us (8%)
  local copies, waits for them, and re-layouts  5.67 us (5%)
  other arithmetic  3.14 us (3%)
    ppermute x9, starting transfers between devices, shift(): return lax.ppermute(value, AXES, pairs)  31.4 us
    ppermute x3, starting transfers between devices, z_exchange(): return lax.ppermute((value * SCALE).astype(jnp.float16), TENSOR, pairs)  18.6 us
    ppermute x9, waiting for transfers between devices, shift(): return lax.ppermute(value, AXES, pairs)  10.2 us
    all_to_all x1, starting transfers between devices, on_device(): lax.all_to_all(outgoing, REPLICA, split_axis=0, concat_axis=0, tiled=True)  7.28 us
    all_to_all x1, waiting for transfers between devices, on_device(): lax.all_to_all(outgoing, REPLICA, split_axis=0, concat_axis=0, tiled=True)  6.2 us
    all_to_all x1, starting transfers between devices, gather_weight(): lax.all_to_all(jnp.broadcast_to(held[None], (SIDE,) + held.shape), 'zl',...  5.89 us
    all_to_all x1, waiting for transfers between devices, gather_weight(): lax.all_to_all(jnp.broadcast_to(held[None], (SIDE,) + held.shape), 'zl',...  4.94 us
    ppermute x3, waiting for transfers between devices, z_exchange(): return lax.ppermute((value * SCALE).astype(jnp.float16), TENSOR, pairs)  3.65 us
  transfers between devices with their start and end apart: 15, of which 8 were waited for; matrix products, arithmetic and copies ran while one was open for 6% of the time, Pallas kernels for 6%

profile of v6, /device:TPU:128, one launch (start us, length us, event | category | flops | bytes accessed | tf_op | source)
XLA Modules:
  0.0 111.3 jit_solution(11809502421158820492)
XLA Ops:
  0.6 1.6 %broadcast_in_dim.43 = bf16[4,32,1024]{2,1,0:T(8,128)(2,1)} broadcast(bf16[32,1024]{1,0:T(8,128)(2,1)} %param.9), dimensions={1,2} | broadcast | bytes 327680 | tf_op jit(solution)/shard_map/broadcast_in_dim | solution.py:64
  2.2 5.9 %all-to-all-start = ((bf16[4,32,1024]{2,1,0:T(8,128)(2,1)}), bf16[4,32,1024]{2,1,0:T(8,128)(2,1)S(1)}, u32[]{:S(2)}, u32[]{:S(2)}) async-start(bf16[4,32,1024]{2,1,0:T(8,128)(2,1)} %broadcast_in_dim.43), calls=%async_computation | async-start | bytes 524288 | tf_op jit(solution)/shard_map/all_to_all | solution.py:63
  8.1 0.8 copy.14
  9.0 3.0 %gather_fusion = bf16[128,16,256]{2,1,0:T(8,128)(2,1)} fusion(bf16[192,16,256]{2,1,0:T(8,128)(2,1)} %pool.1, s32[1024]{0:T(1024)S(1)} %pad_clamp_fusion), kind=kCustom, calls=%fused_computation | custom fusion | bytes 2097664 | tf_op jit(solution)/shard_map/jit(_take)/gather | solution.py:277
  12.1 4.9 %all-to-all-done = bf16[4,32,1024]{2,1,0:T(8,128)(2,1)S(1)} async-done(((bf16[4,32,1024]{2,1,0:T(8,128)(2,1)}), bf16[4,32,1024]{2,1,0:T(8,128)(2,1)S(1)}, u32[]{:S(2)}, u32[]{:S(2)}) %all-to-all-start) | async-done | bytes 262176 | tf_op jit(solution)/shard_map/all_to_all | solution.py:63
  17.0 5.1 %collective-permute-start.1 = (bf16[128,1024]{1,0:T(8,128)(2,1)S(1)}, bf16[128,1024]{1,0:T(8,128)(2,1)S(1)}, u32[]{:S(2)}, u32[]{:S(2)}) collective-permute-start(bf16[128,1024]{1,0:T(8,128)(2,1)S(1)} %bitcast.9), channel_id=1, source_target_pairs={{0,16},{8,24},{16,0},{24,8},{1,257},{129,385},{257,1},{385,129},{2... | collective-permute-start | bytes 786440 | tf_op jit(solution)/shard_map/ppermute | solution.py:40
  22.1 3.0 %collective-permute-start.2 = (bf16[128,1024]{1,0:T(8,128)(2,1)S(1)}, bf16[128,1024]{1,0:T(8,128)(2,1)S(1)}, u32[]{:S(2)}, u32[]{:S(2)}) collective-permute-start(bf16[128,1024]{1,0:T(8,128)(2,1)S(1)} %bitcast.10), channel_id=1, source_target_pairs={{0,24},{8,0},{16,8},{24,16},{1,385},{129,1},{257,129},{385,257},{2... | collective-permute-start | bytes 786440 | tf_op jit(solution)/shard_map/ppermute | solution.py:40
  25.1 2.9 %collective-permute-start = (bf16[128,1024]{1,0:T(8,128)(2,1)S(1)}, bf16[128,1024]{1,0:T(8,128)(2,1)S(1)}, u32[]{:S(2)}, u32[]{:S(2)}) collective-permute-start(bf16[128,1024]{1,0:T(8,128)(2,1)S(1)} %bitcast.11), channel_id=1, source_target_pairs={{0,8},{8,16},{16,24},{24,0},{1,129},{129,257},{257,385},{385,1},{2... | collective-permute-start | bytes 786440 | tf_op jit(solution)/shard_map/ppermute | solution.py:40
  28.0 2.4 %collective-permute-done.2 = bf16[128,1024]{1,0:T(8,128)(2,1)S(1)} collective-permute-done((bf16[128,1024]{1,0:T(8,128)(2,1)S(1)}, bf16[128,1024]{1,0:T(8,128)(2,1)S(1)}, u32[]{:S(2)}, u32[]{:S(2)}) %collective-permute-start.2) | collective-permute-done | bytes 262176 | tf_op jit(solution)/shard_map/ppermute | solution.py:40
  30.4 4.8 %collective-permute-start.6 = (bf16[256,1024]{1,0:T(8,128)(2,1)S(1)}, bf16[256,1024]{1,0:T(8,128)(2,1)}, u32[]{:S(2)}, u32[]{:S(2)}) collective-permute-start(bf16[256,1024]{1,0:T(8,128)(2,1)S(1)} %constant_dynamic-update-slice_fusion.high), channel_id=1, source_target_pairs={{0,384},{128,0},{256,128},{384,256},{1,25},{9,1},{17,9},{25,17},{2... | collective-permute-start | bytes 1572872 | tf_op jit(solution)/shard_map/ppermute | solution.py:40
  35.3 2.7 %collective-permute-start.3 = (bf16[256,1024]{1,0:T(8,128)(2,1)S(1)}, bf16[256,1024]{1,0:T(8,128)(2,1)}, u32[]{:S(2)}, u32[]{:S(2)}) collective-permute-start(bf16[256,1024]{1,0:T(8,128)(2,1)S(1)} %pad_maximum_fusion.low), channel_id=1, source_target_pairs={{0,128},{128,256},{256,384},{384,0},{1,9},{9,17},{17,25},{25,1},{2... | collective-permute-start | bytes 1572872 | tf_op jit(solution)/shard_map/ppermute | solution.py:40
  38.0 3.4 %collective-permute-start.4 = (bf16[256,1024]{1,0:T(8,128)(2,1)S(1)}, bf16[256,1024]{1,0:T(8,128)(2,1)}, u32[]{:S(2)}, u32[]{:S(2)}) collective-permute-start(bf16[256,1024]{1,0:T(8,128)(2,1)S(1)} %constant_dynamic-update-slice_fusion.high), channel_id=1, source_target_pairs={{0,128},{128,256},{256,384},{384,0},{1,9},{9,17},{17,25},{25,1},{2... | collective-permute-start | bytes 1572872 | tf_op jit(solution)/shard_map/ppermute | solution.py:40
  41.4 3.7 %collective-permute-start.5 = (bf16[256,1024]{1,0:T(8,128)(2,1)S(1)}, bf16[256,1024]{1,0:T(8,128)(2,1)}, u32[]{:S(2)}, u32[]{:S(2)}) collective-permute-start(bf16[256,1024]{1,0:T(8,128)(2,1)S(1)} %pad_maximum_fusion.low), channel_id=1, source_target_pairs={{0,384},{128,0},{256,128},{384,256},{1,25},{9,1},{17,9},{25,17},{2... | collective-permute-start | bytes 1572872 | tf_op jit(solution)/shard_map/ppermute | solution.py:40
  45.1 3.1 %collective-permute-start.8 = (bf16[256,1024]{1,0:T(8,128)(2,1)}, bf16[256,1024]{1,0:T(8,128)(2,1)}, u32[]{:S(2)}, u32[]{:S(2)}) collective-permute-start(bf16[256,1024]{1,0:T(8,128)(2,1)} %collective-permute-done.6.down_on), channel_id=1, source_target_pairs={{0,384},{128,0},{256,128},{384,256},{1,25},{9,1},{17,9},{25,17},{2... | collective-permute-start | bytes 1572872 | tf_op jit(solution)/shard_map/ppermute | solution.py:40
  48.2 2.7 %collective-permute-start.7 = (bf16[256,1024]{1,0:T(8,128)(2,1)}, bf16[256,1024]{1,0:T(8,128)(2,1)}, u32[]{:S(2)}, u32[]{:S(2)}) collective-permute-start(bf16[256,1024]{1,0:T(8,128)(2,1)} %collective-permute-done.3.up_on), channel_id=1, source_target_pairs={{0,128},{128,256},{256,384},{384,0},{1,9},{9,17},{17,25},{25,1},{2... | collective-permute-start | bytes 1572872 | tf_op jit(solution)/shard_map/ppermute | solution.py:40
  51.2 7.3 %all-to-all-start.1 = ((bf16[64,32,256]{2,1,0:T(8,128)(2,1)}), bf16[64,32,256]{2,1,0:T(8,128)(2,1)S(1)}, u32[]{:S(2)}, u32[]{:S(2)}) async-start(bf16[64,32,256]{2,1,0:T(8,128)(2,1)} %bitcast.8), calls=%async_computation.1 | async-start | bytes 2097152 | tf_op jit(solution)/shard_map/all_to_all | solution.py:279
  58.5 1.7 %collective-permute-done.8.far_down = bf16[256,1024]{1,0:T(8,128)(2,1)} collective-permute-done((bf16[256,1024]{1,0:T(8,128)(2,1)}, bf16[256,1024]{1,0:T(8,128)(2,1)}, u32[]{:S(2)}, u32[]{:S(2)}) %collective-permute-start.8) | collective-permute-done | bytes 524320 | tf_op jit(solution)/shard_map/ppermute | solution.py:40
  60.2 6.1 %collective-permute-done.7.far_up = bf16[256,1024]{1,0:T(8,128)(2,1)} collective-permute-done((bf16[256,1024]{1,0:T(8,128)(2,1)}, bf16[256,1024]{1,0:T(8,128)(2,1)}, u32[]{:S(2)}, u32[]{:S(2)}) %collective-permute-start.7) | collective-permute-done | bytes 524320 | tf_op jit(solution)/shard_map/ppermute | solution.py:40
  66.3 3.3 %project.1 = (f32[1024,256]{1,0:T(8,128)S(1)}, f32[512,256]{1,0:T(8,128)S(1)}, f32[512,256]{1,0:T(8,128)S(1)}) custom-call(s32[64]{0:T(128)S(1)} %fusion.4.places, bf16[256,1024]{1,0:T(8,128)(2,1)S(1)} %bitcast.7, bf16[256,1024]{1,0:T(8,128)(2,1)S(1)} %pad_maximum_fusion.low, bf16[256,1024]{1,0:T(8,128)(2,1)S(1)} %constant_dynamic-update-slice_fusion.high, ...), custom_call_target="tpu_custom_call" | custom-call | flops 40000000000 | bytes 6000000 | tf_op jit(solution)/shard_map/project/pallas_call | solution.py:119
  69.7 1.9 %collective-permute-start.9 = (f32[1024,256]{1,0:T(8,128)S(1)}, f32[1024,256]{1,0:T(8,128)S(1)}, u32[]{:S(2)}, u32[]{:S(2)}) collective-permute-start(f32[1024,256]{1,0:T(8,128)S(1)} %get-tuple-element.19), channel_id=1, source_target_pairs={{0,1},{1,0},{2,3},{3,2},{4,5},{5,4},{6,7},{7,6},{8,9},{9,8},{10,11... | collective-permute-start | bytes 3145736 | tf_op jit(solution)/shard_map/ppermute | solution.py:59
  71.6 2.6 %collective-permute-done.9 = f32[1024,256]{1,0:T(8,128)S(1)} collective-permute-done((f32[1024,256]{1,0:T(8,128)S(1)}, f32[1024,256]{1,0:T(8,128)S(1)}, u32[]{:S(2)}, u32[]{:S(2)}) %collective-permute-start.9) | collective-permute-done | bytes 1048608 | tf_op jit(solution)/shard_map/ppermute | solution.py:59
  74.2 0.9 fusion.1
  75.1 1.9 %collective-permute-start.11 = (f16[256,256]{1,0:T(8,128)(2,1)}, f16[256,256]{1,0:T(8,128)(2,1)}, u32[]{:S(2)}, u32[]{:S(2)}) collective-permute-start(f16[256,256]{1,0:T(8,128)(2,1)} %get-tuple-element.32), channel_id=1, source_target_pairs={{0,2},{1,7},{2,0},{3,5},{4,6},{5,3},{6,4},{7,1},{8,10},{9,15},{10,... | collective-permute-start | bytes 393224 | tf_op jit(solution)/shard_map/ppermute | solution.py:51
  77.1 7.8 %collective-permute-start.10 = (f16[256,256]{1,0:T(8,128)(2,1)}, f16[256,256]{1,0:T(8,128)(2,1)}, u32[]{:S(2)}, u32[]{:S(2)}) collective-permute-start(f16[256,256]{1,0:T(8,128)(2,1)} %get-tuple-element.33), channel_id=1, source_target_pairs={{0,2},{1,7},{2,0},{3,5},{4,6},{5,3},{6,4},{7,1},{8,10},{9,15},{10,... | collective-permute-start | bytes 393224 | tf_op jit(solution)/shard_map/ppermute | solution.py:51
  84.9 1.8 %collective-permute-done.11 = f16[256,256]{1,0:T(8,128)(2,1)} collective-permute-done((f16[256,256]{1,0:T(8,128)(2,1)}, f16[256,256]{1,0:T(8,128)(2,1)}, u32[]{:S(2)}, u32[]{:S(2)}) %collective-permute-start.11) | collective-permute-done | bytes 131104 | tf_op jit(solution)/shard_map/ppermute | solution.py:51
  86.7 6.2 %all-to-all-done.1 = bf16[64,32,256]{2,1,0:T(8,128)(2,1)S(1)} async-done(((bf16[64,32,256]{2,1,0:T(8,128)(2,1)}), bf16[64,32,256]{2,1,0:T(8,128)(2,1)S(1)}, u32[]{:S(2)}, u32[]{:S(2)}) %all-to-all-start.1) | async-done | bytes 1048608 | tf_op jit(solution)/shard_map/all_to_all | solution.py:279
  92.9 1.0 multiply_convert_fusion
  94.0 8.9 %collective-permute-start.12 = (f16[256,256]{1,0:T(8,128)(2,1)S(1)}, f16[256,256]{1,0:T(8,128)(2,1)S(1)}, u32[]{:S(2)}, u32[]{:S(2)}) collective-permute-start(f16[256,256]{1,0:T(8,128)(2,1)S(1)} %multiply_convert_fusion), channel_id=1, source_target_pairs={{0,6},{1,3},{2,4},{3,1},{4,2},{5,7},{6,0},{7,5},{8,14},{9,11},{10,... | collective-permute-start | bytes 393224 | tf_op jit(solution)/shard_map/ppermute | solution.py:51
  102.9 0.9 multiply_add_fusion.1
  103.9 2.8 %past.1 = (f32[32,64,128]{2,1,0:T(8,128)S(1)}, bf16[32,64,128]{2,1,0:T(8,128)(2,1)S(1)}, bf16[32,128,128]{2,1,0:T(8,128)(2,1)S(1)}) custom-call(s32[32,6]{1,0:T(8,128)S(1)} %copy.15.table, s32[32]{0:T(128)S(1)} %copy-done.2, bf16[8,32,1024]{2,1,0:T(8,128)(2,1)S(1)} %copy-done.1, bf16[192,16,256]{2,1,0:T(8,128)(2,1)S(1)} %copy-done, ...), custom_call_target="tpu_custom_call" | custom-call | flops 70000000 | bytes 8000000 | tf_op jit(solution)/shard_map/past/pallas_call | solution.py:185
  106.7 1.9 %collective-permute-done.12 = f16[256,256]{1,0:T(8,128)(2,1)S(1)} collective-permute-done((f16[256,256]{1,0:T(8,128)(2,1)S(1)}, f16[256,256]{1,0:T(8,128)(2,1)S(1)}, u32[]{:S(2)}, u32[]{:S(2)}) %collective-permute-start.12) | collective-permute-done | bytes 131104 | tf_op jit(solution)/shard_map/ppermute | solution.py:51
  108.6 2.8 %finish.1 = (bf16[8,32,256]{2,1,0:T(8,128)(2,1)}, bf16[8,32,1024]{2,1,0:T(8,128)(2,1)}) custom-call(f32[256,256]{1,0:T(8,128)S(1)} %multiply_add_fusion.refs_0_, f32[32,64,128]{2,1,0:T(8,128)S(1)} %get-tuple-element.29.refs_1_, bf16[32,64,128]{2,1,0:T(8,128)(2,1)S(1)} %get-tuple-element.30.refs_2_, bf16[32,128,128]{2,1,0:T(8,128)(2,1)S(1)} %get-tuple-element.31.refs_3_), custom_call_target="tpu_custom_call" | custom-call | flops 140000000 | bytes 4000000 | tf_op jit(solution)/shard_map/finish/pallas_call | solution.py:251
  (29 shorter events, 0.6 us)
Async XLA Ops:
  2.2 14.8 %all-to-all-start = ((bf16[4,32,1024]{2,1,0:T(8,128)(2,1)}), bf16[4,32,1024]{2,1,0:T(8,128)(2,1)S(1)}, u32[]{:S(2)}, u32[]{:S(2)}) async-start(bf16[4,32,1024]{2,1,0:T(8,128)(2,1)} %broadcast_in_dim.43), calls=%async_computation | async-start | bytes 524288 | tf_op jit(solution)/shard_map/all_to_all | solution.py:63
  12.1 38.9 %copy-start.5 = (s32[64]{0:T(128)S(1)}, s32[64]{0:T(128)}, u32[]{:S(2)}) copy-start(s32[64]{0:T(128)} %param.10) | copy-start | bytes 772
  17.0 11.0 %collective-permute-start.1 = (bf16[128,1024]{1,0:T(8,128)(2,1)S(1)}, bf16[128,1024]{1,0:T(8,128)(2,1)S(1)}, u32[]{:S(2)}, u32[]{:S(2)}) collective-permute-start(bf16[128,1024]{1,0:T(8,128)(2,1)S(1)} %bitcast.9), channel_id=1, source_target_pairs={{0,16},{8,24},{16,0},{24,8},{1,257},{129,385},{257,1},{385,129},{2... | collective-permute-start | bytes 786440 | tf_op jit(solution)/shard_map/ppermute | solution.py:40
  22.1 8.3 %collective-permute-start.2 = (bf16[128,1024]{1,0:T(8,128)(2,1)S(1)}, bf16[128,1024]{1,0:T(8,128)(2,1)S(1)}, u32[]{:S(2)}, u32[]{:S(2)}) collective-permute-start(bf16[128,1024]{1,0:T(8,128)(2,1)S(1)} %bitcast.10), channel_id=1, source_target_pairs={{0,24},{8,0},{16,8},{24,16},{1,385},{129,1},{257,129},{385,257},{2... | collective-permute-start | bytes 786440 | tf_op jit(solution)/shard_map/ppermute | solution.py:40
  25.1 10.1 %collective-permute-start = (bf16[128,1024]{1,0:T(8,128)(2,1)S(1)}, bf16[128,1024]{1,0:T(8,128)(2,1)S(1)}, u32[]{:S(2)}, u32[]{:S(2)}) collective-permute-start(bf16[128,1024]{1,0:T(8,128)(2,1)S(1)} %bitcast.11), channel_id=1, source_target_pairs={{0,8},{8,16},{16,24},{24,0},{1,129},{129,257},{257,385},{385,1},{2... | collective-permute-start | bytes 786440 | tf_op jit(solution)/shard_map/ppermute | solution.py:40
  30.4 35.9 %copy-start.3 = (bf16[8,32,1024]{2,1,0:T(8,128)(2,1)S(1)}, bf16[8,32,1024]{2,1,0:T(8,128)(2,1)}, u32[]{:S(2)}) copy-start(bf16[8,32,1024]{2,1,0:T(8,128)(2,1)} %param.8) | copy-start | bytes 1572868
  30.4 14.7 %collective-permute-start.6 = (bf16[256,1024]{1,0:T(8,128)(2,1)S(1)}, bf16[256,1024]{1,0:T(8,128)(2,1)}, u32[]{:S(2)}, u32[]{:S(2)}) collective-permute-start(bf16[256,1024]{1,0:T(8,128)(2,1)S(1)} %constant_dynamic-update-slice_fusion.high), channel_id=1, source_target_pairs={{0,384},{128,0},{256,128},{384,256},{1,25},{9,1},{17,9},{25,17},{2... | collective-permute-start | bytes 1572872 | tf_op jit(solution)/shard_map/ppermute | solution.py:40
  35.3 12.9 %collective-permute-start.3 = (bf16[256,1024]{1,0:T(8,128)(2,1)S(1)}, bf16[256,1024]{1,0:T(8,128)(2,1)}, u32[]{:S(2)}, u32[]{:S(2)}) collective-permute-start(bf16[256,1024]{1,0:T(8,128)(2,1)S(1)} %pad_maximum_fusion.low), channel_id=1, source_target_pairs={{0,128},{128,256},{256,384},{384,0},{1,9},{9,17},{17,25},{25,1},{2... | collective-permute-start | bytes 1572872 | tf_op jit(solution)/shard_map/ppermute | solution.py:40
  38.0 20.5 %collective-permute-start.4 = (bf16[256,1024]{1,0:T(8,128)(2,1)S(1)}, bf16[256,1024]{1,0:T(8,128)(2,1)}, u32[]{:S(2)}, u32[]{:S(2)}) collective-permute-start(bf16[256,1024]{1,0:T(8,128)(2,1)S(1)} %constant_dynamic-update-slice_fusion.high), channel_id=1, source_target_pairs={{0,128},{128,256},{256,384},{384,0},{1,9},{9,17},{17,25},{25,1},{2... | collective-permute-start | bytes 1572872 | tf_op jit(solution)/shard_map/ppermute | solution.py:40
  41.4 17.1 %collective-permute-start.5 = (bf16[256,1024]{1,0:T(8,128)(2,1)S(1)}, bf16[256,1024]{1,0:T(8,128)(2,1)}, u32[]{:S(2)}, u32[]{:S(2)}) collective-permute-start(bf16[256,1024]{1,0:T(8,128)(2,1)S(1)} %pad_maximum_fusion.low), channel_id=1, source_target_pairs={{0,384},{128,0},{256,128},{384,256},{1,25},{9,1},{17,9},{25,17},{2... | collective-permute-start | bytes 1572872 | tf_op jit(solution)/shard_map/ppermute | solution.py:40
  45.1 15.2 %collective-permute-start.8 = (bf16[256,1024]{1,0:T(8,128)(2,1)}, bf16[256,1024]{1,0:T(8,128)(2,1)}, u32[]{:S(2)}, u32[]{:S(2)}) collective-permute-start(bf16[256,1024]{1,0:T(8,128)(2,1)} %collective-permute-done.6.down_on), channel_id=1, source_target_pairs={{0,384},{128,0},{256,128},{384,256},{1,25},{9,1},{17,9},{25,17},{2... | collective-permute-start | bytes 1572872 | tf_op jit(solution)/shard_map/ppermute | solution.py:40
  48.2 18.1 %collective-permute-start.7 = (bf16[256,1024]{1,0:T(8,128)(2,1)}, bf16[256,1024]{1,0:T(8,128)(2,1)}, u32[]{:S(2)}, u32[]{:S(2)}) collective-permute-start(bf16[256,1024]{1,0:T(8,128)(2,1)} %collective-permute-done.3.up_on), channel_id=1, source_target_pairs={{0,128},{128,256},{256,384},{384,0},{1,9},{9,17},{17,25},{25,1},{2... | collective-permute-start | bytes 1572872 | tf_op jit(solution)/shard_map/ppermute | solution.py:40
  51.2 41.7 %all-to-all-start.1 = ((bf16[64,32,256]{2,1,0:T(8,128)(2,1)}), bf16[64,32,256]{2,1,0:T(8,128)(2,1)S(1)}, u32[]{:S(2)}, u32[]{:S(2)}) async-start(bf16[64,32,256]{2,1,0:T(8,128)(2,1)} %bitcast.8), calls=%async_computation.1 | async-start | bytes 2097152 | tf_op jit(solution)/shard_map/all_to_all | solution.py:279
  69.7 7.4 %copy-start.4 = (s32[32,6]{0,1:T(8,128)S(1)}, s32[32,6]{0,1:T(8,128)}, u32[]{:S(2)}) copy-start(s32[32,6]{0,1:T(8,128)} %param.13) | copy-start | bytes 2308
  69.7 4.6 %collective-permute-start.9 = (f32[1024,256]{1,0:T(8,128)S(1)}, f32[1024,256]{1,0:T(8,128)S(1)}, u32[]{:S(2)}, u32[]{:S(2)}) collective-permute-start(f32[1024,256]{1,0:T(8,128)S(1)} %get-tuple-element.19), channel_id=1, source_target_pairs={{0,1},{1,0},{2,3},{3,2},{4,5},{5,4},{6,7},{7,6},{8,9},{9,8},{10,11... | collective-permute-start | bytes 3145736 | tf_op jit(solution)/shard_map/ppermute | solution.py:59
  74.2 29.6 %copy-start = (bf16[192,16,256]{2,1,0:T(8,128)(2,1)S(1)}, bf16[192,16,256]{2,1,0:T(8,128)(2,1)}, u32[]{:S(2)}) copy-start(bf16[192,16,256]{2,1,0:T(8,128)(2,1)} %pool.1) | copy-start | bytes 4718596
  74.2 29.6 %copy-start.1 = (bf16[8,32,1024]{2,1,0:T(8,128)(2,1)S(1)}, bf16[8,32,1024]{2,1,0:T(8,128)(2,1)}, u32[]{:S(2)}) copy-start(bf16[8,32,1024]{2,1,0:T(8,128)(2,1)} %queries) | copy-start | bytes 1572868
  74.2 29.6 %copy-start.2 = (s32[32]{0:T(128)S(1)}, s32[32]{0:T(128)}, u32[]{:S(2)}) copy-start(s32[32]{0:T(128)} %lengths.1) | copy-start | bytes 388
  75.1 11.6 %collective-permute-start.11 = (f16[256,256]{1,0:T(8,128)(2,1)}, f16[256,256]{1,0:T(8,128)(2,1)}, u32[]{:S(2)}, u32[]{:S(2)}) collective-permute-start(f16[256,256]{1,0:T(8,128)(2,1)} %get-tuple-element.32), channel_id=1, source_target_pairs={{0,2},{1,7},{2,0},{3,5},{4,6},{5,3},{6,4},{7,1},{8,10},{9,15},{10,... | collective-permute-start | bytes 393224 | tf_op jit(solution)/shard_map/ppermute | solution.py:51
  77.1 25.8 %collective-permute-start.10 = (f16[256,256]{1,0:T(8,128)(2,1)}, f16[256,256]{1,0:T(8,128)(2,1)}, u32[]{:S(2)}, u32[]{:S(2)}) collective-permute-start(f16[256,256]{1,0:T(8,128)(2,1)} %get-tuple-element.33), channel_id=1, source_target_pairs={{0,2},{1,7},{2,0},{3,5},{4,6},{5,3},{6,4},{7,1},{8,10},{9,15},{10,... | collective-permute-start | bytes 393224 | tf_op jit(solution)/shard_map/ppermute | solution.py:51
  94.0 14.6 %collective-permute-start.12 = (f16[256,256]{1,0:T(8,128)(2,1)S(1)}, f16[256,256]{1,0:T(8,128)(2,1)S(1)}, u32[]{:S(2)}, u32[]{:S(2)}) collective-permute-start(f16[256,256]{1,0:T(8,128)(2,1)S(1)} %multiply_convert_fusion), channel_id=1, source_target_pairs={{0,6},{1,3},{2,4},{3,1},{4,2},{5,7},{6,0},{7,5},{8,14},{9,11},{10,... | collective-permute-start | bytes 393224 | tf_op jit(solution)/shard_map/ppermute | solution.py:51
